TPU v7x, 256 devices: a whole 4x4x8 slice. The times are simulated.
256 devices in a mesh: row: 8 (over x, y_hi), col: 32 (over z, y_lo, core).
Axes of the slice: x: 4, y: 4 (y_hi: 2, y_lo: 2; y = y_hi * 2 + y_lo), z: 8, core: 2. Of those that a mesh axis runs over, the one named last changes fastest.
Arguments:
- latent: bfloat16 [8192, 1280], P(('row', 'col')), may hold values from -26 to 26
- gn_gain: float32 [1280], replicated, may hold values from 0.25 to 1.75
- gn_bias: float32 [1280], replicated, may hold values from -3 to 3
- w_in: bfloat16 [1280, 1280], replicated, may hold values from -0.15625 to 0.15625
- b_in: float32 [1280], replicated, may hold values from -3 to 3
- ln_gain: float32 [1280], replicated, may hold values from 0.25 to 1.75
- ln_bias: float32 [1280], replicated, may hold values from -2 to 2
- w_query: bfloat16 [1280, 640], replicated, may hold values from -0.15625 to 0.15625
- w_key: bfloat16 [1280, 640], replicated, may hold values from -0.15625 to 0.15625
- w_value: bfloat16 [1280, 640], replicated, may hold values from -0.15625 to 0.15625
- stale_kv: bfloat16 [2, 8192, 640], P(None, ('row', 'col')), may hold values from -10 to 10
Outputs:
- stream: bfloat16 [8192, 1280], P(('row', 'col'))
- fresh_kv: bfloat16 [2, 8192, 640], P(None, ('row', 'col'))
- attended: bfloat16 [8192, 640], P(('row', 'col'))
All inputs are finite; a program needn't handle non-finite values.
Results may differ from a plain program's by a relative error of at most 0.019.
Values may be sent and summed in bfloat16 or wider, within the bound.
No kernel may reach another device: no remote copies, remote signals or barrier semaphores. Data moves between devices by JAX's collectives and lax.ppermute only.
A program may use at most 128 MiB of HBM per device.

v0:
```python
import math

import jax
import jax.numpy as jnp
from jax import lax
from jax.sharding import PartitionSpec as P

GROUPS = 32
HEADS = 10
HEAD_DIM = 64


def pair_terms(query_heads, key_block, value_block, factor, blocked):
    length = key_block.shape[0]
    key_heads = key_block.reshape(length, HEADS, HEAD_DIM)
    value_heads = value_block.reshape(length, HEADS, HEAD_DIM)
    score = (
        jnp.einsum("qhd,khd->hqk", query_heads, key_heads, preferred_element_type=jnp.float32)
        * factor
    )
    weight = jnp.exp(score)
    if blocked is not None:
        weight = jnp.where(blocked[None, :, :], 0.0, weight)
    total = jnp.sum(weight, axis=-1)
    numer = jnp.einsum(
        "hqk,khd->qhd", weight.astype(jnp.bfloat16), value_heads, preferred_element_type=jnp.float32
    )
    return (numer, total)


def local(
    latent, gn_gain, gn_bias, w_in, b_in, ln_gain, ln_bias, w_query, w_key, w_value, stale_kv
):
    rows = latent.shape[0]
    chans = latent.shape[1]
    width = chans // GROUPS
    devices_all = lax.axis_size("row") * lax.axis_size("col")
    count = rows * devices_all * width
    values_in = latent.astype(jnp.float32).reshape(rows, GROUPS, width)
    mean = lax.psum(jnp.sum(values_in, axis=(0, 2)), ("row", "col")) / count
    centred = values_in - mean[None, :, None]
    spread = lax.psum(jnp.sum(centred * centred, axis=(0, 2)), ("row", "col")) / count
    scaled = (centred * lax.rsqrt(spread + 1e-06)[None, :, None]).reshape(rows, chans)
    normed = (scaled * gn_gain + gn_bias).astype(jnp.bfloat16)
    stream = (jnp.dot(normed, w_in, preferred_element_type=jnp.float32) + b_in).astype(jnp.bfloat16)
    wide = stream.astype(jnp.float32)
    token_mean = jnp.mean(wide, axis=-1, keepdims=True)
    token_dev = wide - token_mean
    token_var = jnp.mean(token_dev * token_dev, axis=-1, keepdims=True)
    lnorm = (token_dev * lax.rsqrt(token_var + 1e-05) * ln_gain + ln_bias).astype(jnp.bfloat16)
    query = jnp.dot(lnorm, w_query, preferred_element_type=jnp.float32).astype(jnp.bfloat16)
    keys_new = jnp.dot(lnorm, w_key, preferred_element_type=jnp.float32).astype(jnp.bfloat16)
    values_new = jnp.dot(lnorm, w_value, preferred_element_type=jnp.float32).astype(jnp.bfloat16)
    fresh_kv = jnp.stack([keys_new, values_new])
    factor = 1.0 / math.sqrt(HEAD_DIM)
    query_heads = query.reshape(rows, HEADS, HEAD_DIM)
    my_patch = lax.axis_index("row") * lax.axis_size("col") + lax.axis_index("col")
    own_start = my_patch * rows
    own_numer, own_total = pair_terms(query_heads, keys_new, values_new, factor, None)
    piece = lax.all_gather(stale_kv, ("row", "col"), axis=1, tiled=True)
    length = piece[0].shape[1 - 1]
    place = lax.iota(jnp.int32, length)
    inside = (place >= own_start) & (place < own_start + rows)
    blocked = jnp.broadcast_to(inside[None, :], (rows, length))
    numer, total = pair_terms(query_heads, piece[0], piece[1], factor, blocked)
    numer, total = (own_numer + numer, own_total + total)
    attended = (
        (numer / jnp.transpose(total)[:, :, None])
        .reshape(rows, HEADS * HEAD_DIM)
        .astype(jnp.bfloat16)
    )
    return (stream, fresh_kv, attended)


def solution(mesh):
    placed = (
        P(("row", "col"), None),
        P(),
        P(),
        P(),
        P(),
        P(),
        P(),
        P(),
        P(),
        P(),
        P(None, ("row", "col"), None),
    )
    return jax.shard_map(
        local,
        mesh=mesh,
        in_specs=placed,
        out_specs=(P(("row", "col"), None), P(None, ("row", "col"), None), P(("row", "col"), None)),
        check_vma=False,
    )
```

profile of v0, /device:TPU:2, one launch (start us, length us, event | category | flops | bytes accessed | tf_op | source)
XLA Modules:
  0.0 513.1 jit_solution(8186084876314725219)
XLA Ops:
  7.2 0.0 all-gather.2.cloned.1.call-start
  7.3 0.7 all-gather.2.cloned.1.call-update
  7.9 1.2 convert_reduce_fusion.1
  9.1 0.1 reduce_sum.69
  9.2 0.1 reduce_sum.70
  9.3 78.9 %psum.14 = f32[32]{0:T(128)S(1)} all-reduce(f32[32]{0:T(128)S(1)} %reduce_sum.70), channel_id=1, replica_groups=mesh['row'=8,'col'=32] {'row','col'}, use_global_device_ids=true, to_apply=%region_2.0 | all-reduce | flops 32 | bytes 256 | tf_op jit(solution)/shard_map/psum | solution.py:40
  88.2 0.1 sub.22
  88.3 0.1 sub.23
  88.3 0.9 fusion.20
  89.3 0.1 reduce_sum.72
  89.4 0.1 reduce_sum.73
  89.5 73.6 %psum.15 = f32[32]{0:T(128)S(1)} all-reduce(f32[32]{0:T(128)S(1)} %reduce_sum.73), channel_id=1, replica_groups=mesh['row'=8,'col'=32] {'row','col'}, use_global_device_ids=true, to_apply=%region_5.0 | all-reduce | flops 32 | bytes 256 | tf_op jit(solution)/shard_map/psum | solution.py:42
  163.1 0.1 mul.63
  163.2 0.1 mul.64
  163.3 1.7 convert_reduce_fusion
  165.0 0.2 fusion.16
  165.2 1.9 convolution_convert_fusion
  167.1 0.1 reshape.45
  167.3 1.9 convolution_convert_fusion.2
  169.2 0.1 reshape.46
  169.3 1.9 convolution_convert_fusion.1
  171.2 0.1 reshape.44
  171.4 0.6 pad_maximum_fusion
  172.0 0.8 fusion.39
  172.8 275.2 %all-gather.2.cloned.1.call-done = bf16[2,8192,640]{2,1,0:T(8,128)(2,1)} async-done(((bf16[2,32,640]{2,1,0:T(8,128)(2,1)}), bf16[2,8192,640]{2,1,0:T(8,128)(2,1)}) %all-gather.2.cloned.1.call-update) | async-done | bytes 20971536 | tf_op jit(solution)/shard_map/all_gather | solution.py:60
  448.0 15.9 %fusion.38 = (bf16[1,8192,640]{2,1,0:T(8,128)(2,1)}, bf16[1,8192,640]{2,1,0:T(8,128)(2,1)}) fusion(bf16[2,8192,640]{2,1,0:T(8,128)(2,1)} %all-gather.2.cloned.1.call-done), kind=kLoop, calls=%fused_computation.51 | loop fusion | bytes 41943040 | tf_op jit(solution)/shard_map/slice | solution.py:65
  463.9 14.3 %copy.33 = bf16[1,8192,640]{1,2,0:T(8,128)(2,1)} copy(bf16[1,8192,640]{2,1,0:T(8,128)(2,1)} %get-tuple-element.3) | data formatting | bytes 20971520 | tf_op jit(solution)/shard_map/slice | solution.py:65
  478.2 14.4 %copy.35 = bf16[1,8192,640]{1,2,0:T(8,128)(2,1)} copy(bf16[1,8192,640]{2,1,0:T(8,128)(2,1)} %get-tuple-element.4) | data formatting | bytes 20971520 | tf_op jit(solution)/shard_map/slice | solution.py:65
  492.6 6.9 %fusion.40 = (f32[10,32]{1,0:T(8,128)S(1)}, bf16[10,32,8192]{2,1,0:T(8,128)(2,1)S(1)}) fusion(bf16[8192,10,64]{0,2,1:T(8,128)(2,1)} %bitcast.25, bf16[32,10,64]{2,1,0:T(8,128)(2,1)S(1)} %reshape.45, pred[8192]{0:T(1024)(128)(4,1)S(1)} %fusion.34), kind=kOutput, calls=%fused_computation.53 | convolution fusion | flops 346029760 | bytes 15779072 | tf_op jit(solution)/shard_map/qhd,khd->hqk/dot_general | solution.py:18
  499.5 5.7 %fusion.5 = f32[32,10,64]{2,0,1:T(8,128)S(1)} fusion(bf16[8192,10,64]{0,2,1:T(8,128)(2,1)} %bitcast.24, bf16[10,32,8192]{2,1,0:T(8,128)(2,1)S(1)} %get-tuple-element.10), kind=kOutput, calls=%fused_computation.7 | convolution fusion | flops 335544320 | bytes 15810560 | tf_op jit(solution)/shard_map/hqk,khd->qhd/dot_general | solution.py:25
  505.2 0.2 fusion.11
  505.5 0.8 convert_element_type.47
  (19 shorter events, 0.1 us)
Async XLA Ops:
  7.2 156.1 %copy-start = (bf16[1280,1280]{1,0:T(8,128)(2,1)S(1)}, bf16[1280,1280]{1,0:T(8,128)(2,1)}, u32[]{:S(2)}) copy-start(bf16[1280,1280]{1,0:T(8,128)(2,1)} %param.14) | copy-start | bytes 9830404
  7.2 160.1 %copy-start.3 = (f32[1280]{0:T(1024)S(1)}, f32[1280]{0:T(1024)}, u32[]{:S(2)}) copy-start(f32[1280]{0:T(1024)} %param.17) | copy-start | bytes 15364
  7.2 160.1 %copy-start.4 = (f32[1280]{0:T(1024)S(1)}, f32[1280]{0:T(1024)}, u32[]{:S(2)}) copy-start(f32[1280]{0:T(1024)} %param.16) | copy-start | bytes 15364
  7.2 440.8 %all-gather.2.cloned.1.call-start = ((), (), s32[]{:S(2)}) async-start(), calls=%async_computation | async-start | bytes 21053440 | tf_op jit(solution)/shard_map/all_gather | solution.py:60
  165.0 298.9 %copy-start.2 = (bf16[32,1280]{1,0:T(8,128)(2,1)}, bf16[32,1280]{1,0:T(8,128)(2,1)S(1)}, u32[]{:S(2)}) copy-start(bf16[32,1280]{1,0:T(8,128)(2,1)S(1)} %get-tuple-element.6) | copy-start | bytes 245764
  499.5 6.8 %copy-start.1 = (bf16[1280,1280]{1,0:T(8,128)(2,1)S(1)}, bf16[1280,1280]{1,0:T(8,128)(2,1)}, u32[]{:S(2)}) copy-start(bf16[1280,1280]{1,0:T(8,128)(2,1)} %param.14) | copy-start | bytes 9830404
  499.5 5.7 %copy-start.5 = (bf16[10,32,32]{1,2,0:T(8,128)(2,1)S(1)}, bf16[10,32,32]{1,2,0:T(8,128)(2,1)}, u32[]{:S(2)}) copy-start(bf16[10,32,32]{1,2,0:T(8,128)(2,1)} %get-tuple-element.8) | copy-start | bytes 61444
Sparse Core Ops, SparseCore 0:
  9.9 438.1 all-gather.1
where the time goes:
time: 515 us; the launch traced here: 513 us
  waiting for transfers between devices  276 us (54%)
  blocking collectives  152 us (30%)
  local copies, waits for them, and re-layouts  46.3 us (9%)
  matrix products  20.9 us (4%)
  between operations  14.2 us (3%)
    all_gather x1, waiting for transfers between devices, local(): piece = lax.all_gather(stale_kv, ('row', 'col'), axis=1, tiled=True)  275 us
    psum x1, blocking collectives, local(): mean = lax.psum(jnp.sum(values_in, axis=(0, 2)), ('row', 'col')) / count  78.9 us
    psum x1, blocking collectives, local(): lax.psum(jnp.sum(centred * centred, axis=(0, 2)), ('row', 'col')) / count  73.6 us
    slice x3, local copies, waits for them, and re-layouts, local(): numer, total = pair_terms(query_heads, piece[0], piece[1], factor, blocked)  44.6 us
  transfers between devices with their start and end apart: 1, of which 1 were waited for; matrix products, arithmetic and copies ran while one was open for 2% of the time, Pallas kernels for 0%

commit v1 on v0

v1 whole, which is shorter than its diff:
```python
import math

import jax
import jax.numpy as jnp
from jax import lax
from jax.experimental import pallas as pl
from jax.experimental.pallas import tpu as pltpu
from jax.sharding import PartitionSpec as P

GROUPS = 32
HEADS = 10
HEAD_DIM = 64
AXES = ("row", "col")
DEVICES = 256
NX, NY, NZ = 4, 4, 8
Z_MASK = 0b00011100
VMEM = pl.BlockSpec(memory_space=pltpu.VMEM)
SMEM = pl.BlockSpec(memory_space=pltpu.SMEM)


def place_of(x, y, z, core):
    return x * 64 + (y // 2) * 32 + z * 4 + (y % 2) * 2 + core


def ring(dx=0, dy=0, dcore=0):
    pairs = []
    for x in range(NX):
        for y in range(NY):
            for z in range(NZ):
                for core in range(2):
                    pairs.append(
                        (
                            place_of(x, y, z, core),
                            place_of((x + dx) % NX, (y + dy) % NY, z, (core + dcore) % 2),
                        )
                    )
    return sorted(pairs)


def groups_of(mask):
    found = {}
    for i in range(DEVICES):
        found.setdefault(i & ~mask, []).append(i)
    return list(found.values())


def spread_out(value, count):
    return jnp.broadcast_to(value[None], (count,) + value.shape)


def attend_kernel(place_ref, q_ref, fresh_ref, *refs):
    key_refs, out_ref = refs[:-1], refs[-1]
    own = place_ref[0]
    rows = q_ref.shape[0]
    patch = fresh_ref.shape[1]
    lane = lax.broadcasted_iota(jnp.int32, (1, 128), 1)
    low = lane < HEAD_DIM
    row = lax.broadcasted_iota(jnp.int32, (2 * rows, 1), 0) % rows
    mine = (row >= own * patch) & (row < (own + 1) * patch)
    totals = jnp.zeros((rows, 128), jnp.float32)
    contract = (((1,), (1,)), ((), ()))
    for pair in range(HEADS // 2):
        lanes = slice(pair * 128, pair * 128 + 128)
        query = q_ref[:, lanes] * jnp.bfloat16(1.0 / math.sqrt(HEAD_DIM))
        zero = jnp.zeros_like(query)
        query = jnp.concatenate(
            [jnp.where(low, query, zero), jnp.where(low, zero, query)], axis=0
        )

        def part(keys, values, keep):
            count = keys.shape[0]
            score = lax.dot_general(query, keys, contract, preferred_element_type=jnp.float32)
            weight = jnp.exp(score)
            if keep is not None:
                weight = jnp.where(keep, weight, 0.0)
            wide = jnp.concatenate([values, jnp.ones((count, 128), jnp.bfloat16)], axis=1)
            return jnp.dot(weight.astype(jnp.bfloat16), wide, preferred_element_type=jnp.float32)

        acc = part(fresh_ref[0, :, lanes], fresh_ref[1, :, lanes], mine)
        for index, ref in enumerate(key_refs):
            count = ref.shape[0] * patch
            keep = None
            if index == 0:
                column = lax.broadcasted_iota(jnp.int32, (1, count), 1)
                keep = jnp.logical_not(mine & (column < patch))
            acc = acc + part(
                ref[:, 0, :, lanes].reshape(count, 128),
                ref[:, 1, :, lanes].reshape(count, 128),
                keep,
            )
        numer = jnp.where(low, acc[:rows, :128], acc[rows:, :128])
        out_ref[:, lanes] = numer.astype(jnp.bfloat16)
        for half in range(2):
            head = 2 * pair + half
            found = acc[half * rows : (half + 1) * rows, 128:]
            totals = jnp.where((lane == head) | (lane == 16 + head), found, totals)
    coarse = totals.astype(jnp.bfloat16)
    fine = (totals - coarse.astype(jnp.float32)).astype(jnp.bfloat16)
    out_ref[:, HEADS * HEAD_DIM :] = jnp.where(lane < 16, coarse, fine)


def attend(place, query, fresh, key_parts):
    rows = query.shape[0]
    return pl.pallas_call(
        attend_kernel,
        out_shape=jax.ShapeDtypeStruct((rows, HEADS * HEAD_DIM + 128), jnp.bfloat16),
        in_specs=[SMEM] + [VMEM] * (2 + len(key_parts)),
        out_specs=VMEM,
        compiler_params=pltpu.CompilerParams(vmem_limit_bytes=32 * 1024 * 1024),
        cost_estimate=pl.CostEstimate(
            flops=4 * rows * 1056 * HEADS * HEAD_DIM,
            bytes_accessed=3 * 1024 * 1024,
            transcendentals=rows * 1056 * HEADS,
        ),
    )(place, query, fresh, *key_parts)


def combine_kernel(parts_ref, out_ref):
    total = jnp.sum(parts_ref[:, :, HEADS * HEAD_DIM :].astype(jnp.float32), axis=0)
    low = lax.broadcasted_iota(jnp.int32, (1, 128), 1) < HEAD_DIM
    for pair in range(HEADS // 2):
        lanes = slice(pair * 128, pair * 128 + 128)
        numer = jnp.sum(parts_ref[:, :, lanes].astype(jnp.float32), axis=0)
        halves = [
            total[:, h : h + 1] + total[:, 16 + h : 17 + h] for h in (2 * pair, 2 * pair + 1)
        ]
        out_ref[:, lanes] = (numer / jnp.where(low, halves[0], halves[1])).astype(jnp.bfloat16)


def combine(parts):
    return pl.pallas_call(
        combine_kernel,
        out_shape=jax.ShapeDtypeStruct((parts.shape[1], HEADS * HEAD_DIM), jnp.bfloat16),
        in_specs=[VMEM],
        out_specs=VMEM,
    )(parts)


def local(
    latent, gn_gain, gn_bias, w_in, b_in, ln_gain, ln_bias, w_query, w_key, w_value, stale_kv
):
    rows, chans = latent.shape
    width = chans // GROUPS

    with jax.named_scope("keys_x"):
        along_x = [lax.ppermute(stale_kv, AXES, ring(dx=d)) for d in (1, 3, 2)]
        plane = jnp.stack([stale_kv] + along_x)
    with jax.named_scope("keys_y"):
        planes = [plane] + [lax.ppermute(plane, AXES, ring(dy=d)) for d in (1, 3, 2)]
    with jax.named_scope("keys_core"):
        planes = planes + [lax.ppermute(part, AXES, ring(dcore=1)) for part in planes]

    with jax.named_scope("statistics"):
        values_in = latent.astype(jnp.float32).reshape(rows, GROUPS, width)
        mean_here = jnp.mean(values_in, axis=(0, 2))
        off = values_in - mean_here[None, :, None]
        square_here = jnp.sum(off * off, axis=(0, 2))
        sent = jnp.concatenate([mean_here, square_here, jnp.zeros((64,), jnp.float32)])
        got = lax.all_to_all(spread_out(sent[None], DEVICES), AXES, 0, 0)[:, 0, :]
        means = got[:, :GROUPS]
        mean = jnp.mean(means, axis=0)
        apart = means - mean[None]
        spread = (
            jnp.sum(got[:, GROUPS : 2 * GROUPS], axis=0)
            + (rows * width) * jnp.sum(apart * apart, axis=0)
        ) / (rows * width * DEVICES)

    centred = values_in - mean[None, :, None]
    scaled = (centred * lax.rsqrt(spread + 1e-06)[None, :, None]).reshape(rows, chans)
    normed = (scaled * gn_gain + gn_bias).astype(jnp.bfloat16)
    stream = (jnp.dot(normed, w_in, preferred_element_type=jnp.float32) + b_in).astype(jnp.bfloat16)
    wide = stream.astype(jnp.float32)
    token_mean = jnp.mean(wide, axis=-1, keepdims=True)
    token_dev = wide - token_mean
    token_var = jnp.mean(token_dev * token_dev, axis=-1, keepdims=True)
    lnorm = (token_dev * lax.rsqrt(token_var + 1e-05) * ln_gain + ln_bias).astype(jnp.bfloat16)
    query = jnp.dot(lnorm, w_query, preferred_element_type=jnp.float32).astype(jnp.bfloat16)
    keys_new = jnp.dot(lnorm, w_key, preferred_element_type=jnp.float32).astype(jnp.bfloat16)
    values_new = jnp.dot(lnorm, w_value, preferred_element_type=jnp.float32).astype(jnp.bfloat16)
    fresh_kv = jnp.stack([keys_new, values_new])

    with jax.named_scope("queries"):
        queries = lax.all_to_all(
            spread_out(query, NZ), AXES, 0, 0, axis_index_groups=groups_of(Z_MASK)
        ).reshape(NZ * rows, HEADS * HEAD_DIM)
    my_z = (lax.axis_index("col") >> 2) & (NZ - 1)
    partial = attend(my_z.reshape(1).astype(jnp.int32), queries, fresh_kv, planes)
    with jax.named_scope("partials"):
        parts = lax.all_to_all(
            partial.reshape(NZ, rows, partial.shape[1]),
            AXES,
            0,
            0,
            axis_index_groups=groups_of(Z_MASK),
        )
    attended = combine(parts)
    return (stream, fresh_kv, attended)


def solution(mesh):
    placed = (
        P(AXES, None),
        P(),
        P(),
        P(),
        P(),
        P(),
        P(),
        P(),
        P(),
        P(),
        P(None, AXES, None),
    )
    return jax.shard_map(
        local,
        mesh=mesh,
        in_specs=placed,
        out_specs=(P(AXES, None), P(None, AXES, None), P(AXES, None)),
        check_vma=False,
    )
```

time: 515 us -> 89.6 us (0.17)
  waiting for transfers between devices: 276 us -> 9.46 us
  blocking collectives: 152 us -> 17.4 us
  local copies, waits for them, and re-layouts: 46.3 us -> 10.5 us
  starting transfers between devices: 0.04 us -> 33.4 us
  matrix products: 20.9 us -> 3.49 us
  between operations: 14.2 us -> 0.96 us
  Pallas kernels: 0 us -> 8.84 us
    all_gather x1 -> x0, waiting for transfers between devices: 275 us -> none  [local(): piece = lax.all_gather(stale_kv, ('row', 'col'), axis=1, tiled=True)]
    psum x2 -> x0, blocking collectives: 152 us -> none  [the longest x1 78.9 us: local(): mean = lax.psum(jnp.sum(values_in, axis=(0, 2)), ('row', 'col')) / count]
    slice x3 -> x0, local copies, waits for them, and re-layouts: 44.6 us -> none  [local(): numer, total = pair_terms(query_heads, piece[0], piece[1], factor, blocked)]
    all_to_all x0 -> x2, starting transfers between devices: none -> 22.6 us  [the longest x1 15.7 us: local(): got = lax.all_to_all(spread_out(sent[None], DEVICES), AXES, 0, 0)[:, 0, :]]
    all_to_all x0 -> x1, blocking collectives: none -> 17.4 us  [local(): lax.all_to_all(partial.reshape(NZ, rows, partial.shape[1]), AXES, 0, 0, a...]
    dot_general x4 -> x0, matrix products: 13.6 us -> none  [the longest x2 7.69 us: pair_terms(): jnp.einsum('qhd,khd->hqk', query_heads, key_heads, preferred_element_type...]
    ppermute x0 -> x10, starting transfers between devices: none -> 10.8 us  [the longest x3 4.93 us: local(): lax.ppermute(plane, AXES, ring(dy=d))]
    pallas_call x0 -> x2, Pallas kernels: none -> 8.84 us  [the longest x1 7.01 us: attend(): pl.pallas_call(attend_kernel, out_shape=jax.ShapeDtypeStruct((rows, HEADS...]
  transfers between devices with their start and end apart: 1 -> 12, of which waited for: 1 -> 5; matrix products, arithmetic and copies ran while one was open for 2% -> 9% of each run, Pallas kernels for 0% -> 0%
where the time goes in v1:
time: 89.6 us; the launch traced here: 88.5 us
  starting transfers between devices  33.4 us (37%)
  blocking collectives  17.4 us (19%)
  local copies, waits for them, and re-layouts  10.5 us (12%)
  waiting for transfers between devices  9.46 us (11%)
  Pallas kernels  8.84 us (10%)
  other arithmetic  4.48 us (5%)
  matrix products  3.49 us (4%)
  between operations  0.96 us (1%)
    all_to_all x1, blocking collectives, local(): lax.all_to_all(partial.reshape(NZ, rows, partial.shape[1]), AXES, 0, 0, a...  17.4 us
    all_to_all x1, starting transfers between devices, local(): got = lax.all_to_all(spread_out(sent[None], DEVICES), AXES, 0, 0)[:, 0, :]  15.7 us
    unnamed x38, local copies, waits for them, and re-layouts  7.33 us
    pallas_call x1, Pallas kernels, attend(): pl.pallas_call(attend_kernel, out_shape=jax.ShapeDtypeStruct((rows, HEADS...  7.01 us
    all_to_all x1, starting transfers between devices, local(): lax.all_to_all(spread_out(query, NZ), AXES, 0, 0, axis_index_groups=group...  6.96 us
    ppermute x3, starting transfers between devices, local(): lax.ppermute(plane, AXES, ring(dy=d))  4.93 us
    ppermute x3, starting transfers between devices, local(): along_x = [lax.ppermute(stale_kv, AXES, ring(dx=d)) for d in (1, 3, 2)]  4.78 us
    ppermute x3, waiting for transfers between devices, local(): along_x = [lax.ppermute(stale_kv, AXES, ring(dx=d)) for d in (1, 3, 2)]  4.65 us
  transfers between devices with their start and end apart: 12, of which 5 were waited for; matrix products, arithmetic and copies ran while one was open for 9% of the time, Pallas kernels for 0%

profile of v1, /device:TPU:2, one launch (start us, length us, event | category | flops | bytes accessed | tf_op | source)
XLA Modules:
  0.0 88.5 jit_solution(7312492837348569032)
XLA Ops:
  0.7 1.1 %convert_reduce_fusion = f32[1280]{0:T(1024)S(1)} fusion(bf16[32,1280]{1,0:T(8,128)(2,1)} %param.11), kind=kLoop, calls=%fused_computation.10 | loop fusion | flops 80640 | bytes 87040 | tf_op jit(solution)/shard_map/statistics/reduce_sum | solution.py:155
  2.1 0.9 %fusion.10 = f32[1280]{0:T(1024)S(1)} fusion(bf16[32,1280]{1,0:T(8,128)(2,1)} %param.11, f32[1280]{0:T(1024)S(1)} %sub.43), kind=kLoop, calls=%fused_computation.20 | loop fusion | flops 162560 | bytes 92160 | tf_op jit(solution)/shard_map/statistics/reduce_sum | solution.py:157
  3.3 0.7 broadcast_in_dim.7
  4.1 15.7 %all-to-all-start = ((f32[256,1,128]{2,1,0:T(1,128)}), f32[256,1,128]{2,1,0:T(1,128)}, u32[]{:S(2)}, u32[]{:S(2)}) async-start(f32[256,1,128]{2,1,0:T(1,128)} %broadcast_in_dim.7), calls=%async_computation | async-start | bytes 262144 | tf_op jit(solution)/shard_map/statistics/all_to_all | solution.py:159
  19.8 1.5 %collective-permute-start = (bf16[2,32,640]{2,1,0:T(8,128)(2,1)}, bf16[2,32,640]{2,1,0:T(8,128)(2,1)S(1)}, u32[]{:S(2)}, u32[]{:S(2)}) collective-permute-start(bf16[2,32,640]{2,1,0:T(8,128)(2,1)} %param.21), channel_id=1, source_target_pairs={{0,64},{1,65},{2,66},{3,67},{4,68},{5,69},{6,70},{7,71},{8,72},{9,... | collective-permute-start | bytes 245768 | tf_op jit(solution)/shard_map/keys_x/ppermute | solution.py:146
  21.3 2.8 %collective-permute-start.2 = (bf16[2,32,640]{2,1,0:T(8,128)(2,1)}, bf16[2,32,640]{2,1,0:T(8,128)(2,1)S(1)}, u32[]{:S(2)}, u32[]{:S(2)}) collective-permute-start(bf16[2,32,640]{2,1,0:T(8,128)(2,1)} %param.21), channel_id=1, source_target_pairs={{0,128},{1,129},{2,130},{3,131},{4,132},{5,133},{6,134},{7,135},{8... | collective-permute-start | bytes 245768 | tf_op jit(solution)/shard_map/keys_x/ppermute | solution.py:146
  24.5 0.6 collective-permute-done
  25.1 3.6 %collective-permute-done.2 = bf16[2,32,640]{2,1,0:T(8,128)(2,1)S(1)} collective-permute-done((bf16[2,32,640]{2,1,0:T(8,128)(2,1)}, bf16[2,32,640]{2,1,0:T(8,128)(2,1)S(1)}, u32[]{:S(2)}, u32[]{:S(2)}) %collective-permute-start.2) | collective-permute-done | bytes 81952 | tf_op jit(solution)/shard_map/keys_x/ppermute | solution.py:146
  28.7 0.5 collective-permute-done.1
  29.2 1.7 %pad_maximum_fusion.refs_0_ = bf16[4,2,32,640]{3,2,1,0:T(8,128)(2,1)} fusion(bf16[1,2,32,640]{3,2,1,0:T(8,128)(2,1)S(1)} %bitcast.21, bf16[1,2,32,640]{3,2,1,0:T(8,128)(2,1)S(1)} %bitcast.22, bf16[1,2,32,640]{3,2,1,0:T(8,128)(2,1)S(1)} %bitcast.20, bf16[1,2,32,640]{3,2,1,0:T(8,128)(2,1)} %bitcast.19), kind=kLoop, calls=%fused_computation.7 | loop fusion | flops 491520 | bytes 655360 | tf_op jit(solution)/shard_map/keys_x/stack | solution.py:147
  30.9 2.9 %collective-permute-start.5 = (bf16[4,2,32,640]{3,2,1,0:T(8,128)(2,1)}, bf16[4,2,32,640]{3,2,1,0:T(8,128)(2,1)}, u32[]{:S(2)}, u32[]{:S(2)}) collective-permute-start(bf16[4,2,32,640]{3,2,1,0:T(8,128)(2,1)} %pad_maximum_fusion.refs_0_), channel_id=1, source_target_pairs={{0,32},{1,33},{2,34},{3,35},{4,36},{5,37},{6,38},{7,39},{8,40},{9,... | collective-permute-start | bytes 983048 | tf_op jit(solution)/shard_map/keys_y/ppermute | solution.py:149
  33.8 1.2 %collective-permute-start.4 = (bf16[4,2,32,640]{3,2,1,0:T(8,128)(2,1)}, bf16[4,2,32,640]{3,2,1,0:T(8,128)(2,1)}, u32[]{:S(2)}, u32[]{:S(2)}) collective-permute-start(bf16[4,2,32,640]{3,2,1,0:T(8,128)(2,1)} %pad_maximum_fusion.refs_0_), channel_id=1, source_target_pairs={{0,34},{1,35},{2,0},{3,1},{4,38},{5,39},{6,4},{7,5},{8,42},{9,43},... | collective-permute-start | bytes 983048 | tf_op jit(solution)/shard_map/keys_y/ppermute | solution.py:149
  34.9 0.9 collective-permute-start.3
  35.8 1.0 %copy.17 = f32[256,1,128]{0,2,1:T(8,128)S(1)} copy(f32[256,1,128]{2,1,0:T(1,128)} %all-to-all-done) | data formatting | bytes 262144 | tf_op jit(solution)/shard_map/statistics/all_to_all | solution.py:159
  37.5 0.8 convert_reduce_fusion.1
  39.4 0.8 broadcast_in_dim.8
  40.1 7.0 %all-to-all-start.1 = ((bf16[8,32,640]{2,1,0:T(8,128)(2,1)}), bf16[8,32,640]{2,1,0:T(8,128)(2,1)}, u32[]{:S(2)}, u32[]{:S(2)}) async-start(bf16[8,32,640]{2,1,0:T(8,128)(2,1)} %broadcast_in_dim.8), calls=%async_computation.1 | async-start | bytes 655360 | tf_op jit(solution)/shard_map/queries/all_to_all | solution.py:183
  47.7 1.0 %collective-permute-done.4.refs_2_ = bf16[4,2,32,640]{3,2,1,0:T(8,128)(2,1)} collective-permute-done((bf16[4,2,32,640]{3,2,1,0:T(8,128)(2,1)}, bf16[4,2,32,640]{3,2,1,0:T(8,128)(2,1)}, u32[]{:S(2)}, u32[]{:S(2)}) %collective-permute-start.4) | collective-permute-done | bytes 327712 | tf_op jit(solution)/shard_map/keys_y/ppermute | solution.py:149
  48.8 0.5 collective-permute-start.7
  49.3 1.9 %fusion.2 = bf16[1,32,640]{2,1,0:T(8,128)(2,1)S(1)} fusion(bf16[1280,640]{1,0:T(8,128)(2,1)} %param.20, bf16[32,1280]{1,0:T(8,128)(2,1)S(1)} %get-tuple-element.6, f32[1280]{0:T(1024)S(1)} %copy-done.14, f32[1280]{0:T(1024)S(1)} %copy-done.15, f32[32]{0:T(128)S(1)} %add_rsqrt_fusion, f32[32]{0:T(128)S(1)} %broadcast_multiply_fusion.1), kind=kOutput, calls=%fused_computation.6 | convolution fusion | flops 52695040 | bytes 1771776 | tf_op jit(solution)/shard_map/dot_general | solution.py:179
  51.7 0.8 copy-done.2
  52.4 0.8 copy-done.4
  53.2 0.7 copy-done.6
  53.9 0.7 copy-done.8
  54.6 3.8 %all-to-all-done.1 = bf16[8,32,640]{2,1,0:T(8,128)(2,1)} async-done(((bf16[8,32,640]{2,1,0:T(8,128)(2,1)}), bf16[8,32,640]{2,1,0:T(8,128)(2,1)}, u32[]{:S(2)}, u32[]{:S(2)}) %all-to-all-start.1) | async-done | bytes 327712 | tf_op jit(solution)/shard_map/queries/all_to_all | solution.py:183
  58.4 1.0 %copy-done.3 = bf16[4,2,32,640]{3,2,1,0:T(8,128)(2,1)S(1)} copy-done((bf16[4,2,32,640]{3,2,1,0:T(8,128)(2,1)S(1)}, bf16[4,2,32,640]{3,2,1,0:T(8,128)(2,1)}, u32[]{:S(2)}) %copy-start.3) | copy-done | bytes 327704
  59.4 1.0 %copy-done.5 = bf16[4,2,32,640]{3,2,1,0:T(8,128)(2,1)S(1)} copy-done((bf16[4,2,32,640]{3,2,1,0:T(8,128)(2,1)S(1)}, bf16[4,2,32,640]{3,2,1,0:T(8,128)(2,1)}, u32[]{:S(2)}) %copy-start.5) | copy-done | bytes 327704
  60.3 1.0 %copy-done.7 = bf16[4,2,32,640]{3,2,1,0:T(8,128)(2,1)S(1)} copy-done((bf16[4,2,32,640]{3,2,1,0:T(8,128)(2,1)S(1)}, bf16[4,2,32,640]{3,2,1,0:T(8,128)(2,1)}, u32[]{:S(2)}) %copy-start.7) | copy-done | bytes 327704
  61.3 1.0 %copy-done.9 = bf16[4,2,32,640]{3,2,1,0:T(8,128)(2,1)S(1)} copy-done((bf16[4,2,32,640]{3,2,1,0:T(8,128)(2,1)S(1)}, bf16[4,2,32,640]{3,2,1,0:T(8,128)(2,1)}, u32[]{:S(2)}) %copy-start.9) | copy-done | bytes 327704
  62.3 7.0 %shard_map.130 = bf16[256,768]{1,0:T(8,128)(2,1)S(1)} custom-call(s32[1]{0:T(128)} %bitcast.3.place_ref, bf16[256,640]{1,0:T(8,128)(2,1)} %bitcast.4.q_ref, bf16[2,32,640]{2,1,0:T(8,128)(2,1)S(1)} %pad_maximum_fusion.1.fresh_ref, bf16[4,2,32,640]{3,2,1,0:T(8,128)(2,1)} %pad_maximum_fusion.refs_0_, bf16[4,2,32,640]{3,2,1,0:T(8,128)(2,1)} %collective-permute-done.3.refs_1_, ...), custom_call_target="tpu_custom_call" | custom-call | flops 692060160 | bytes 3145728 | tf_op jit(solution)/shard_map/pallas_call | solution.py:104
  69.3 17.4 %all_to_all.15.parts_ref = bf16[8,32,768]{2,1,0:T(8,128)(2,1)} all-to-all(bf16[8,32,768]{2,1,0:T(8,128)(2,1)S(1)} %bitcast.16), channel_id=1, replica_groups={{0,4,8,12,16,20,24,28},{1,5,9,13,17,21,25,29},{2,6,10,14,18,22,26,30},{..., dimensions={0} | all-to-all | bytes 786432 | tf_op jit(solution)/shard_map/partials/all_to_all | solution.py:189
  86.7 1.8 %shard_map.131 = bf16[32,640]{1,0:T(8,128)(2,1)} custom-call(bf16[8,32,768]{2,1,0:T(8,128)(2,1)} %all_to_all.15.parts_ref), custom_call_target="tpu_custom_call" | custom-call | tf_op jit(solution)/shard_map/pallas_call | solution.py:131
  (64 shorter events, 3.9 us)
Async XLA Ops:
  0.6 36.8 %copy-start = (bf16[1280,1280]{1,0:T(8,128)(2,1)S(1)}, bf16[1280,1280]{1,0:T(8,128)(2,1)}, u32[]{:S(2)}) copy-start(bf16[1280,1280]{1,0:T(8,128)(2,1)} %param.14) | copy-start | bytes 9830404
  0.6 36.8 %copy-start.13 = (bf16[32,1280]{1,0:T(8,128)(2,1)S(1)}, bf16[32,1280]{1,0:T(8,128)(2,1)}, u32[]{:S(2)}) copy-start(bf16[32,1280]{1,0:T(8,128)(2,1)} %param.11) | copy-start | bytes 245764
  0.7 36.8 %copy-start.16 = (f32[1280]{0:T(1024)S(1)}, f32[1280]{0:T(1024)}, u32[]{:S(2)}) copy-start(f32[1280]{0:T(1024)} %param.15) | copy-start | bytes 15364
  0.7 36.8 %copy-start.17 = (f32[1280]{0:T(1024)S(1)}, f32[1280]{0:T(1024)}, u32[]{:S(2)}) copy-start(f32[1280]{0:T(1024)} %param.13) | copy-start | bytes 15364
  0.7 36.8 %copy-start.18 = (f32[1280]{0:T(1024)S(1)}, f32[1280]{0:T(1024)}, u32[]{:S(2)}) copy-start(f32[1280]{0:T(1024)} %param.12) | copy-start | bytes 15364
  4.1 31.7 %all-to-all-start = ((f32[256,1,128]{2,1,0:T(1,128)}), f32[256,1,128]{2,1,0:T(1,128)}, u32[]{:S(2)}, u32[]{:S(2)}) async-start(f32[256,1,128]{2,1,0:T(1,128)} %broadcast_in_dim.7), calls=%async_computation | async-start | bytes 262144 | tf_op jit(solution)/shard_map/statistics/all_to_all | solution.py:159
  19.8 5.3 %collective-permute-start = (bf16[2,32,640]{2,1,0:T(8,128)(2,1)}, bf16[2,32,640]{2,1,0:T(8,128)(2,1)S(1)}, u32[]{:S(2)}, u32[]{:S(2)}) collective-permute-start(bf16[2,32,640]{2,1,0:T(8,128)(2,1)} %param.21), channel_id=1, source_target_pairs={{0,64},{1,65},{2,66},{3,67},{4,68},{5,69},{6,70},{7,71},{8,72},{9,... | collective-permute-start | bytes 245768 | tf_op jit(solution)/shard_map/keys_x/ppermute | solution.py:146
  21.3 7.4 %collective-permute-start.2 = (bf16[2,32,640]{2,1,0:T(8,128)(2,1)}, bf16[2,32,640]{2,1,0:T(8,128)(2,1)S(1)}, u32[]{:S(2)}, u32[]{:S(2)}) collective-permute-start(bf16[2,32,640]{2,1,0:T(8,128)(2,1)} %param.21), channel_id=1, source_target_pairs={{0,128},{1,129},{2,130},{3,131},{4,132},{5,133},{6,134},{7,135},{8... | collective-permute-start | bytes 245768 | tf_op jit(solution)/shard_map/keys_x/ppermute | solution.py:146
  24.1 5.1 %collective-permute-start.1 = (bf16[2,32,640]{2,1,0:T(8,128)(2,1)}, bf16[2,32,640]{2,1,0:T(8,128)(2,1)S(1)}, u32[]{:S(2)}, u32[]{:S(2)}) collective-permute-start(bf16[2,32,640]{2,1,0:T(8,128)(2,1)} %param.21), channel_id=1, source_target_pairs={{0,192},{1,193},{2,194},{3,195},{4,196},{5,197},{6,198},{7,199},{8... | collective-permute-start | bytes 245768 | tf_op jit(solution)/shard_map/keys_x/ppermute | solution.py:146
  30.9 16.4 %collective-permute-start.5 = (bf16[4,2,32,640]{3,2,1,0:T(8,128)(2,1)}, bf16[4,2,32,640]{3,2,1,0:T(8,128)(2,1)}, u32[]{:S(2)}, u32[]{:S(2)}) collective-permute-start(bf16[4,2,32,640]{3,2,1,0:T(8,128)(2,1)} %pad_maximum_fusion.refs_0_), channel_id=1, source_target_pairs={{0,32},{1,33},{2,34},{3,35},{4,36},{5,37},{6,38},{7,39},{8,40},{9,... | collective-permute-start | bytes 983048 | tf_op jit(solution)/shard_map/keys_y/ppermute | solution.py:149
  33.8 15.0 %collective-permute-start.4 = (bf16[4,2,32,640]{3,2,1,0:T(8,128)(2,1)}, bf16[4,2,32,640]{3,2,1,0:T(8,128)(2,1)}, u32[]{:S(2)}, u32[]{:S(2)}) collective-permute-start(bf16[4,2,32,640]{3,2,1,0:T(8,128)(2,1)} %pad_maximum_fusion.refs_0_), channel_id=1, source_target_pairs={{0,34},{1,35},{2,0},{3,1},{4,38},{5,39},{6,4},{7,5},{8,42},{9,43},... | collective-permute-start | bytes 983048 | tf_op jit(solution)/shard_map/keys_y/ppermute | solution.py:149
  34.9 13.8 %collective-permute-start.3 = (bf16[4,2,32,640]{3,2,1,0:T(8,128)(2,1)}, bf16[4,2,32,640]{3,2,1,0:T(8,128)(2,1)}, u32[]{:S(2)}, u32[]{:S(2)}) collective-permute-start(bf16[4,2,32,640]{3,2,1,0:T(8,128)(2,1)} %pad_maximum_fusion.refs_0_), channel_id=1, source_target_pairs={{0,2},{1,3},{2,32},{3,33},{4,6},{5,7},{6,36},{7,37},{8,10},{9,11},... | collective-permute-start | bytes 983048 | tf_op jit(solution)/shard_map/keys_y/ppermute | solution.py:149
  37.5 1.4 %copy-start.11 = (bf16[1280,640]{1,0:T(8,128)(2,1)S(1)}, bf16[1280,640]{1,0:T(8,128)(2,1)}, u32[]{:S(2)}) copy-start(bf16[1280,640]{1,0:T(8,128)(2,1)} %param.18) | copy-start | bytes 4915204
  37.5 1.4 %copy-start.14 = (f32[1280]{0:T(1024)S(1)}, f32[1280]{0:T(1024)}, u32[]{:S(2)}) copy-start(f32[1280]{0:T(1024)} %param.17) | copy-start | bytes 15364
  37.5 1.4 %copy-start.15 = (f32[1280]{0:T(1024)S(1)}, f32[1280]{0:T(1024)}, u32[]{:S(2)}) copy-start(f32[1280]{0:T(1024)} %param.16) | copy-start | bytes 15364
  38.3 12.8 %copy-start.10 = (bf16[32,1280]{1,0:T(8,128)(2,1)}, bf16[32,1280]{1,0:T(8,128)(2,1)S(1)}, u32[]{:S(2)}) copy-start(bf16[32,1280]{1,0:T(8,128)(2,1)S(1)} %get-tuple-element.6) | copy-start | bytes 245764
  40.1 18.3 %all-to-all-start.1 = ((bf16[8,32,640]{2,1,0:T(8,128)(2,1)}), bf16[8,32,640]{2,1,0:T(8,128)(2,1)}, u32[]{:S(2)}, u32[]{:S(2)}) async-start(bf16[8,32,640]{2,1,0:T(8,128)(2,1)} %broadcast_in_dim.8), calls=%async_computation.1 | async-start | bytes 655360 | tf_op jit(solution)/shard_map/queries/all_to_all | solution.py:183
  47.1 4.0 %copy-start.12 = (bf16[1280,640]{1,0:T(8,128)(2,1)S(1)}, bf16[1280,640]{1,0:T(8,128)(2,1)}, u32[]{:S(2)}) copy-start(bf16[1280,640]{1,0:T(8,128)(2,1)} %param.19) | copy-start | bytes 4915204
  47.1 4.5 %collective-permute-start.6 = (bf16[4,2,32,640]{3,2,1,0:T(8,128)(2,1)}, bf16[4,2,32,640]{3,2,1,0:T(8,128)(2,1)S(1)}, u32[]{:S(2)}, u32[]{:S(2)}) collective-permute-start(bf16[4,2,32,640]{3,2,1,0:T(8,128)(2,1)} %pad_maximum_fusion.refs_0_), channel_id=1, source_target_pairs={{0,1},{1,0},{2,3},{3,2},{4,5},{5,4},{6,7},{7,6},{8,9},{9,8},{10,11... | collective-permute-start | bytes 983048 | tf_op jit(solution)/shard_map/keys_core/ppermute | solution.py:151
  47.2 5.2 %collective-permute-start.9 = (bf16[4,2,32,640]{3,2,1,0:T(8,128)(2,1)}, bf16[4,2,32,640]{3,2,1,0:T(8,128)(2,1)S(1)}, u32[]{:S(2)}, u32[]{:S(2)}) collective-permute-start(bf16[4,2,32,640]{3,2,1,0:T(8,128)(2,1)} %collective-permute-done.5.refs_3_), channel_id=1, source_target_pairs={{0,1},{1,0},{2,3},{3,2},{4,5},{5,4},{6,7},{7,6},{8,9},{9,8},{10,11... | collective-permute-start | bytes 983048 | tf_op jit(solution)/shard_map/keys_core/ppermute | solution.py:151
  48.8 4.4 %collective-permute-start.8 = (bf16[4,2,32,640]{3,2,1,0:T(8,128)(2,1)}, bf16[4,2,32,640]{3,2,1,0:T(8,128)(2,1)S(1)}, u32[]{:S(2)}, u32[]{:S(2)}) collective-permute-start(bf16[4,2,32,640]{3,2,1,0:T(8,128)(2,1)} %collective-permute-done.4.refs_2_), channel_id=1, source_target_pairs={{0,1},{1,0},{2,3},{3,2},{4,5},{5,4},{6,7},{7,6},{8,9},{9,8},{10,11... | collective-permute-start | bytes 983048 | tf_op jit(solution)/shard_map/keys_core/ppermute | solution.py:151
  48.8 5.2 %collective-permute-start.7 = (bf16[4,2,32,640]{3,2,1,0:T(8,128)(2,1)}, bf16[4,2,32,640]{3,2,1,0:T(8,128)(2,1)S(1)}, u32[]{:S(2)}, u32[]{:S(2)}) collective-permute-start(bf16[4,2,32,640]{3,2,1,0:T(8,128)(2,1)} %collective-permute-done.3.refs_1_), channel_id=1, source_target_pairs={{0,1},{1,0},{2,3},{3,2},{4,5},{5,4},{6,7},{7,6},{8,9},{9,8},{10,11... | collective-permute-start | bytes 983048 | tf_op jit(solution)/shard_map/keys_core/ppermute | solution.py:151
  51.6 17.7 %copy-start.1 = (bf16[2,32,640]{2,1,0:T(8,128)(2,1)}, bf16[2,32,640]{2,1,0:T(8,128)(2,1)S(1)}, u32[]{:S(2)}) copy-start(bf16[2,32,640]{2,1,0:T(8,128)(2,1)S(1)} %pad_maximum_fusion.1.fresh_ref) | copy-start | bytes 245764
  51.6 0.8 copy-start.2
  52.4 0.8 copy-start.4
  53.2 0.7 copy-start.6
  53.9 0.7 copy-start.8
  58.4 1.0 %copy-start.3 = (bf16[4,2,32,640]{3,2,1,0:T(8,128)(2,1)S(1)}, bf16[4,2,32,640]{3,2,1,0:T(8,128)(2,1)}, u32[]{:S(2)}) copy-start(bf16[4,2,32,640]{3,2,1,0:T(8,128)(2,1)} %copy-done.2) | copy-start | bytes 983044
  59.4 1.0 %copy-start.5 = (bf16[4,2,32,640]{3,2,1,0:T(8,128)(2,1)S(1)}, bf16[4,2,32,640]{3,2,1,0:T(8,128)(2,1)}, u32[]{:S(2)}) copy-start(bf16[4,2,32,640]{3,2,1,0:T(8,128)(2,1)} %copy-done.4) | copy-start | bytes 983044
  60.3 1.0 %copy-start.7 = (bf16[4,2,32,640]{3,2,1,0:T(8,128)(2,1)S(1)}, bf16[4,2,32,640]{3,2,1,0:T(8,128)(2,1)}, u32[]{:S(2)}) copy-start(bf16[4,2,32,640]{3,2,1,0:T(8,128)(2,1)} %copy-done.6) | copy-start | bytes 983044
  61.3 1.0 %copy-start.9 = (bf16[4,2,32,640]{3,2,1,0:T(8,128)(2,1)S(1)}, bf16[4,2,32,640]{3,2,1,0:T(8,128)(2,1)}, u32[]{:S(2)}) copy-start(bf16[4,2,32,640]{3,2,1,0:T(8,128)(2,1)} %copy-done.8) | copy-start | bytes 983044

commit v2 on v0

v2 whole, which is shorter than its diff:
```python
import math
import jax
import jax.numpy as jnp
from jax import lax
from jax.experimental import pallas as pl
from jax.experimental.pallas import tpu as pltpu
from jax.sharding import PartitionSpec as P

GROUPS = 32
HEADS = 10
HEAD_DIM = 64
INNER = HEADS * HEAD_DIM
VMEM = pl.BlockSpec(memory_space=pltpu.VMEM)
SMEM = pl.BlockSpec(memory_space=pltpu.SMEM)
HBM = pl.BlockSpec(memory_space=pltpu.HBM)
NT = (((1,), (1,)), ((), ()))


def member_of(chans):
    width = chans // GROUPS
    first = lax.broadcasted_iota(jnp.int32, (chans, 128), 1) * width
    chan = lax.broadcasted_iota(jnp.int32, (chans, 128), 0)
    inside = (chan >= first) & (chan < first + width)
    return jnp.where(inside, 1.0, 0.0).astype(jnp.bfloat16)


def pieces(value):
    a = value.astype(jnp.bfloat16)
    rest = value - a.astype(jnp.float32)
    b = rest.astype(jnp.bfloat16)
    c = (rest - b.astype(jnp.float32)).astype(jnp.bfloat16)
    return jnp.concatenate([a, b, c], axis=0)


def to_groups(row, member):
    got = jnp.dot(pieces(row), member, preferred_element_type=jnp.float32)
    return got[0:1] + got[1:2] + got[2:3]


def to_channels(row, member):
    got = lax.dot_general(pieces(row), member, NT, preferred_element_type=jnp.float32)
    return got[0:1] + got[1:2] + got[2:3]


def statistics_kernel(x_ref, out_ref):
    rows, chans = x_ref.shape
    entries = rows * (chans // GROUPS)
    member = member_of(chans)
    x = x_ref[...].astype(jnp.float32)
    mean = to_groups(jnp.sum(x, axis=0, keepdims=True), member) * (1.0 / entries)
    off = x - to_channels(mean, member)
    square = to_groups(jnp.sum(off * off, axis=0, keepdims=True), member)
    lane = lax.broadcasted_iota(jnp.int32, (1, 128), 1)
    both = jnp.where(lane < GROUPS, mean, pltpu.roll(square, GROUPS, axis=1))
    out_ref[...] = jnp.broadcast_to(both, out_ref.shape)


def statistics(x, peers):
    return pl.pallas_call(
        statistics_kernel,
        out_shape=jax.ShapeDtypeStruct((peers, 128), jnp.float32),
        in_specs=[VMEM],
        out_specs=VMEM,
    )(x)


def project_kernel(stats_ref, vec_ref, x_ref, w_in_ref, w_q_hbm, stream_ref, lnorm_ref, query_ref, w_q_ref, sem):
    copy = pltpu.make_async_copy(w_q_hbm, w_q_ref, sem)
    copy.start()
    rows, chans = x_ref.shape

    peers = stats_ref.shape[0]
    entries = rows * (chans // GROUPS)
    lane = lax.broadcasted_iota(jnp.int32, (1, 128), 1)
    stats = stats_ref[...]
    sums = jnp.sum(stats, axis=0, keepdims=True)
    mean = jnp.where(lane < GROUPS, sums * (1.0 / peers), 0.0)
    apart = jnp.where(lane < GROUPS, stats - mean, 0.0)
    square = pltpu.roll(sums, 128 - GROUPS, axis=1) + entries * jnp.sum(
        apart * apart, axis=0, keepdims=True
    )
    square = jnp.where(lane < GROUPS, square, 0.0)
    member = member_of(chans)
    mean = to_channels(mean, member)
    scale = to_channels(lax.rsqrt(square * (1.0 / (entries * peers)) + 1e-06), member)

    x = x_ref[...].astype(jnp.float32)
    normed = ((x - mean) * scale * vec_ref[0:1] + vec_ref[1:2]).astype(jnp.bfloat16)
    stream = (
        jnp.dot(normed, w_in_ref[...], preferred_element_type=jnp.float32) + vec_ref[2:3]
    ).astype(jnp.bfloat16)
    stream_ref[...] = stream
    wide = stream.astype(jnp.float32)
    token_mean = jnp.mean(wide, axis=-1, keepdims=True)
    token_dev = wide - token_mean
    token_var = jnp.mean(token_dev * token_dev, axis=-1, keepdims=True)
    lnorm = token_dev * lax.rsqrt(token_var + 1e-05) * vec_ref[3:4] + vec_ref[4:5]
    lnorm = lnorm.astype(jnp.bfloat16)
    lnorm_ref[...] = lnorm
    copy.wait()
    query = jnp.dot(lnorm, w_q_ref[...], preferred_element_type=jnp.float32)
    query = query.astype(jnp.bfloat16) * jnp.bfloat16(1.0 / math.sqrt(HEAD_DIM))
    query_ref[...] = jnp.broadcast_to(query[None], query_ref.shape)


def project(stats, vectors, x, w_in, w_query, copies):
    patch, chans = x.shape
    bf16 = jnp.bfloat16
    return pl.pallas_call(
        project_kernel,
        out_shape=(
            jax.ShapeDtypeStruct((patch, chans), bf16),
            jax.ShapeDtypeStruct((patch, chans), bf16),
            jax.ShapeDtypeStruct((copies, patch, INNER), bf16),
        ),
        in_specs=[VMEM] * 4 + [HBM],
        out_specs=(VMEM, VMEM, VMEM),
        scratch_shapes=[pltpu.VMEM(w_query.shape, bf16), pltpu.SemaphoreType.DMA(())],
        compiler_params=pltpu.CompilerParams(vmem_limit_bytes=56 * 1024 * 1024),
        cost_estimate=pl.CostEstimate(
            flops=patch * 2 * chans * (chans + INNER),
            bytes_accessed=6 * 1024 * 1024,
            transcendentals=patch,
        ),
    )(stats, vectors, x, w_in, w_query)


def fresh_kernel(x_ref, w_k_ref, w_v_ref, out_ref):
    for i, w_ref in enumerate((w_k_ref, w_v_ref)):
        out_ref[i] = jnp.dot(x_ref[...], w_ref[...], preferred_element_type=jnp.float32).astype(
            jnp.bfloat16
        )


def fresh_keys(x, w_key, w_value):
    return pl.pallas_call(
        fresh_kernel,
        out_shape=jax.ShapeDtypeStruct((2, x.shape[0], INNER), jnp.bfloat16),
        in_specs=[VMEM] * 3,
        out_specs=VMEM,
        compiler_params=pltpu.CompilerParams(vmem_limit_bytes=56 * 1024 * 1024),
    )(x, w_key, w_value)


def attend_kernel(place_ref, q_ref, fresh_ref, *refs):
    sources, (out_ref, kv_ref, p_ref, sems) = refs[:-4], refs[-4:]
    copies = [
        pltpu.make_async_copy(source, kv_ref.at[i], sems.at[i])
        for i, source in enumerate(sources)
    ]
    for copy in copies:
        copy.start()
    patch = fresh_ref.shape[1]
    rows = q_ref.shape[0]
    count = rows // patch
    own = place_ref[0] * patch
    for copy in copies:
        copy.wait()
    keys = kv_ref.shape[0] * kv_ref.shape[1] * patch
    lane = lax.broadcasted_iota(jnp.int32, (1, 128), 1)
    low = lane < HEAD_DIM
    row = lax.broadcasted_iota(jnp.int32, (2 * rows, 1), 0)
    row = jnp.where(row >= rows, row - rows, row)
    is_own = (row >= own) & (row < own + patch)
    totals = jnp.zeros((rows, 128), jnp.float32)
    for pair in range(HEADS // 2):
        lanes = slice(pair * 128, pair * 128 + 128)
        part = q_ref[:, lanes]
        zero = jnp.zeros_like(part)
        part = jnp.concatenate([jnp.where(low, part, zero), jnp.where(low, zero, part)], axis=0)
        key = kv_ref[:, :, 0, :, lanes].reshape(keys, 128)
        value = kv_ref[:, :, 1, :, lanes].reshape(keys, 128)
        step = 128
        for at in range(0, keys, step):
            score = lax.dot_general(
                part, key[at : at + step], NT, preferred_element_type=jnp.float32
            )
            weight = jnp.exp(score)
            if at == 0:
                column = lax.broadcasted_iota(jnp.int32, (1, step), 1)
                weight = jnp.where(is_own & (column < patch), 0.0, weight)
            p_ref[:, at : at + step] = weight.astype(jnp.bfloat16)
        ones = jnp.ones((keys, 128), jnp.bfloat16)
        acc = jnp.dot(
            p_ref[...],
            jnp.concatenate([value, ones], axis=1),
            preferred_element_type=jnp.float32,
        )
        score = lax.dot_general(part, fresh_ref[0, :, lanes], NT, preferred_element_type=jnp.float32)
        weight = jnp.where(is_own, jnp.exp(score), 0.0).astype(jnp.bfloat16)
        acc = acc + jnp.dot(
            weight,
            jnp.concatenate([fresh_ref[1, :, lanes], ones[:patch]], axis=1),
            preferred_element_type=jnp.float32,
        )
        numer = jnp.where(low, acc[:rows, :128], acc[rows:, :128])
        out_ref[:, :, lanes] = numer.astype(jnp.bfloat16).reshape(count, patch, 128)
        for half in range(2):
            head = 2 * pair + half
            found = acc[half * rows : (half + 1) * rows, 128:]
            totals = jnp.where((lane == head) | (lane == 16 + head), found, totals)
    coarse = totals.astype(jnp.bfloat16)
    fine = (totals - coarse.astype(jnp.float32)).astype(jnp.bfloat16)
    out_ref[:, :, INNER:] = jnp.where(lane < 16, coarse, fine).reshape(count, patch, 128)


def attend(place, query, fresh, key_parts):
    rows, patch = query.shape[0], fresh.shape[1]
    keys = sum(p.shape[0] for p in key_parts) * patch
    return pl.pallas_call(
        attend_kernel,
        out_shape=jax.ShapeDtypeStruct((rows // patch, patch, INNER + 128), jnp.bfloat16),
        in_specs=[SMEM, VMEM, VMEM] + [HBM] * len(key_parts),
        out_specs=VMEM,
        scratch_shapes=[
            pltpu.VMEM((len(key_parts),) + key_parts[0].shape, jnp.bfloat16),
            pltpu.VMEM((2 * rows, keys), jnp.bfloat16),
            pltpu.SemaphoreType.DMA((len(key_parts),)),
        ],
        compiler_params=pltpu.CompilerParams(vmem_limit_bytes=56 * 1024 * 1024),
        cost_estimate=pl.CostEstimate(
            flops=rows * 4 * keys * INNER,
            bytes_accessed=4 * 1024 * 1024,
            transcendentals=rows * keys * HEADS,
        ),
    )(place, query, fresh, *key_parts)


def combine_kernel(parts_ref, out_ref):
    total = jnp.sum(parts_ref[:, :, INNER:].astype(jnp.float32), axis=0)
    low = lax.broadcasted_iota(jnp.int32, (1, 128), 1) < HEAD_DIM
    for pair in range(HEADS // 2):
        lanes = slice(pair * 128, pair * 128 + 128)
        numer = jnp.sum(parts_ref[:, :, lanes].astype(jnp.float32), axis=0)
        halves = [
            total[:, h : h + 1] + total[:, 16 + h : 17 + h] for h in (2 * pair, 2 * pair + 1)
        ]
        out_ref[:, lanes] = (numer / jnp.where(low, halves[0], halves[1])).astype(jnp.bfloat16)


def combine(parts):
    return pl.pallas_call(
        combine_kernel,
        out_shape=jax.ShapeDtypeStruct((parts.shape[1], INNER), jnp.bfloat16),
        in_specs=[VMEM],
        out_specs=VMEM,
    )(parts)


AXES = ("row", "col")
DEVICES = 256
NX, NY, NZ = 4, 4, 8
SHARE = 0b00100110
REST = 0b11111111 ^ SHARE


def place_of(x, y, z, core):
    return x * 64 + (y // 2) * 32 + z * 4 + (y % 2) * 2 + core


def moved(dx=0, dz=0, dcore=0):
    pairs = []
    for x in range(NX):
        for y in range(NY):
            for z in range(NZ):
                for core in range(2):
                    target = place_of((x + dx) % NX, y, (z + dz) % NZ, (core + dcore) % 2)
                    pairs.append((place_of(x, y, z, core), target))
    return sorted(pairs)


def groups_of(mask):
    found = {}
    for i in range(DEVICES):
        found.setdefault(i & ~mask, []).append(i)
    return list(found.values())


def exchange(value, mask):
    return lax.all_to_all(value, AXES, 0, 0, axis_index_groups=groups_of(mask))


def local(
    latent, gn_gain, gn_bias, w_in, b_in, ln_gain, ln_bias, w_query, w_key, w_value, stale_kv
):
    shared = 8
    with jax.named_scope("keys_z"):
        along_z = [lax.ppermute(stale_kv, AXES, moved(dz=d)) for d in (4, 2, 6)]
    with jax.named_scope("statistics"):
        here = statistics(latent, DEVICES)[:, None, :]
        stats = lax.all_to_all(here, AXES, 0, 0).reshape(DEVICES, 128)
    vectors = jnp.stack([gn_gain, gn_bias, b_in, ln_gain, ln_bias] + [jnp.zeros_like(b_in)] * 3)
    with jax.named_scope("keys_x"):
        line = jnp.stack([stale_kv] + along_z)
        parts = [line] + [lax.ppermute(line, AXES, moved(dx=d)) for d in (1, 3, 2)]
    stream, lnorm, query = project(stats, vectors, latent, w_in, w_query, shared)
    with jax.named_scope("queries"):
        query = exchange(query, SHARE).reshape(shared * latent.shape[0], INNER)
    fresh_kv = fresh_keys(lnorm, w_key, w_value)
    with jax.named_scope("keys_core"):
        parts = parts + [lax.ppermute(part, AXES, moved(dcore=1)) for part in parts]
    row, col = lax.axis_index("row"), lax.axis_index("col")
    place = ((row & 1) << 2) | (((col >> 2) & 1) << 1) | ((col >> 1) & 1)
    place = place.reshape(1).astype(jnp.int32)
    partial = attend(place, query, fresh_kv, parts)
    with jax.named_scope("partials"):
        attended = combine(exchange(partial, SHARE))
    return (stream, fresh_kv, attended)


def solution(mesh):
    placed = (
        P(AXES, None),
        P(),
        P(),
        P(),
        P(),
        P(),
        P(),
        P(),
        P(),
        P(),
        P(None, AXES, None),
    )
    return jax.shard_map(
        local,
        mesh=mesh,
        in_specs=placed,
        out_specs=(P(AXES, None), P(None, AXES, None), P(AXES, None)),
        check_vma=False,
    )
```

time: 515 us -> 76.7 us (0.15)
  waiting for transfers between devices: 276 us -> 7.08 us
  blocking collectives: 152 us -> 12.4 us
  local copies, waits for them, and re-layouts: 46.3 us -> 5.56 us
  starting transfers between devices: 0.04 us -> 29.6 us
  matrix products: 20.9 us -> 0 us
  Pallas kernels: 0 us -> 19.6 us
  between operations: 14.2 us -> 0.83 us
    all_gather x1 -> x0, waiting for transfers between devices: 275 us -> none  [local(): piece = lax.all_gather(stale_kv, ('row', 'col'), axis=1, tiled=True)]
    psum x2 -> x0, blocking collectives: 152 us -> none  [the longest x1 78.9 us: local(): mean = lax.psum(jnp.sum(values_in, axis=(0, 2)), ('row', 'col')) / count]
    slice x3 -> x0, local copies, waits for them, and re-layouts: 44.6 us -> none  [local(): numer, total = pair_terms(query_heads, piece[0], piece[1], factor, blocked)]
    dot_general x8 -> x0, matrix products: 20.9 us -> none  [the longest x2 7.69 us: pair_terms(): jnp.einsum('qhd,khd->hqk', query_heads, key_heads, preferred_element_type...]
    pallas_call x0 -> x5, Pallas kernels: none -> 19.6 us  [the longest x1 7.7 us: attend(): pl.pallas_call(attend_kernel, out_shape=jax.ShapeDtypeStruct((rows // pat...]
    ppermute x0 -> x10, starting transfers between devices: none -> 15.5 us  [the longest x3 10.2 us: local(): along_z = [lax.ppermute(stale_kv, AXES, moved(dz=d)) for d in (4, 2, 6)]]
    all_to_all x0 -> x2, starting transfers between devices: none -> 14.1 us  [the longest x1 10.6 us: local(): stats = lax.all_to_all(here, AXES, 0, 0).reshape(DEVICES, 128)]
    all_to_all x0 -> x1, blocking collectives: none -> 12.4 us  [exchange(): return lax.all_to_all(value, AXES, 0, 0, axis_index_groups=groups_of(mask))]
  transfers between devices with their start and end apart: 1 -> 12, of which waited for: 1 -> 2; matrix products, arithmetic and copies ran while one was open for 2% -> 7% of each run, Pallas kernels for 0% -> 13%
where the time goes in v2:
time: 76.7 us; the launch traced here: 75.9 us
  starting transfers between devices  29.6 us (39%)
  Pallas kernels  19.6 us (26%)
  blocking collectives  12.4 us (16%)
  waiting for transfers between devices  7.08 us (9%)
  local copies, waits for them, and re-layouts  5.56 us (7%)
  other arithmetic  0.94 us (1%)
  between operations  0.83 us (1%)
    all_to_all x1, blocking collectives, exchange(): return lax.all_to_all(value, AXES, 0, 0, axis_index_groups=groups_of(mask))  12.4 us
    all_to_all x1, starting transfers between devices, local(): stats = lax.all_to_all(here, AXES, 0, 0).reshape(DEVICES, 128)  10.6 us
    ppermute x3, starting transfers between devices, local(): along_z = [lax.ppermute(stale_kv, AXES, moved(dz=d)) for d in (4, 2, 6)]  10.2 us
    pallas_call x1, Pallas kernels, attend(): pl.pallas_call(attend_kernel, out_shape=jax.ShapeDtypeStruct((rows // pat...  7.7 us
    pallas_call x1, Pallas kernels, project(): pl.pallas_call(project_kernel, out_shape=(jax.ShapeDtypeStruct((patch, ch...  4.68 us
    all_to_all x1, waiting for transfers between devices, exchange(): return lax.all_to_all(value, AXES, 0, 0, axis_index_groups=groups_of(mask))  4.24 us
    another operation x8, local copies, waits for them, and re-layouts, local(): jnp.stack([gn_gain, gn_bias, b_in, ln_gain, ln_bias] + [jnp.zeros_like(b_...  4.18 us
    ppermute x3, starting transfers between devices, local(): parts = [line] + [lax.ppermute(line, AXES, moved(dx=d)) for d in (1, 3, 2)]  4.18 us
  transfers between devices with their start and end apart: 12, of which 2 were waited for; matrix products, arithmetic and copies ran while one was open for 7% of the time, Pallas kernels for 13%

profile of v2, /device:TPU:2, one launch (start us, length us, event | category | flops | bytes accessed | tf_op | source)
XLA Modules:
  0.0 75.9 jit_solution(9052509086113883632)
XLA Ops:
  0.6 7.3 %collective-permute-start = (bf16[2,32,640]{2,1,0:T(8,128)(2,1)}, bf16[2,32,640]{2,1,0:T(8,128)(2,1)S(1)}, u32[]{:S(2)}, u32[]{:S(2)}) collective-permute-start(bf16[2,32,640]{2,1,0:T(8,128)(2,1)} %param.21), channel_id=1, source_target_pairs={{0,16},{1,17},{2,18},{3,19},{4,20},{5,21},{6,22},{7,23},{8,24},{9,... | collective-permute-start | bytes 245768 | tf_op jit(solution)/shard_map/keys_z/ppermute | solution.py:288
  7.9 0.0 collective-permute-start.2
  7.9 2.9 %collective-permute-start.1 = (bf16[2,32,640]{2,1,0:T(8,128)(2,1)}, bf16[2,32,640]{2,1,0:T(8,128)(2,1)S(1)}, u32[]{:S(2)}, u32[]{:S(2)}) collective-permute-start(bf16[2,32,640]{2,1,0:T(8,128)(2,1)} %param.21), channel_id=1, source_target_pairs={{0,8},{1,9},{2,10},{3,11},{4,12},{5,13},{6,14},{7,15},{8,16},{9,17... | collective-permute-start | bytes 245768 | tf_op jit(solution)/shard_map/keys_z/ppermute | solution.py:288
  10.8 2.2 %statistics.1 = f32[256,128]{1,0:T(8,128)} custom-call(bf16[32,1280]{1,0:T(8,128)(2,1)} %x_ref.3), custom_call_target="tpu_custom_call" | custom-call | tf_op jit(solution)/shard_map/statistics/pallas_call | solution.py:59
  13.1 10.6 %all-to-all-start = ((f32[256,1,128]{2,1,0:T(1,128)}), f32[256,1,128]{2,1,0:T(1,128)S(1)}, u32[]{:S(2)}, u32[]{:S(2)}) async-start(f32[256,1,128]{2,1,0:T(1,128)} %bitcast.11), calls=%async_computation | async-start | bytes 262144 | tf_op jit(solution)/shard_map/statistics/all_to_all | solution.py:291
  23.7 0.0 collective-permute-done
  23.7 0.0 collective-permute-done.2
  23.7 0.9 %pad_maximum_fusion.refs_0_ = bf16[4,2,32,640]{3,2,1,0:T(8,128)(2,1)S(1)} fusion(bf16[1,2,32,640]{3,2,1,0:T(8,128)(2,1)S(1)} %bitcast.15, bf16[1,2,32,640]{3,2,1,0:T(8,128)(2,1)S(1)} %bitcast.16, bf16[1,2,32,640]{3,2,1,0:T(8,128)(2,1)S(1)} %bitcast.14, bf16[1,2,32,640]{3,2,1,0:T(8,128)(2,1)} %bitcast.13), kind=kLoop, calls=%fused_computation | loop fusion | flops 491520 | bytes 655360 | tf_op jit(solution)/shard_map/keys_x/stack | solution.py:294
  24.7 2.2 %collective-permute-start.5 = (bf16[4,2,32,640]{3,2,1,0:T(8,128)(2,1)S(1)}, bf16[4,2,32,640]{3,2,1,0:T(8,128)(2,1)S(1)}, u32[]{:S(2)}, u32[]{:S(2)}) collective-permute-start(bf16[4,2,32,640]{3,2,1,0:T(8,128)(2,1)S(1)} %pad_maximum_fusion.refs_0_), channel_id=1, source_target_pairs={{0,128},{1,129},{2,130},{3,131},{4,132},{5,133},{6,134},{7,135},{8... | collective-permute-start | bytes 983048 | tf_op jit(solution)/shard_map/keys_x/ppermute | solution.py:295
  26.9 1.5 %collective-permute-start.4 = (bf16[4,2,32,640]{3,2,1,0:T(8,128)(2,1)S(1)}, bf16[4,2,32,640]{3,2,1,0:T(8,128)(2,1)S(1)}, u32[]{:S(2)}, u32[]{:S(2)}) collective-permute-start(bf16[4,2,32,640]{3,2,1,0:T(8,128)(2,1)S(1)} %pad_maximum_fusion.refs_0_), channel_id=1, source_target_pairs={{0,192},{1,193},{2,194},{3,195},{4,196},{5,197},{6,198},{7,199},{8... | collective-permute-start | bytes 983048 | tf_op jit(solution)/shard_map/keys_x/ppermute | solution.py:295
  28.3 0.6 collective-permute-start.3
  28.9 0.7 stack.36
  29.6 0.7 stack.37
  30.3 0.7 stack.38
  31.0 0.7 stack.39
  31.7 0.7 stack.40
  32.4 0.7 stack.42.vec_ref
  33.1 2.8 %all-to-all-done = f32[256,1,128]{2,1,0:T(1,128)S(1)} async-done(((f32[256,1,128]{2,1,0:T(1,128)}), f32[256,1,128]{2,1,0:T(1,128)S(1)}, u32[]{:S(2)}, u32[]{:S(2)}) %all-to-all-start) | async-done | bytes 131104 | tf_op jit(solution)/shard_map/statistics/all_to_all | solution.py:291
  35.9 0.6 copy-done
  36.5 4.7 %shard_map.130 = (bf16[32,1280]{1,0:T(8,128)(2,1)}, bf16[32,1280]{1,0:T(8,128)(2,1)}, bf16[8,32,640]{2,1,0:T(8,128)(2,1)}) custom-call(f32[256,128]{1,0:T(8,128)} %bitcast.10, f32[8,1280]{1,0:T(8,128)} %stack.42.vec_ref, bf16[32,1280]{1,0:T(8,128)(2,1)} %x_ref.3, bf16[1280,1280]{1,0:T(8,128)(2,1)} %w_in_ref.1, bf16[1280,640]{1,0:T(8,128)(2,1)} %w_q_hbm.1), custom_call_target="tpu_custom_call" | custom-call | flops 157286400 | bytes 6291456 | tf_op jit(solution)/shard_map/pallas_call | solution.py:109
  41.2 3.4 %all-to-all-start.1 = ((bf16[8,32,640]{2,1,0:T(8,128)(2,1)}), bf16[8,32,640]{2,1,0:T(8,128)(2,1)S(1)}, u32[]{:S(2)}, u32[]{:S(2)}) async-start(bf16[8,32,640]{2,1,0:T(8,128)(2,1)} %get-tuple-element.8), calls=%async_computation.1 | async-start | bytes 655360 | tf_op jit(solution)/shard_map/queries/all_to_all | solution.py:280
  44.7 0.1 collective-permute-start.6
  44.8 0.0 collective-permute-done.5.refs_3_
  44.8 0.5 collective-permute-start.9
  45.3 0.1 collective-permute-start.8
  45.4 0.4 collective-permute-start.7
  45.8 3.2 %shard_map.131.fresh_ref = bf16[2,32,640]{2,1,0:T(8,128)(2,1)} custom-call(bf16[32,1280]{1,0:T(8,128)(2,1)} %get-tuple-element.7.x_ref, bf16[1280,640]{1,0:T(8,128)(2,1)} %w_k_ref.1, bf16[1280,640]{1,0:T(8,128)(2,1)} %w_v_ref.1), custom_call_target="tpu_custom_call" | custom-call | tf_op jit(solution)/shard_map/pallas_call | solution.py:136
  49.1 4.2 %all-to-all-done.1 = bf16[8,32,640]{2,1,0:T(8,128)(2,1)S(1)} async-done(((bf16[8,32,640]{2,1,0:T(8,128)(2,1)}), bf16[8,32,640]{2,1,0:T(8,128)(2,1)S(1)}, u32[]{:S(2)}, u32[]{:S(2)}) %all-to-all-start.1) | async-done | bytes 327712 | tf_op jit(solution)/shard_map/queries/all_to_all | solution.py:280
  53.4 0.7 copy-done.2
  54.0 7.7 %shard_map.132 = bf16[8,32,768]{2,1,0:T(8,128)(2,1)} custom-call(s32[1]{0:T(128)} %bitcast.3.place_ref, bf16[256,640]{1,0:T(8,128)(2,1)} %bitcast.12, bf16[2,32,640]{2,1,0:T(8,128)(2,1)} %shard_map.131.fresh_ref, bf16[4,2,32,640]{3,2,1,0:T(8,128)(2,1)} %copy-done.1, bf16[4,2,32,640]{3,2,1,0:T(8,128)(2,1)} %copy-done.5, bf16[4,2,32,640]{3,2,1,0:T(8,128)(2,1)} %copy-done.4, ...), custom_call_target="tpu_custom_call" | custom-call | flops 671088640 | bytes 4194304 | tf_op jit(solution)/shard_map/pallas_call | solution.py:210
  61.8 12.4 %all_to_all.15.parts_ref = bf16[8,32,768]{2,1,0:T(8,128)(2,1)} all-to-all(bf16[8,32,768]{2,1,0:T(8,128)(2,1)} %shard_map.132), channel_id=1, replica_groups={{0,2,4,6,32,34,36,38},{1,3,5,7,33,35,37,39},{8,10,12,14,40,42,44,46},{9..., dimensions={0} | all-to-all | bytes 786432 | tf_op jit(solution)/shard_map/partials/all_to_all | solution.py:280
  74.1 1.8 %partials.1 = bf16[32,640]{1,0:T(8,128)(2,1)} custom-call(bf16[8,32,768]{2,1,0:T(8,128)(2,1)} %all_to_all.15.parts_ref), custom_call_target="tpu_custom_call" | custom-call | tf_op jit(solution)/shard_map/partials/pallas_call | solution.py:242
  (27 shorter events, 0.1 us)
Async XLA Ops:
  0.6 23.1 %collective-permute-start = (bf16[2,32,640]{2,1,0:T(8,128)(2,1)}, bf16[2,32,640]{2,1,0:T(8,128)(2,1)S(1)}, u32[]{:S(2)}, u32[]{:S(2)}) collective-permute-start(bf16[2,32,640]{2,1,0:T(8,128)(2,1)} %param.21), channel_id=1, source_target_pairs={{0,16},{1,17},{2,18},{3,19},{4,20},{5,21},{6,22},{7,23},{8,24},{9,... | collective-permute-start | bytes 245768 | tf_op jit(solution)/shard_map/keys_z/ppermute | solution.py:288
  7.9 15.8 %collective-permute-start.2 = (bf16[2,32,640]{2,1,0:T(8,128)(2,1)}, bf16[2,32,640]{2,1,0:T(8,128)(2,1)S(1)}, u32[]{:S(2)}, u32[]{:S(2)}) collective-permute-start(bf16[2,32,640]{2,1,0:T(8,128)(2,1)} %param.21), channel_id=1, source_target_pairs={{0,24},{1,25},{2,26},{3,27},{4,28},{5,29},{6,30},{7,31},{8,0},{9,1... | collective-permute-start | bytes 245768 | tf_op jit(solution)/shard_map/keys_z/ppermute | solution.py:288
  7.9 15.8 %collective-permute-start.1 = (bf16[2,32,640]{2,1,0:T(8,128)(2,1)}, bf16[2,32,640]{2,1,0:T(8,128)(2,1)S(1)}, u32[]{:S(2)}, u32[]{:S(2)}) collective-permute-start(bf16[2,32,640]{2,1,0:T(8,128)(2,1)} %param.21), channel_id=1, source_target_pairs={{0,8},{1,9},{2,10},{3,11},{4,12},{5,13},{6,14},{7,15},{8,16},{9,17... | collective-permute-start | bytes 245768 | tf_op jit(solution)/shard_map/keys_z/ppermute | solution.py:288
  13.1 22.8 %all-to-all-start = ((f32[256,1,128]{2,1,0:T(1,128)}), f32[256,1,128]{2,1,0:T(1,128)S(1)}, u32[]{:S(2)}, u32[]{:S(2)}) async-start(f32[256,1,128]{2,1,0:T(1,128)} %bitcast.11), calls=%async_computation | async-start | bytes 262144 | tf_op jit(solution)/shard_map/statistics/all_to_all | solution.py:291
  24.7 28.6 %copy-start.1 = (bf16[4,2,32,640]{3,2,1,0:T(8,128)(2,1)}, bf16[4,2,32,640]{3,2,1,0:T(8,128)(2,1)S(1)}, u32[]{:S(2)}) copy-start(bf16[4,2,32,640]{3,2,1,0:T(8,128)(2,1)S(1)} %pad_maximum_fusion.refs_0_) | copy-start | bytes 983044
  24.7 20.1 %collective-permute-start.5 = (bf16[4,2,32,640]{3,2,1,0:T(8,128)(2,1)S(1)}, bf16[4,2,32,640]{3,2,1,0:T(8,128)(2,1)S(1)}, u32[]{:S(2)}, u32[]{:S(2)}) collective-permute-start(bf16[4,2,32,640]{3,2,1,0:T(8,128)(2,1)S(1)} %pad_maximum_fusion.refs_0_), channel_id=1, source_target_pairs={{0,128},{1,129},{2,130},{3,131},{4,132},{5,133},{6,134},{7,135},{8... | collective-permute-start | bytes 983048 | tf_op jit(solution)/shard_map/keys_x/ppermute | solution.py:295
  26.9 18.4 %collective-permute-start.4 = (bf16[4,2,32,640]{3,2,1,0:T(8,128)(2,1)S(1)}, bf16[4,2,32,640]{3,2,1,0:T(8,128)(2,1)S(1)}, u32[]{:S(2)}, u32[]{:S(2)}) collective-permute-start(bf16[4,2,32,640]{3,2,1,0:T(8,128)(2,1)S(1)} %pad_maximum_fusion.refs_0_), channel_id=1, source_target_pairs={{0,192},{1,193},{2,194},{3,195},{4,196},{5,197},{6,198},{7,199},{8... | collective-permute-start | bytes 983048 | tf_op jit(solution)/shard_map/keys_x/ppermute | solution.py:295
  28.3 17.1 %collective-permute-start.3 = (bf16[4,2,32,640]{3,2,1,0:T(8,128)(2,1)S(1)}, bf16[4,2,32,640]{3,2,1,0:T(8,128)(2,1)S(1)}, u32[]{:S(2)}, u32[]{:S(2)}) collective-permute-start(bf16[4,2,32,640]{3,2,1,0:T(8,128)(2,1)S(1)} %pad_maximum_fusion.refs_0_), channel_id=1, source_target_pairs={{0,64},{1,65},{2,66},{3,67},{4,68},{5,69},{6,70},{7,71},{8,72},{9,... | collective-permute-start | bytes 983048 | tf_op jit(solution)/shard_map/keys_x/ppermute | solution.py:295
  35.9 0.6 copy-start
  41.2 12.1 %all-to-all-start.1 = ((bf16[8,32,640]{2,1,0:T(8,128)(2,1)}), bf16[8,32,640]{2,1,0:T(8,128)(2,1)S(1)}, u32[]{:S(2)}, u32[]{:S(2)}) async-start(bf16[8,32,640]{2,1,0:T(8,128)(2,1)} %get-tuple-element.8), calls=%async_computation.1 | async-start | bytes 655360 | tf_op jit(solution)/shard_map/queries/all_to_all | solution.py:280
  44.7 4.3 %collective-permute-start.6 = (bf16[4,2,32,640]{3,2,1,0:T(8,128)(2,1)S(1)}, bf16[4,2,32,640]{3,2,1,0:T(8,128)(2,1)S(1)}, u32[]{:S(2)}, u32[]{:S(2)}) collective-permute-start(bf16[4,2,32,640]{3,2,1,0:T(8,128)(2,1)S(1)} %pad_maximum_fusion.refs_0_), channel_id=1, source_target_pairs={{0,1},{1,0},{2,3},{3,2},{4,5},{5,4},{6,7},{7,6},{8,9},{9,8},{10,11... | collective-permute-start | bytes 983048 | tf_op jit(solution)/shard_map/keys_core/ppermute | solution.py:301
  44.8 4.2 %copy-start.3 = (bf16[4,2,32,640]{3,2,1,0:T(8,128)(2,1)}, bf16[4,2,32,640]{3,2,1,0:T(8,128)(2,1)S(1)}, u32[]{:S(2)}) copy-start(bf16[4,2,32,640]{3,2,1,0:T(8,128)(2,1)S(1)} %collective-permute-done.5.refs_3_) | copy-start | bytes 983044
  44.8 4.2 %collective-permute-start.9 = (bf16[4,2,32,640]{3,2,1,0:T(8,128)(2,1)S(1)}, bf16[4,2,32,640]{3,2,1,0:T(8,128)(2,1)S(1)}, u32[]{:S(2)}, u32[]{:S(2)}) collective-permute-start(bf16[4,2,32,640]{3,2,1,0:T(8,128)(2,1)S(1)} %collective-permute-done.5.refs_3_), channel_id=1, source_target_pairs={{0,1},{1,0},{2,3},{3,2},{4,5},{5,4},{6,7},{7,6},{8,9},{9,8},{10,11... | collective-permute-start | bytes 983048 | tf_op jit(solution)/shard_map/keys_core/ppermute | solution.py:301
  45.3 3.7 %copy-start.4 = (bf16[4,2,32,640]{3,2,1,0:T(8,128)(2,1)}, bf16[4,2,32,640]{3,2,1,0:T(8,128)(2,1)S(1)}, u32[]{:S(2)}) copy-start(bf16[4,2,32,640]{3,2,1,0:T(8,128)(2,1)S(1)} %collective-permute-done.4.refs_2_) | copy-start | bytes 983044
  45.3 3.8 %collective-permute-start.8 = (bf16[4,2,32,640]{3,2,1,0:T(8,128)(2,1)S(1)}, bf16[4,2,32,640]{3,2,1,0:T(8,128)(2,1)S(1)}, u32[]{:S(2)}, u32[]{:S(2)}) collective-permute-start(bf16[4,2,32,640]{3,2,1,0:T(8,128)(2,1)S(1)} %collective-permute-done.4.refs_2_), channel_id=1, source_target_pairs={{0,1},{1,0},{2,3},{3,2},{4,5},{5,4},{6,7},{7,6},{8,9},{9,8},{10,11... | collective-permute-start | bytes 983048 | tf_op jit(solution)/shard_map/keys_core/ppermute | solution.py:301
  45.4 3.6 %copy-start.5 = (bf16[4,2,32,640]{3,2,1,0:T(8,128)(2,1)}, bf16[4,2,32,640]{3,2,1,0:T(8,128)(2,1)S(1)}, u32[]{:S(2)}) copy-start(bf16[4,2,32,640]{3,2,1,0:T(8,128)(2,1)S(1)} %collective-permute-done.3.refs_1_) | copy-start | bytes 983044
  45.4 3.7 %collective-permute-start.7 = (bf16[4,2,32,640]{3,2,1,0:T(8,128)(2,1)S(1)}, bf16[4,2,32,640]{3,2,1,0:T(8,128)(2,1)S(1)}, u32[]{:S(2)}, u32[]{:S(2)}) collective-permute-start(bf16[4,2,32,640]{3,2,1,0:T(8,128)(2,1)S(1)} %collective-permute-done.3.refs_1_), channel_id=1, source_target_pairs={{0,1},{1,0},{2,3},{3,2},{4,5},{5,4},{6,7},{7,6},{8,9},{9,8},{10,11... | collective-permute-start | bytes 983048 | tf_op jit(solution)/shard_map/keys_core/ppermute | solution.py:301
  49.0 4.3 %copy-start.6 = (bf16[4,2,32,640]{3,2,1,0:T(8,128)(2,1)}, bf16[4,2,32,640]{3,2,1,0:T(8,128)(2,1)S(1)}, u32[]{:S(2)}) copy-start(bf16[4,2,32,640]{3,2,1,0:T(8,128)(2,1)S(1)} %collective-permute-done.6.refs_4_) | copy-start | bytes 983044
  49.0 4.3 %copy-start.7 = (bf16[4,2,32,640]{3,2,1,0:T(8,128)(2,1)}, bf16[4,2,32,640]{3,2,1,0:T(8,128)(2,1)S(1)}, u32[]{:S(2)}) copy-start(bf16[4,2,32,640]{3,2,1,0:T(8,128)(2,1)S(1)} %collective-permute-done.9.refs_7_) | copy-start | bytes 983044
  49.0 4.3 %copy-start.8 = (bf16[4,2,32,640]{3,2,1,0:T(8,128)(2,1)}, bf16[4,2,32,640]{3,2,1,0:T(8,128)(2,1)S(1)}, u32[]{:S(2)}) copy-start(bf16[4,2,32,640]{3,2,1,0:T(8,128)(2,1)S(1)} %collective-permute-done.8.refs_6_) | copy-start | bytes 983044
  49.1 4.3 %copy-start.9 = (bf16[4,2,32,640]{3,2,1,0:T(8,128)(2,1)}, bf16[4,2,32,640]{3,2,1,0:T(8,128)(2,1)S(1)}, u32[]{:S(2)}) copy-start(bf16[4,2,32,640]{3,2,1,0:T(8,128)(2,1)S(1)} %collective-permute-done.7.refs_5_) | copy-start | bytes 983044
  53.3 0.7 copy-start.2

commit v3 on v2

--- a/solution.py
+++ b/solution.py
@@ -61,13 +61,22 @@
         out_shape=jax.ShapeDtypeStruct((peers, 128), jnp.float32),
         in_specs=[VMEM],
         out_specs=VMEM,
+        compiler_params=pltpu.CompilerParams(vmem_limit_bytes=8 * 1024 * 1024),
     )(x)
 
 
-def project_kernel(stats_ref, vec_ref, x_ref, w_in_ref, w_q_hbm, stream_ref, lnorm_ref, query_ref, w_q_ref, sem):
-    copy = pltpu.make_async_copy(w_q_hbm, w_q_ref, sem)
-    copy.start()
+def project_kernel(stats_ref, gain_ref, bias_ref, b_in_ref, ln_gain_ref, ln_bias_ref, x_ref, *refs):
+    w_in_hbm, w_q_hbm, stream_ref, lnorm_ref, query_ref, w_in_ref, w_q_ref, sems = refs
     rows, chans = x_ref.shape
+    parts = w_in_ref.shape[0] // 320
+    copies = [
+        pltpu.make_async_copy(
+            w_in_hbm.at[pl.ds(i * 320, 320)], w_in_ref.at[pl.ds(i * 320, 320)], sems.at[i]
+        )
+        for i in range(parts)
+    ] + [pltpu.make_async_copy(w_q_hbm, w_q_ref, sems.at[parts])]
+    for copy in copies:
+        copy.start()
 
     peers = stats_ref.shape[0]
     entries = rows * (chans // GROUPS)
@@ -81,23 +90,35 @@
     )
     square = jnp.where(lane < GROUPS, square, 0.0)
     member = member_of(chans)
-    mean = to_channels(mean, member)
-    scale = to_channels(lax.rsqrt(square * (1.0 / (entries * peers)) + 1e-06), member)
+    scale = lax.rsqrt(square * (1.0 / (entries * peers)) + 1e-06)
+    both = lax.dot_general(
+        jnp.concatenate([pieces(mean), pieces(scale)], axis=0),
+        member,
+        NT,
+        preferred_element_type=jnp.float32,
+    )
+    mean = both[0:1] + both[1:2] + both[2:3]
+    scale = both[3:4] + both[4:5] + both[5:6]
+
+    def row(ref):
+        return ref[...].reshape(1, chans)
 
     x = x_ref[...].astype(jnp.float32)
-    normed = ((x - mean) * scale * vec_ref[0:1] + vec_ref[1:2]).astype(jnp.bfloat16)
-    stream = (
-        jnp.dot(normed, w_in_ref[...], preferred_element_type=jnp.float32) + vec_ref[2:3]
-    ).astype(jnp.bfloat16)
+    normed = ((x - mean) * scale * row(gain_ref) + row(bias_ref)).astype(jnp.bfloat16)
+    stream = row(b_in_ref)
+    for i in range(parts):
+        copies[i].wait()
+    stream = stream + jnp.dot(normed, w_in_ref[...], preferred_element_type=jnp.float32)
+    stream = stream.astype(jnp.bfloat16)
     stream_ref[...] = stream
     wide = stream.astype(jnp.float32)
     token_mean = jnp.mean(wide, axis=-1, keepdims=True)
     token_dev = wide - token_mean
     token_var = jnp.mean(token_dev * token_dev, axis=-1, keepdims=True)
-    lnorm = token_dev * lax.rsqrt(token_var + 1e-05) * vec_ref[3:4] + vec_ref[4:5]
+    lnorm = token_dev * lax.rsqrt(token_var + 1e-05) * row(ln_gain_ref) + row(ln_bias_ref)
     lnorm = lnorm.astype(jnp.bfloat16)
     lnorm_ref[...] = lnorm
-    copy.wait()
+    copies[parts].wait()
     query = jnp.dot(lnorm, w_q_ref[...], preferred_element_type=jnp.float32)
     query = query.astype(jnp.bfloat16) * jnp.bfloat16(1.0 / math.sqrt(HEAD_DIM))
     query_ref[...] = jnp.broadcast_to(query[None], query_ref.shape)
@@ -113,21 +134,32 @@
             jax.ShapeDtypeStruct((patch, chans), bf16),
             jax.ShapeDtypeStruct((copies, patch, INNER), bf16),
         ),
-        in_specs=[VMEM] * 4 + [HBM],
+        in_specs=[VMEM] * 7 + [HBM] * 2,
         out_specs=(VMEM, VMEM, VMEM),
-        scratch_shapes=[pltpu.VMEM(w_query.shape, bf16), pltpu.SemaphoreType.DMA(())],
+        scratch_shapes=[
+            pltpu.VMEM(w_in.shape, bf16),
+            pltpu.VMEM(w_query.shape, bf16),
+            pltpu.SemaphoreType.DMA((5,)),
+        ],
         compiler_params=pltpu.CompilerParams(vmem_limit_bytes=56 * 1024 * 1024),
         cost_estimate=pl.CostEstimate(
             flops=patch * 2 * chans * (chans + INNER),
             bytes_accessed=6 * 1024 * 1024,
             transcendentals=patch,
         ),
-    )(stats, vectors, x, w_in, w_query)
-
-
-def fresh_kernel(x_ref, w_k_ref, w_v_ref, out_ref):
-    for i, w_ref in enumerate((w_k_ref, w_v_ref)):
-        out_ref[i] = jnp.dot(x_ref[...], w_ref[...], preferred_element_type=jnp.float32).astype(
+    )(stats, *vectors, x, w_in, w_query)
+
+
+def fresh_kernel(x_ref, w_k_hbm, w_v_hbm, out_ref, w_ref, sems):
+    copies = [
+        pltpu.make_async_copy(source, w_ref.at[i], sems.at[i])
+        for i, source in enumerate((w_k_hbm, w_v_hbm))
+    ]
+    for copy in copies:
+        copy.start()
+    for i, copy in enumerate(copies):
+        copy.wait()
+        out_ref[i] = jnp.dot(x_ref[...], w_ref[i], preferred_element_type=jnp.float32).astype(
             jnp.bfloat16
         )
 
@@ -136,14 +168,21 @@
     return pl.pallas_call(
         fresh_kernel,
         out_shape=jax.ShapeDtypeStruct((2, x.shape[0], INNER), jnp.bfloat16),
-        in_specs=[VMEM] * 3,
+        in_specs=[VMEM, HBM, HBM],
         out_specs=VMEM,
+        scratch_shapes=[
+            pltpu.VMEM((2,) + w_key.shape, jnp.bfloat16),
+            pltpu.SemaphoreType.DMA((2,)),
+        ],
         compiler_params=pltpu.CompilerParams(vmem_limit_bytes=56 * 1024 * 1024),
     )(x, w_key, w_value)
 
 
-def attend_kernel(place_ref, q_ref, fresh_ref, *refs):
-    sources, (out_ref, kv_ref, p_ref, sems) = refs[:-4], refs[-4:]
+def attend_kernel(place_ref, q_hbm, fresh_ref, *refs):
+    sources, refs = refs[:-9], refs[-9:]
+    out_ref, kv_ref, p_ref, q_ref, more_ref, numer_ref, total_ref, sems, q_sem = refs
+    q_copy = pltpu.make_async_copy(q_hbm, q_ref, q_sem)
+    q_copy.start()
     copies = [
         pltpu.make_async_copy(source, kv_ref.at[i], sems.at[i])
         for i, source in enumerate(sources)
@@ -153,55 +192,78 @@
     patch = fresh_ref.shape[1]
     rows = q_ref.shape[0]
     count = rows // patch
-    own = place_ref[0] * patch
+    place = place_ref[0]
+    own = place * patch
+    lane = lax.broadcasted_iota(jnp.int32, (1, 128), 1)
+    low = lane < HEAD_DIM
+    pairs = [slice(at * 128, at * 128 + 128) for at in range(HEADS // 2)]
+
+    def two_heads(part):
+        zero = jnp.zeros_like(part)
+        return jnp.concatenate([jnp.where(low, part, zero), jnp.where(low, zero, part)], axis=0)
+
+    def with_ones(value):
+        return jnp.concatenate([value, jnp.ones((value.shape[0], 128), jnp.bfloat16)], axis=1)
+
+    q_copy.wait()
+    for pair, lanes in enumerate(pairs):
+        score = lax.dot_general(
+            two_heads(q_ref[pl.ds(own, patch), lanes]),
+            fresh_ref[0, :, lanes],
+            NT,
+            preferred_element_type=jnp.float32,
+        )
+        more_ref[pair] = jnp.dot(
+            jnp.exp(score).astype(jnp.bfloat16),
+            with_ones(fresh_ref[1, :, lanes]),
+            preferred_element_type=jnp.float32,
+        )
     for copy in copies:
         copy.wait()
-    keys = kv_ref.shape[0] * kv_ref.shape[1] * patch
-    lane = lax.broadcasted_iota(jnp.int32, (1, 128), 1)
-    low = lane < HEAD_DIM
+
+    keys = p_ref.shape[1]
     row = lax.broadcasted_iota(jnp.int32, (2 * rows, 1), 0)
     row = jnp.where(row >= rows, row - rows, row)
     is_own = (row >= own) & (row < own + patch)
     totals = jnp.zeros((rows, 128), jnp.float32)
-    for pair in range(HEADS // 2):
-        lanes = slice(pair * 128, pair * 128 + 128)
-        part = q_ref[:, lanes]
-        zero = jnp.zeros_like(part)
-        part = jnp.concatenate([jnp.where(low, part, zero), jnp.where(low, zero, part)], axis=0)
+    own_totals = jnp.zeros((patch, 128), jnp.float32)
+    step = 128
+    for pair, lanes in enumerate(pairs):
+        query = two_heads(q_ref[:, lanes])
         key = kv_ref[:, :, 0, :, lanes].reshape(keys, 128)
         value = kv_ref[:, :, 1, :, lanes].reshape(keys, 128)
-        step = 128
         for at in range(0, keys, step):
             score = lax.dot_general(
-                part, key[at : at + step], NT, preferred_element_type=jnp.float32
+                query, key[at : at + step], NT, preferred_element_type=jnp.float32
             )
             weight = jnp.exp(score)
             if at == 0:
                 column = lax.broadcasted_iota(jnp.int32, (1, step), 1)
                 weight = jnp.where(is_own & (column < patch), 0.0, weight)
             p_ref[:, at : at + step] = weight.astype(jnp.bfloat16)
-        ones = jnp.ones((keys, 128), jnp.bfloat16)
-        acc = jnp.dot(
-            p_ref[...],
-            jnp.concatenate([value, ones], axis=1),
-            preferred_element_type=jnp.float32,
-        )
-        score = lax.dot_general(part, fresh_ref[0, :, lanes], NT, preferred_element_type=jnp.float32)
-        weight = jnp.where(is_own, jnp.exp(score), 0.0).astype(jnp.bfloat16)
-        acc = acc + jnp.dot(
-            weight,
-            jnp.concatenate([fresh_ref[1, :, lanes], ones[:patch]], axis=1),
-            preferred_element_type=jnp.float32,
-        )
+        acc = jnp.dot(p_ref[...], with_ones(value), preferred_element_type=jnp.float32)
         numer = jnp.where(low, acc[:rows, :128], acc[rows:, :128])
         out_ref[:, :, lanes] = numer.astype(jnp.bfloat16).reshape(count, patch, 128)
+        numer_ref[...] = numer
+        more = more_ref[pair]
+        mine = numer_ref[pl.ds(own, patch), :] + jnp.where(
+            low, more[:patch, :128], more[patch:, :128]
+        )
+        out_ref[place, :, lanes] = mine.astype(jnp.bfloat16)
         for half in range(2):
             head = 2 * pair + half
-            found = acc[half * rows : (half + 1) * rows, 128:]
-            totals = jnp.where((lane == head) | (lane == 16 + head), found, totals)
-    coarse = totals.astype(jnp.bfloat16)
-    fine = (totals - coarse.astype(jnp.float32)).astype(jnp.bfloat16)
-    out_ref[:, :, INNER:] = jnp.where(lane < 16, coarse, fine).reshape(count, patch, 128)
+            here = (lane == head) | (lane == 16 + head)
+            totals = jnp.where(here, acc[half * rows : (half + 1) * rows, 128:], totals)
+            own_totals = jnp.where(here, more[half * patch : (half + 1) * patch, 128:], own_totals)
+
+    def coded(total):
+        coarse = total.astype(jnp.bfloat16)
+        fine = (total - coarse.astype(jnp.float32)).astype(jnp.bfloat16)
+        return jnp.where(lane < 16, coarse, fine)
+
+    out_ref[:, :, INNER:] = coded(totals).reshape(count, patch, 128)
+    total_ref[...] = totals
+    out_ref[place, :, INNER:] = coded(total_ref[pl.ds(own, patch), :] + own_totals)
 
 
 def attend(place, query, fresh, key_parts):
@@ -210,12 +272,17 @@
     return pl.pallas_call(
         attend_kernel,
         out_shape=jax.ShapeDtypeStruct((rows // patch, patch, INNER + 128), jnp.bfloat16),
-        in_specs=[SMEM, VMEM, VMEM] + [HBM] * len(key_parts),
+        in_specs=[SMEM, HBM, VMEM] + [HBM] * len(key_parts),
         out_specs=VMEM,
         scratch_shapes=[
             pltpu.VMEM((len(key_parts),) + key_parts[0].shape, jnp.bfloat16),
             pltpu.VMEM((2 * rows, keys), jnp.bfloat16),
+            pltpu.VMEM(query.shape, jnp.bfloat16),
+            pltpu.VMEM((HEADS // 2, 2 * patch, 256), jnp.float32),
+            pltpu.VMEM((rows, 128), jnp.float32),
+            pltpu.VMEM((rows, 128), jnp.float32),
             pltpu.SemaphoreType.DMA((len(key_parts),)),
+            pltpu.SemaphoreType.DMA(()),
         ],
         compiler_params=pltpu.CompilerParams(vmem_limit_bytes=56 * 1024 * 1024),
         cost_estimate=pl.CostEstimate(
@@ -244,6 +311,7 @@
         out_shape=jax.ShapeDtypeStruct((parts.shape[1], INNER), jnp.bfloat16),
         in_specs=[VMEM],
         out_specs=VMEM,
+        compiler_params=pltpu.CompilerParams(vmem_limit_bytes=8 * 1024 * 1024),
     )(parts)
 
 
@@ -289,7 +357,7 @@
     with jax.named_scope("statistics"):
         here = statistics(latent, DEVICES)[:, None, :]
         stats = lax.all_to_all(here, AXES, 0, 0).reshape(DEVICES, 128)
-    vectors = jnp.stack([gn_gain, gn_bias, b_in, ln_gain, ln_bias] + [jnp.zeros_like(b_in)] * 3)
+    vectors = [gn_gain, gn_bias, b_in, ln_gain, ln_bias]
     with jax.named_scope("keys_x"):
         line = jnp.stack([stale_kv] + along_z)
         parts = [line] + [lax.ppermute(line, AXES, moved(dx=d)) for d in (1, 3, 2)]

time: 76.7 us -> 74.5 us (0.971)
  waiting for transfers between devices: 7.08 us -> 10.6 us
  local copies, waits for them, and re-layouts: 5.56 us -> 2.27 us
  Pallas kernels: 19.6 us -> 17.9 us
    all_to_all x1, waiting for transfers between devices: 2.81 us -> 7.01 us  [local(): stats = lax.all_to_all(here, AXES, 0, 0).reshape(DEVICES, 128)]
    another operation x8 -> x0, local copies, waits for them, and re-layouts: 4.18 us -> none  [local(): jnp.stack([gn_gain, gn_bias, b_in, ln_gain, ln_bias] + [jnp.zeros_like(b_...]
    pallas_call x1, Pallas kernels: 1.83 us -> 0.83 us  [combine(): pl.pallas_call(combine_kernel, out_shape=jax.ShapeDtypeStruct((parts.shap...]
    unnamed x20 -> x22, local copies, waits for them, and re-layouts: 1.37 us -> 2.27 us
    pallas_call x1, Pallas kernels: 2.23 us -> 1.35 us  [statistics(): pl.pallas_call(statistics_kernel, out_shape=jax.ShapeDtypeStruct((peers,...]
    pallas_call x1, Pallas kernels: 7.7 us -> 6.85 us  [attend(): pl.pallas_call(attend_kernel, out_shape=jax.ShapeDtypeStruct((rows // pat...]
  transfers between devices with their start and end apart: 12 -> 12, of which waited for: 2 -> 2; matrix products, arithmetic and copies ran while one was open for 7% -> 1% of each run, Pallas kernels for 13% -> 14%
where the time goes in v3:
time: 74.5 us; the launch traced here: 73.9 us
  starting transfers between devices  29.6 us (40%)
  Pallas kernels  17.9 us (24%)
  blocking collectives  11.8 us (16%)
  waiting for transfers between devices  10.6 us (14%)
  local copies, waits for them, and re-layouts  2.27 us (3%)
  other arithmetic  0.94 us (1%)
  between operations  0.85 us (1%)
    all_to_all x1, blocking collectives, exchange(): return lax.all_to_all(value, AXES, 0, 0, axis_index_groups=groups_of(mask))  11.8 us
    all_to_all x1, starting transfers between devices, local(): stats = lax.all_to_all(here, AXES, 0, 0).reshape(DEVICES, 128)  10.6 us
    ppermute x3, starting transfers between devices, local(): along_z = [lax.ppermute(stale_kv, AXES, moved(dz=d)) for d in (4, 2, 6)]  10.2 us
    all_to_all x1, waiting for transfers between devices, local(): stats = lax.all_to_all(here, AXES, 0, 0).reshape(DEVICES, 128)  7.01 us
    pallas_call x1, Pallas kernels, attend(): pl.pallas_call(attend_kernel, out_shape=jax.ShapeDtypeStruct((rows // pat...  6.85 us
    pallas_call x1, Pallas kernels, project(): pl.pallas_call(project_kernel, out_shape=(jax.ShapeDtypeStruct((patch, ch...  5.05 us
    ppermute x3, starting transfers between devices, local(): parts = [line] + [lax.ppermute(line, AXES, moved(dx=d)) for d in (1, 3, 2)]  4.18 us
    pallas_call x1, Pallas kernels, fresh_keys(): pl.pallas_call(fresh_kernel, out_shape=jax.ShapeDtypeStruct((2, x.shape[0...  3.86 us
  transfers between devices with their start and end apart: 12, of which 2 were waited for; matrix products, arithmetic and copies ran while one was open for 1% of the time, Pallas kernels for 14%

profile of v3, /device:TPU:2, one launch (start us, length us, event | category | flops | bytes accessed | tf_op | source)
XLA Modules:
  0.0 73.9 jit_solution(685382579217760040)
XLA Ops:
  0.6 7.3 %collective-permute-start = (bf16[2,32,640]{2,1,0:T(8,128)(2,1)}, bf16[2,32,640]{2,1,0:T(8,128)(2,1)S(1)}, u32[]{:S(2)}, u32[]{:S(2)}) collective-permute-start(bf16[2,32,640]{2,1,0:T(8,128)(2,1)} %param.21), channel_id=1, source_target_pairs={{0,16},{1,17},{2,18},{3,19},{4,20},{5,21},{6,22},{7,23},{8,24},{9,... | collective-permute-start | bytes 245768 | tf_op jit(solution)/shard_map/keys_z/ppermute | solution.py:356
  7.9 0.0 collective-permute-start.2
  7.9 2.9 %collective-permute-start.1 = (bf16[2,32,640]{2,1,0:T(8,128)(2,1)}, bf16[2,32,640]{2,1,0:T(8,128)(2,1)S(1)}, u32[]{:S(2)}, u32[]{:S(2)}) collective-permute-start(bf16[2,32,640]{2,1,0:T(8,128)(2,1)} %param.21), channel_id=1, source_target_pairs={{0,8},{1,9},{2,10},{3,11},{4,12},{5,13},{6,14},{7,15},{8,16},{9,17... | collective-permute-start | bytes 245768 | tf_op jit(solution)/shard_map/keys_z/ppermute | solution.py:356
  10.8 0.9 %copy-done = bf16[32,1280]{1,0:T(8,128)(2,1)S(1)} copy-done((bf16[32,1280]{1,0:T(8,128)(2,1)S(1)}, bf16[32,1280]{1,0:T(8,128)(2,1)}, u32[]{:S(2)}) %copy-start) | copy-done | bytes 81944
  11.7 1.3 %statistics.1 = f32[256,128]{1,0:T(8,128)} custom-call(bf16[32,1280]{1,0:T(8,128)(2,1)S(1)} %copy-done), custom_call_target="tpu_custom_call" | custom-call | tf_op jit(solution)/shard_map/statistics/pallas_call | solution.py:59
  13.1 10.6 %all-to-all-start = ((f32[256,1,128]{2,1,0:T(1,128)}), f32[256,1,128]{2,1,0:T(1,128)S(1)}, u32[]{:S(2)}, u32[]{:S(2)}) async-start(f32[256,1,128]{2,1,0:T(1,128)} %bitcast.1), calls=%async_computation | async-start | bytes 262144 | tf_op jit(solution)/shard_map/statistics/all_to_all | solution.py:359
  23.7 0.0 collective-permute-done
  23.7 0.0 collective-permute-done.2
  23.7 0.0 collective-permute-done.1
  23.7 0.9 %pad_maximum_fusion.refs_0_ = bf16[4,2,32,640]{3,2,1,0:T(8,128)(2,1)S(1)} fusion(bf16[1,2,32,640]{3,2,1,0:T(8,128)(2,1)S(1)} %bitcast.14, bf16[1,2,32,640]{3,2,1,0:T(8,128)(2,1)S(1)} %bitcast.15, bf16[1,2,32,640]{3,2,1,0:T(8,128)(2,1)S(1)} %bitcast.13, bf16[1,2,32,640]{3,2,1,0:T(8,128)(2,1)} %bitcast.12), kind=kLoop, calls=%fused_computation | loop fusion | flops 491520 | bytes 655360 | tf_op jit(solution)/shard_map/keys_x/stack | solution.py:362
  24.7 2.2 %collective-permute-start.5 = (bf16[4,2,32,640]{3,2,1,0:T(8,128)(2,1)S(1)}, bf16[4,2,32,640]{3,2,1,0:T(8,128)(2,1)S(1)}, u32[]{:S(2)}, u32[]{:S(2)}) collective-permute-start(bf16[4,2,32,640]{3,2,1,0:T(8,128)(2,1)S(1)} %pad_maximum_fusion.refs_0_), channel_id=1, source_target_pairs={{0,128},{1,129},{2,130},{3,131},{4,132},{5,133},{6,134},{7,135},{8... | collective-permute-start | bytes 983048 | tf_op jit(solution)/shard_map/keys_x/ppermute | solution.py:363
  26.9 1.5 %collective-permute-start.4 = (bf16[4,2,32,640]{3,2,1,0:T(8,128)(2,1)S(1)}, bf16[4,2,32,640]{3,2,1,0:T(8,128)(2,1)S(1)}, u32[]{:S(2)}, u32[]{:S(2)}) collective-permute-start(bf16[4,2,32,640]{3,2,1,0:T(8,128)(2,1)S(1)} %pad_maximum_fusion.refs_0_), channel_id=1, source_target_pairs={{0,192},{1,193},{2,194},{3,195},{4,196},{5,197},{6,198},{7,199},{8... | collective-permute-start | bytes 983048 | tf_op jit(solution)/shard_map/keys_x/ppermute | solution.py:363
  28.3 0.6 collective-permute-start.3
  28.9 7.0 %all-to-all-done = f32[256,1,128]{2,1,0:T(1,128)S(1)} async-done(((f32[256,1,128]{2,1,0:T(1,128)}), f32[256,1,128]{2,1,0:T(1,128)S(1)}, u32[]{:S(2)}, u32[]{:S(2)}) %all-to-all-start) | async-done | bytes 131104 | tf_op jit(solution)/shard_map/statistics/all_to_all | solution.py:359
  35.9 0.6 copy-done.1
  36.5 5.0 %shard_map.130 = (bf16[32,1280]{1,0:T(8,128)(2,1)}, bf16[32,1280]{1,0:T(8,128)(2,1)}, bf16[8,32,640]{2,1,0:T(8,128)(2,1)}) custom-call(f32[256,128]{1,0:T(8,128)} %bitcast.10, f32[1280]{0:T(1024)} %gain_ref.1, f32[1280]{0:T(1024)} %bias_ref.1, f32[1280]{0:T(1024)} %b_in_ref.1, f32[1280]{0:T(1024)} %ln_gain_ref.1, f32[1280]{0:T(1024)} %ln_bias_ref.1, ...), custom_call_target="tpu_custom_call" | custom-call | flops 157286400 | bytes 6291456 | tf_op jit(solution)/shard_map/pallas_call | solution.py:130
  41.6 3.4 %all-to-all-start.1 = ((bf16[8,32,640]{2,1,0:T(8,128)(2,1)}), bf16[8,32,640]{2,1,0:T(8,128)(2,1)S(1)}, u32[]{:S(2)}, u32[]{:S(2)}) async-start(bf16[8,32,640]{2,1,0:T(8,128)(2,1)} %get-tuple-element.8), calls=%async_computation.1 | async-start | bytes 655360 | tf_op jit(solution)/shard_map/queries/all_to_all | solution.py:348
  45.0 0.1 collective-permute-start.6
  45.1 0.0 collective-permute-done.5.refs_3_
  45.2 0.5 collective-permute-start.9
  45.7 0.0 collective-permute-done.4.refs_2_
  45.7 0.1 collective-permute-start.8
  45.8 0.0 collective-permute-done.3.refs_1_
  45.8 0.4 collective-permute-start.7
  46.2 3.9 %shard_map.131.fresh_ref = bf16[2,32,640]{2,1,0:T(8,128)(2,1)} custom-call(bf16[32,1280]{1,0:T(8,128)(2,1)} %get-tuple-element.7.x_ref, bf16[1280,640]{1,0:T(8,128)(2,1)} %w_k_hbm.1, bf16[1280,640]{1,0:T(8,128)(2,1)} %w_v_hbm.1), custom_call_target="tpu_custom_call" | custom-call | tf_op jit(solution)/shard_map/pallas_call | solution.py:168
  50.1 0.0 collective-permute-done.9.refs_7_
  50.1 0.0 collective-permute-done.8.refs_6_
  50.2 3.5 %all-to-all-done.1 = bf16[8,32,640]{2,1,0:T(8,128)(2,1)S(1)} async-done(((bf16[8,32,640]{2,1,0:T(8,128)(2,1)}), bf16[8,32,640]{2,1,0:T(8,128)(2,1)S(1)}, u32[]{:S(2)}, u32[]{:S(2)}) %all-to-all-start.1) | async-done | bytes 327712 | tf_op jit(solution)/shard_map/queries/all_to_all | solution.py:348
  53.7 0.7 copy-done.3
  54.4 6.8 %shard_map.132 = bf16[8,32,768]{2,1,0:T(8,128)(2,1)} custom-call(s32[1]{0:T(128)} %bitcast.3.place_ref, bf16[256,640]{1,0:T(8,128)(2,1)} %bitcast.11, bf16[2,32,640]{2,1,0:T(8,128)(2,1)} %shard_map.131.fresh_ref, bf16[4,2,32,640]{3,2,1,0:T(8,128)(2,1)} %copy-done.2, bf16[4,2,32,640]{3,2,1,0:T(8,128)(2,1)} %copy-done.6, bf16[4,2,32,640]{3,2,1,0:T(8,128)(2,1)} %copy-done.5, ...), custom_call_target="tpu_custom_call" | custom-call | flops 671088640 | bytes 4194304 | tf_op jit(solution)/shard_map/pallas_call | solution.py:272
  61.3 11.8 %all_to_all.15.parts_ref = bf16[8,32,768]{2,1,0:T(8,128)(2,1)S(1)} all-to-all(bf16[8,32,768]{2,1,0:T(8,128)(2,1)} %shard_map.132), channel_id=1, replica_groups={{0,2,4,6,32,34,36,38},{1,3,5,7,33,35,37,39},{8,10,12,14,40,42,44,46},{9..., dimensions={0} | all-to-all | bytes 786432 | tf_op jit(solution)/shard_map/partials/all_to_all | solution.py:348
  73.1 0.8 %partials.1 = bf16[32,640]{1,0:T(8,128)(2,1)} custom-call(bf16[8,32,768]{2,1,0:T(8,128)(2,1)S(1)} %all_to_all.15.parts_ref), custom_call_target="tpu_custom_call" | custom-call | tf_op jit(solution)/shard_map/partials/pallas_call | solution.py:309
  (21 shorter events, 0.0 us)
Async XLA Ops:
  0.6 23.1 %collective-permute-start = (bf16[2,32,640]{2,1,0:T(8,128)(2,1)}, bf16[2,32,640]{2,1,0:T(8,128)(2,1)S(1)}, u32[]{:S(2)}, u32[]{:S(2)}) collective-permute-start(bf16[2,32,640]{2,1,0:T(8,128)(2,1)} %param.21), channel_id=1, source_target_pairs={{0,16},{1,17},{2,18},{3,19},{4,20},{5,21},{6,22},{7,23},{8,24},{9,... | collective-permute-start | bytes 245768 | tf_op jit(solution)/shard_map/keys_z/ppermute | solution.py:356
  7.9 15.8 %collective-permute-start.2 = (bf16[2,32,640]{2,1,0:T(8,128)(2,1)}, bf16[2,32,640]{2,1,0:T(8,128)(2,1)S(1)}, u32[]{:S(2)}, u32[]{:S(2)}) collective-permute-start(bf16[2,32,640]{2,1,0:T(8,128)(2,1)} %param.21), channel_id=1, source_target_pairs={{0,24},{1,25},{2,26},{3,27},{4,28},{5,29},{6,30},{7,31},{8,0},{9,1... | collective-permute-start | bytes 245768 | tf_op jit(solution)/shard_map/keys_z/ppermute | solution.py:356
  7.9 15.8 %collective-permute-start.1 = (bf16[2,32,640]{2,1,0:T(8,128)(2,1)}, bf16[2,32,640]{2,1,0:T(8,128)(2,1)S(1)}, u32[]{:S(2)}, u32[]{:S(2)}) collective-permute-start(bf16[2,32,640]{2,1,0:T(8,128)(2,1)} %param.21), channel_id=1, source_target_pairs={{0,8},{1,9},{2,10},{3,11},{4,12},{5,13},{6,14},{7,15},{8,16},{9,17... | collective-permute-start | bytes 245768 | tf_op jit(solution)/shard_map/keys_z/ppermute | solution.py:356
  10.8 0.9 %copy-start = (bf16[32,1280]{1,0:T(8,128)(2,1)S(1)}, bf16[32,1280]{1,0:T(8,128)(2,1)}, u32[]{:S(2)}) copy-start(bf16[32,1280]{1,0:T(8,128)(2,1)} %x_ref.3) | copy-start | bytes 245764
  13.1 22.8 %all-to-all-start = ((f32[256,1,128]{2,1,0:T(1,128)}), f32[256,1,128]{2,1,0:T(1,128)S(1)}, u32[]{:S(2)}, u32[]{:S(2)}) async-start(f32[256,1,128]{2,1,0:T(1,128)} %bitcast.1), calls=%async_computation | async-start | bytes 262144 | tf_op jit(solution)/shard_map/statistics/all_to_all | solution.py:359
  24.7 29.0 %copy-start.2 = (bf16[4,2,32,640]{3,2,1,0:T(8,128)(2,1)}, bf16[4,2,32,640]{3,2,1,0:T(8,128)(2,1)S(1)}, u32[]{:S(2)}) copy-start(bf16[4,2,32,640]{3,2,1,0:T(8,128)(2,1)S(1)} %pad_maximum_fusion.refs_0_) | copy-start | bytes 983044
  24.7 20.5 %collective-permute-start.5 = (bf16[4,2,32,640]{3,2,1,0:T(8,128)(2,1)S(1)}, bf16[4,2,32,640]{3,2,1,0:T(8,128)(2,1)S(1)}, u32[]{:S(2)}, u32[]{:S(2)}) collective-permute-start(bf16[4,2,32,640]{3,2,1,0:T(8,128)(2,1)S(1)} %pad_maximum_fusion.refs_0_), channel_id=1, source_target_pairs={{0,128},{1,129},{2,130},{3,131},{4,132},{5,133},{6,134},{7,135},{8... | collective-permute-start | bytes 983048 | tf_op jit(solution)/shard_map/keys_x/ppermute | solution.py:363
  26.9 18.8 %collective-permute-start.4 = (bf16[4,2,32,640]{3,2,1,0:T(8,128)(2,1)S(1)}, bf16[4,2,32,640]{3,2,1,0:T(8,128)(2,1)S(1)}, u32[]{:S(2)}, u32[]{:S(2)}) collective-permute-start(bf16[4,2,32,640]{3,2,1,0:T(8,128)(2,1)S(1)} %pad_maximum_fusion.refs_0_), channel_id=1, source_target_pairs={{0,192},{1,193},{2,194},{3,195},{4,196},{5,197},{6,198},{7,199},{8... | collective-permute-start | bytes 983048 | tf_op jit(solution)/shard_map/keys_x/ppermute | solution.py:363
  28.3 17.5 %collective-permute-start.3 = (bf16[4,2,32,640]{3,2,1,0:T(8,128)(2,1)S(1)}, bf16[4,2,32,640]{3,2,1,0:T(8,128)(2,1)S(1)}, u32[]{:S(2)}, u32[]{:S(2)}) collective-permute-start(bf16[4,2,32,640]{3,2,1,0:T(8,128)(2,1)S(1)} %pad_maximum_fusion.refs_0_), channel_id=1, source_target_pairs={{0,64},{1,65},{2,66},{3,67},{4,68},{5,69},{6,70},{7,71},{8,72},{9,... | collective-permute-start | bytes 983048 | tf_op jit(solution)/shard_map/keys_x/ppermute | solution.py:363
  35.9 0.6 copy-start.1
  41.6 12.1 %all-to-all-start.1 = ((bf16[8,32,640]{2,1,0:T(8,128)(2,1)}), bf16[8,32,640]{2,1,0:T(8,128)(2,1)S(1)}, u32[]{:S(2)}, u32[]{:S(2)}) async-start(bf16[8,32,640]{2,1,0:T(8,128)(2,1)} %get-tuple-element.8), calls=%async_computation.1 | async-start | bytes 655360 | tf_op jit(solution)/shard_map/queries/all_to_all | solution.py:348
  45.0 5.0 %collective-permute-start.6 = (bf16[4,2,32,640]{3,2,1,0:T(8,128)(2,1)S(1)}, bf16[4,2,32,640]{3,2,1,0:T(8,128)(2,1)S(1)}, u32[]{:S(2)}, u32[]{:S(2)}) collective-permute-start(bf16[4,2,32,640]{3,2,1,0:T(8,128)(2,1)S(1)} %pad_maximum_fusion.refs_0_), channel_id=1, source_target_pairs={{0,1},{1,0},{2,3},{3,2},{4,5},{5,4},{6,7},{7,6},{8,9},{9,8},{10,11... | collective-permute-start | bytes 983048 | tf_op jit(solution)/shard_map/keys_core/ppermute | solution.py:369
  45.2 4.9 %copy-start.4 = (bf16[4,2,32,640]{3,2,1,0:T(8,128)(2,1)}, bf16[4,2,32,640]{3,2,1,0:T(8,128)(2,1)S(1)}, u32[]{:S(2)}) copy-start(bf16[4,2,32,640]{3,2,1,0:T(8,128)(2,1)S(1)} %collective-permute-done.5.refs_3_) | copy-start | bytes 983044
  45.2 4.9 %collective-permute-start.9 = (bf16[4,2,32,640]{3,2,1,0:T(8,128)(2,1)S(1)}, bf16[4,2,32,640]{3,2,1,0:T(8,128)(2,1)S(1)}, u32[]{:S(2)}, u32[]{:S(2)}) collective-permute-start(bf16[4,2,32,640]{3,2,1,0:T(8,128)(2,1)S(1)} %collective-permute-done.5.refs_3_), channel_id=1, source_target_pairs={{0,1},{1,0},{2,3},{3,2},{4,5},{5,4},{6,7},{7,6},{8,9},{9,8},{10,11... | collective-permute-start | bytes 983048 | tf_op jit(solution)/shard_map/keys_core/ppermute | solution.py:369
  45.7 4.4 %copy-start.5 = (bf16[4,2,32,640]{3,2,1,0:T(8,128)(2,1)}, bf16[4,2,32,640]{3,2,1,0:T(8,128)(2,1)S(1)}, u32[]{:S(2)}) copy-start(bf16[4,2,32,640]{3,2,1,0:T(8,128)(2,1)S(1)} %collective-permute-done.4.refs_2_) | copy-start | bytes 983044
  45.7 4.5 %collective-permute-start.8 = (bf16[4,2,32,640]{3,2,1,0:T(8,128)(2,1)S(1)}, bf16[4,2,32,640]{3,2,1,0:T(8,128)(2,1)S(1)}, u32[]{:S(2)}, u32[]{:S(2)}) collective-permute-start(bf16[4,2,32,640]{3,2,1,0:T(8,128)(2,1)S(1)} %collective-permute-done.4.refs_2_), channel_id=1, source_target_pairs={{0,1},{1,0},{2,3},{3,2},{4,5},{5,4},{6,7},{7,6},{8,9},{9,8},{10,11... | collective-permute-start | bytes 983048 | tf_op jit(solution)/shard_map/keys_core/ppermute | solution.py:369
  45.8 4.3 %copy-start.6 = (bf16[4,2,32,640]{3,2,1,0:T(8,128)(2,1)}, bf16[4,2,32,640]{3,2,1,0:T(8,128)(2,1)S(1)}, u32[]{:S(2)}) copy-start(bf16[4,2,32,640]{3,2,1,0:T(8,128)(2,1)S(1)} %collective-permute-done.3.refs_1_) | copy-start | bytes 983044
  45.8 4.4 %collective-permute-start.7 = (bf16[4,2,32,640]{3,2,1,0:T(8,128)(2,1)S(1)}, bf16[4,2,32,640]{3,2,1,0:T(8,128)(2,1)S(1)}, u32[]{:S(2)}, u32[]{:S(2)}) collective-permute-start(bf16[4,2,32,640]{3,2,1,0:T(8,128)(2,1)S(1)} %collective-permute-done.3.refs_1_), channel_id=1, source_target_pairs={{0,1},{1,0},{2,3},{3,2},{4,5},{5,4},{6,7},{7,6},{8,9},{9,8},{10,11... | collective-permute-start | bytes 983048 | tf_op jit(solution)/shard_map/keys_core/ppermute | solution.py:369
  50.1 3.6 %copy-start.7 = (bf16[4,2,32,640]{3,2,1,0:T(8,128)(2,1)}, bf16[4,2,32,640]{3,2,1,0:T(8,128)(2,1)S(1)}, u32[]{:S(2)}) copy-start(bf16[4,2,32,640]{3,2,1,0:T(8,128)(2,1)S(1)} %collective-permute-done.6.refs_4_) | copy-start | bytes 983044
  50.1 3.6 %copy-start.8 = (bf16[4,2,32,640]{3,2,1,0:T(8,128)(2,1)}, bf16[4,2,32,640]{3,2,1,0:T(8,128)(2,1)S(1)}, u32[]{:S(2)}) copy-start(bf16[4,2,32,640]{3,2,1,0:T(8,128)(2,1)S(1)} %collective-permute-done.9.refs_7_) | copy-start | bytes 983044
  50.1 3.6 %copy-start.9 = (bf16[4,2,32,640]{3,2,1,0:T(8,128)(2,1)}, bf16[4,2,32,640]{3,2,1,0:T(8,128)(2,1)S(1)}, u32[]{:S(2)}) copy-start(bf16[4,2,32,640]{3,2,1,0:T(8,128)(2,1)S(1)} %collective-permute-done.8.refs_6_) | copy-start | bytes 983044
  50.1 3.6 %copy-start.10 = (bf16[4,2,32,640]{3,2,1,0:T(8,128)(2,1)}, bf16[4,2,32,640]{3,2,1,0:T(8,128)(2,1)S(1)}, u32[]{:S(2)}) copy-start(bf16[4,2,32,640]{3,2,1,0:T(8,128)(2,1)S(1)} %collective-permute-done.7.refs_5_) | copy-start | bytes 983044
  53.7 0.7 copy-start.3

commit v4 on v3

--- a/solution.py
+++ b/solution.py
@@ -1,3 +1,4 @@
+import functools
 import math
 import jax
 import jax.numpy as jnp
@@ -14,6 +15,7 @@
 SMEM = pl.BlockSpec(memory_space=pltpu.SMEM)
 HBM = pl.BlockSpec(memory_space=pltpu.HBM)
 NT = (((1,), (1,)), ((), ()))
+ATT_LIMIT = 16 * 1024 * 1024
 
 
 def member_of(chans):
@@ -52,144 +54,63 @@
     square = to_groups(jnp.sum(off * off, axis=0, keepdims=True), member)
     lane = lax.broadcasted_iota(jnp.int32, (1, 128), 1)
     both = jnp.where(lane < GROUPS, mean, pltpu.roll(square, GROUPS, axis=1))
-    out_ref[...] = jnp.broadcast_to(both, out_ref.shape)
+    out_ref[...] = jnp.broadcast_to(both[:, : 2 * GROUPS], out_ref.shape)
 
 
 def statistics(x, peers):
     return pl.pallas_call(
         statistics_kernel,
-        out_shape=jax.ShapeDtypeStruct((peers, 128), jnp.float32),
+        out_shape=jax.ShapeDtypeStruct((peers, 2 * GROUPS), jnp.float32),
         in_specs=[VMEM],
         out_specs=VMEM,
         compiler_params=pltpu.CompilerParams(vmem_limit_bytes=8 * 1024 * 1024),
     )(x)
 
 
-def project_kernel(stats_ref, gain_ref, bias_ref, b_in_ref, ln_gain_ref, ln_bias_ref, x_ref, *refs):
-    w_in_hbm, w_q_hbm, stream_ref, lnorm_ref, query_ref, w_in_ref, w_q_ref, sems = refs
-    rows, chans = x_ref.shape
-    parts = w_in_ref.shape[0] // 320
-    copies = [
-        pltpu.make_async_copy(
-            w_in_hbm.at[pl.ds(i * 320, 320)], w_in_ref.at[pl.ds(i * 320, 320)], sems.at[i]
-        )
-        for i in range(parts)
-    ] + [pltpu.make_async_copy(w_q_hbm, w_q_ref, sems.at[parts])]
-    for copy in copies:
-        copy.start()
-
+def coefficients_kernel(entries, stats_ref, out_ref):
     peers = stats_ref.shape[0]
-    entries = rows * (chans // GROUPS)
-    lane = lax.broadcasted_iota(jnp.int32, (1, 128), 1)
-    stats = stats_ref[...]
-    sums = jnp.sum(stats, axis=0, keepdims=True)
-    mean = jnp.where(lane < GROUPS, sums * (1.0 / peers), 0.0)
-    apart = jnp.where(lane < GROUPS, stats - mean, 0.0)
-    square = pltpu.roll(sums, 128 - GROUPS, axis=1) + entries * jnp.sum(
-        apart * apart, axis=0, keepdims=True
-    )
-    square = jnp.where(lane < GROUPS, square, 0.0)
-    member = member_of(chans)
+    means = stats_ref[:, :GROUPS]
+    mean = jnp.sum(means, axis=0, keepdims=True) * (1.0 / peers)
+    apart = means - mean
+    square = jnp.sum(stats_ref[:, GROUPS:] + entries * (apart * apart), axis=0, keepdims=True)
     scale = lax.rsqrt(square * (1.0 / (entries * peers)) + 1e-06)
+    rest = jnp.zeros((1, 128 - GROUPS), jnp.float32)
+    mean = jnp.concatenate([mean, rest], axis=1)
+    scale = jnp.concatenate([scale, rest], axis=1)
     both = lax.dot_general(
         jnp.concatenate([pieces(mean), pieces(scale)], axis=0),
-        member,
+        member_of(out_ref.shape[1]),
         NT,
         preferred_element_type=jnp.float32,
     )
-    mean = both[0:1] + both[1:2] + both[2:3]
-    scale = both[3:4] + both[4:5] + both[5:6]
-
-    def row(ref):
-        return ref[...].reshape(1, chans)
-
-    x = x_ref[...].astype(jnp.float32)
-    normed = ((x - mean) * scale * row(gain_ref) + row(bias_ref)).astype(jnp.bfloat16)
-    stream = row(b_in_ref)
-    for i in range(parts):
-        copies[i].wait()
-    stream = stream + jnp.dot(normed, w_in_ref[...], preferred_element_type=jnp.float32)
-    stream = stream.astype(jnp.bfloat16)
-    stream_ref[...] = stream
-    wide = stream.astype(jnp.float32)
-    token_mean = jnp.mean(wide, axis=-1, keepdims=True)
-    token_dev = wide - token_mean
-    token_var = jnp.mean(token_dev * token_dev, axis=-1, keepdims=True)
-    lnorm = token_dev * lax.rsqrt(token_var + 1e-05) * row(ln_gain_ref) + row(ln_bias_ref)
-    lnorm = lnorm.astype(jnp.bfloat16)
-    lnorm_ref[...] = lnorm
-    copies[parts].wait()
-    query = jnp.dot(lnorm, w_q_ref[...], preferred_element_type=jnp.float32)
-    query = query.astype(jnp.bfloat16) * jnp.bfloat16(1.0 / math.sqrt(HEAD_DIM))
-    query_ref[...] = jnp.broadcast_to(query[None], query_ref.shape)
-
-
-def project(stats, vectors, x, w_in, w_query, copies):
-    patch, chans = x.shape
-    bf16 = jnp.bfloat16
+    out_ref[...] = jnp.concatenate(
+        [both[at : at + 1] + both[at + 1 : at + 2] + both[at + 2 : at + 3] for at in (0, 3)], axis=0
+    )
+
+
+def coefficients(stats, entries, chans):
     return pl.pallas_call(
-        project_kernel,
-        out_shape=(
-            jax.ShapeDtypeStruct((patch, chans), bf16),
-            jax.ShapeDtypeStruct((patch, chans), bf16),
-            jax.ShapeDtypeStruct((copies, patch, INNER), bf16),
-        ),
-        in_specs=[VMEM] * 7 + [HBM] * 2,
-        out_specs=(VMEM, VMEM, VMEM),
-        scratch_shapes=[
-            pltpu.VMEM(w_in.shape, bf16),
-            pltpu.VMEM(w_query.shape, bf16),
-            pltpu.SemaphoreType.DMA((5,)),
-        ],
-        compiler_params=pltpu.CompilerParams(vmem_limit_bytes=56 * 1024 * 1024),
-        cost_estimate=pl.CostEstimate(
-            flops=patch * 2 * chans * (chans + INNER),
-            bytes_accessed=6 * 1024 * 1024,
-            transcendentals=patch,
-        ),
-    )(stats, *vectors, x, w_in, w_query)
-
-
-def fresh_kernel(x_ref, w_k_hbm, w_v_hbm, out_ref, w_ref, sems):
+        functools.partial(coefficients_kernel, entries),
+        out_shape=jax.ShapeDtypeStruct((2, chans), jnp.float32),
+        in_specs=[VMEM],
+        out_specs=VMEM,
+        compiler_params=pltpu.CompilerParams(vmem_limit_bytes=8 * 1024 * 1024),
+    )(stats)
+
+
+def attend_kernel(place_ref, q_ref, x_ref, w_k_hbm, w_v_hbm, *refs):
+    sources, refs = refs[:-9], refs[-9:]
+    out_ref, fresh_ref, w_ref, kv_ref, p_ref, more_ref, numer_ref, total_ref, sems = refs
     copies = [
-        pltpu.make_async_copy(source, w_ref.at[i], sems.at[i])
-        for i, source in enumerate((w_k_hbm, w_v_hbm))
+        pltpu.make_async_copy(source, target, sems.at[i])
+        for i, (source, target) in enumerate(
+            [(w_k_hbm, w_ref.at[0]), (w_v_hbm, w_ref.at[1])]
+            + [(source, kv_ref.at[i]) for i, source in enumerate(sources)]
+        )
     ]
     for copy in copies:
         copy.start()
-    for i, copy in enumerate(copies):
-        copy.wait()
-        out_ref[i] = jnp.dot(x_ref[...], w_ref[i], preferred_element_type=jnp.float32).astype(
-            jnp.bfloat16
-        )
-
-
-def fresh_keys(x, w_key, w_value):
-    return pl.pallas_call(
-        fresh_kernel,
-        out_shape=jax.ShapeDtypeStruct((2, x.shape[0], INNER), jnp.bfloat16),
-        in_specs=[VMEM, HBM, HBM],
-        out_specs=VMEM,
-        scratch_shapes=[
-            pltpu.VMEM((2,) + w_key.shape, jnp.bfloat16),
-            pltpu.SemaphoreType.DMA((2,)),
-        ],
-        compiler_params=pltpu.CompilerParams(vmem_limit_bytes=56 * 1024 * 1024),
-    )(x, w_key, w_value)
-
-
-def attend_kernel(place_ref, q_hbm, fresh_ref, *refs):
-    sources, refs = refs[:-9], refs[-9:]
-    out_ref, kv_ref, p_ref, q_ref, more_ref, numer_ref, total_ref, sems, q_sem = refs
-    q_copy = pltpu.make_async_copy(q_hbm, q_ref, q_sem)
-    q_copy.start()
-    copies = [
-        pltpu.make_async_copy(source, kv_ref.at[i], sems.at[i])
-        for i, source in enumerate(sources)
-    ]
-    for copy in copies:
-        copy.start()
-    patch = fresh_ref.shape[1]
+    patch = x_ref.shape[0]
     rows = q_ref.shape[0]
     count = rows // patch
     place = place_ref[0]
@@ -205,7 +126,11 @@
     def with_ones(value):
         return jnp.concatenate([value, jnp.ones((value.shape[0], 128), jnp.bfloat16)], axis=1)
 
-    q_copy.wait()
+    for i in range(2):
+        copies[i].wait()
+        fresh_ref[i] = jnp.dot(x_ref[...], w_ref[i], preferred_element_type=jnp.float32).astype(
+            jnp.bfloat16
+        )
     for pair, lanes in enumerate(pairs):
         score = lax.dot_general(
             two_heads(q_ref[pl.ds(own, patch), lanes]),
@@ -218,7 +143,7 @@
             with_ones(fresh_ref[1, :, lanes]),
             preferred_element_type=jnp.float32,
         )
-    for copy in copies:
+    for copy in copies[2:]:
         copy.wait()
 
     keys = p_ref.shape[1]
@@ -266,31 +191,33 @@
     out_ref[place, :, INNER:] = coded(total_ref[pl.ds(own, patch), :] + own_totals)
 
 
-def attend(place, query, fresh, key_parts):
-    rows, patch = query.shape[0], fresh.shape[1]
+def attend(place, query, x, w_key, w_value, key_parts):
+    rows, patch = query.shape[0], x.shape[0]
     keys = sum(p.shape[0] for p in key_parts) * patch
     return pl.pallas_call(
         attend_kernel,
-        out_shape=jax.ShapeDtypeStruct((rows // patch, patch, INNER + 128), jnp.bfloat16),
-        in_specs=[SMEM, HBM, VMEM] + [HBM] * len(key_parts),
-        out_specs=VMEM,
+        out_shape=(
+            jax.ShapeDtypeStruct((rows // patch, patch, INNER + 128), jnp.bfloat16),
+            jax.ShapeDtypeStruct((2, patch, INNER), jnp.bfloat16),
+        ),
+        in_specs=[SMEM, VMEM, VMEM] + [HBM] * (2 + len(key_parts)),
+        out_specs=(VMEM, VMEM),
         scratch_shapes=[
+            pltpu.VMEM((2,) + w_key.shape, jnp.bfloat16),
             pltpu.VMEM((len(key_parts),) + key_parts[0].shape, jnp.bfloat16),
             pltpu.VMEM((2 * rows, keys), jnp.bfloat16),
-            pltpu.VMEM(query.shape, jnp.bfloat16),
             pltpu.VMEM((HEADS // 2, 2 * patch, 256), jnp.float32),
             pltpu.VMEM((rows, 128), jnp.float32),
             pltpu.VMEM((rows, 128), jnp.float32),
-            pltpu.SemaphoreType.DMA((len(key_parts),)),
-            pltpu.SemaphoreType.DMA(()),
+            pltpu.SemaphoreType.DMA((2 + len(key_parts),)),
         ],
-        compiler_params=pltpu.CompilerParams(vmem_limit_bytes=56 * 1024 * 1024),
+        compiler_params=pltpu.CompilerParams(vmem_limit_bytes=ATT_LIMIT),
         cost_estimate=pl.CostEstimate(
             flops=rows * 4 * keys * INNER,
-            bytes_accessed=4 * 1024 * 1024,
+            bytes_accessed=8 * 1024 * 1024,
             transcendentals=rows * keys * HEADS,
         ),
-    )(place, query, fresh, *key_parts)
+    )(place, query, x, w_key, w_value, *key_parts)
 
 
 def combine_kernel(parts_ref, out_ref):
@@ -356,21 +283,31 @@
         along_z = [lax.ppermute(stale_kv, AXES, moved(dz=d)) for d in (4, 2, 6)]
     with jax.named_scope("statistics"):
         here = statistics(latent, DEVICES)[:, None, :]
-        stats = lax.all_to_all(here, AXES, 0, 0).reshape(DEVICES, 128)
-    vectors = [gn_gain, gn_bias, b_in, ln_gain, ln_bias]
+        stats = lax.all_to_all(here, AXES, 0, 0).reshape(DEVICES, 2 * GROUPS)
     with jax.named_scope("keys_x"):
         line = jnp.stack([stale_kv] + along_z)
         parts = [line] + [lax.ppermute(line, AXES, moved(dx=d)) for d in (1, 3, 2)]
-    stream, lnorm, query = project(stats, vectors, latent, w_in, w_query, shared)
+    rows, chans = latent.shape
+    group = coefficients(stats, rows * (chans // GROUPS), chans)
+    scaled = (latent.astype(jnp.float32) - group[0:1]) * group[1:2]
+    normed = (scaled * gn_gain + gn_bias).astype(jnp.bfloat16)
+    stream = (jnp.dot(normed, w_in, preferred_element_type=jnp.float32) + b_in).astype(jnp.bfloat16)
+    wide = stream.astype(jnp.float32)
+    token_mean = jnp.mean(wide, axis=-1, keepdims=True)
+    token_dev = wide - token_mean
+    token_var = jnp.mean(token_dev * token_dev, axis=-1, keepdims=True)
+    lnorm = (token_dev * lax.rsqrt(token_var + 1e-05) * ln_gain + ln_bias).astype(jnp.bfloat16)
+    query = jnp.dot(lnorm, w_query, preferred_element_type=jnp.float32).astype(jnp.bfloat16)
+    query = query * jnp.bfloat16(1.0 / math.sqrt(HEAD_DIM))
+    query = jnp.broadcast_to(query[None], (shared, rows, INNER))
     with jax.named_scope("queries"):
         query = exchange(query, SHARE).reshape(shared * latent.shape[0], INNER)
-    fresh_kv = fresh_keys(lnorm, w_key, w_value)
     with jax.named_scope("keys_core"):
         parts = parts + [lax.ppermute(part, AXES, moved(dcore=1)) for part in parts]
     row, col = lax.axis_index("row"), lax.axis_index("col")
     place = ((row & 1) << 2) | (((col >> 2) & 1) << 1) | ((col >> 1) & 1)
     place = place.reshape(1).astype(jnp.int32)
-    partial = attend(place, query, fresh_kv, parts)
+    partial, fresh_kv = attend(place, query, lnorm, w_key, w_value, parts)
     with jax.named_scope("partials"):
         attended = combine(exchange(partial, SHARE))
     return (stream, fresh_kv, attended)

time: 74.5 us -> 73.6 us (0.988)
  Pallas kernels: 17.9 us -> 8.74 us
  waiting for transfers between devices: 10.6 us -> 14 us
  local copies, waits for them, and re-layouts: 2.27 us -> 4.59 us
  matrix products: 0 us -> 2.18 us
  blocking collectives: 11.8 us -> 10.7 us
  other arithmetic: 0.94 us -> 2.04 us
    pallas_call x3 -> x2, Pallas kernels: 15.8 us -> 6.56 us  [the longest x1 6.15 us: attend(): pl.pallas_call(attend_kernel, out_shape=(jax.ShapeDtypeStruct((rows // pa...]
    all_to_all x1, waiting for transfers between devices: 3.52 us -> 6.68 us  [exchange(): return lax.all_to_all(value, AXES, 0, 0, axis_index_groups=groups_of(mask))]
    dot_general x0 -> x2, matrix products: none -> 2.18 us  [the longest x1 1.79 us: local(): jnp.dot(normed, w_in, preferred_element_type=jnp.float32) + b_in]
    unnamed x22 -> x16, local copies, waits for them, and re-layouts: 2.27 us -> 3.78 us
    all_to_all x1, blocking collectives: 11.8 us -> 10.7 us  [exchange(): return lax.all_to_all(value, AXES, 0, 0, axis_index_groups=groups_of(mask))]
    another operation x1, other arithmetic: 0.94 us -> 1.73 us  [local(): line = jnp.stack([stale_kv] + along_z)]
    broadcast_in_dim x0 -> x1, local copies, waits for them, and re-layouts: none -> 0.77 us  [local(): query = jnp.broadcast_to(query[None], (shared, rows, INNER))]
  transfers between devices with their start and end apart: 12 -> 12, of which waited for: 2 -> 4; matrix products, arithmetic and copies ran while one was open for 1% -> 7% of each run, Pallas kernels for 14% -> 2%
where the time goes in v4:
time: 73.6 us; the launch traced here: 73.1 us
  starting transfers between devices  30.1 us (41%)
  waiting for transfers between devices  14 us (19%)
  blocking collectives  10.7 us (15%)
  Pallas kernels  8.74 us (12%)
  local copies, waits for them, and re-layouts  4.59 us (6%)
  matrix products  2.18 us (3%)
  other arithmetic  2.04 us (3%)
  between operations  0.83 us (1%)
    all_to_all x1, blocking collectives, exchange(): return lax.all_to_all(value, AXES, 0, 0, axis_index_groups=groups_of(mask))  10.7 us
    all_to_all x1, starting transfers between devices, local(): stats = lax.all_to_all(here, AXES, 0, 0).reshape(DEVICES, 2 * GROUPS)  10.6 us
    ppermute x3, starting transfers between devices, local(): along_z = [lax.ppermute(stale_kv, AXES, moved(dz=d)) for d in (4, 2, 6)]  10.2 us
    all_to_all x1, waiting for transfers between devices, exchange(): return lax.all_to_all(value, AXES, 0, 0, axis_index_groups=groups_of(mask))  6.68 us
    all_to_all x1, waiting for transfers between devices, local(): stats = lax.all_to_all(here, AXES, 0, 0).reshape(DEVICES, 2 * GROUPS)  6.31 us
    pallas_call x1, Pallas kernels, attend(): pl.pallas_call(attend_kernel, out_shape=(jax.ShapeDtypeStruct((rows // pa...  6.15 us
    ppermute x3, starting transfers between devices, local(): parts = [line] + [lax.ppermute(line, AXES, moved(dx=d)) for d in (1, 3, 2)]  4.1 us
    all_to_all x1, starting transfers between devices, exchange(): return lax.all_to_all(value, AXES, 0, 0, axis_index_groups=groups_of(mask))  4.06 us
  transfers between devices with their start and end apart: 12, of which 4 were waited for; matrix products, arithmetic and copies ran while one was open for 7% of the time, Pallas kernels for 2%

profile of v4, /device:TPU:2, one launch (start us, length us, event | category | flops | bytes accessed | tf_op | source)
XLA Modules:
  0.0 73.1 jit_solution(12321446631364620976)
XLA Ops:
  0.6 0.0 copy-start
  0.6 7.3 %collective-permute-start = (bf16[2,32,640]{2,1,0:T(8,128)(2,1)}, bf16[2,32,640]{2,1,0:T(8,128)(2,1)S(1)}, u32[]{:S(2)}, u32[]{:S(2)}) collective-permute-start(bf16[2,32,640]{2,1,0:T(8,128)(2,1)} %param.21), channel_id=1, source_target_pairs={{0,16},{1,17},{2,18},{3,19},{4,20},{5,21},{6,22},{7,23},{8,24},{9,... | collective-permute-start | bytes 245768 | tf_op jit(solution)/shard_map/keys_z/ppermute | solution.py:283
  7.9 2.9 %collective-permute-start.1 = (bf16[2,32,640]{2,1,0:T(8,128)(2,1)}, bf16[2,32,640]{2,1,0:T(8,128)(2,1)}, u32[]{:S(2)}, u32[]{:S(2)}) collective-permute-start(bf16[2,32,640]{2,1,0:T(8,128)(2,1)} %param.21), channel_id=1, source_target_pairs={{0,8},{1,9},{2,10},{3,11},{4,12},{5,13},{6,14},{7,15},{8,16},{9,17... | collective-permute-start | bytes 245768 | tf_op jit(solution)/shard_map/keys_z/ppermute | solution.py:283
  10.8 0.9 %copy-done.3 = bf16[32,1280]{1,0:T(8,128)(2,1)S(1)} copy-done((bf16[32,1280]{1,0:T(8,128)(2,1)S(1)}, bf16[32,1280]{1,0:T(8,128)(2,1)}, u32[]{:S(2)}) %copy-start.3) | copy-done | bytes 81944
  11.7 1.3 %statistics.1 = f32[256,64]{1,0:T(8,128)} custom-call(bf16[32,1280]{1,0:T(8,128)(2,1)S(1)} %copy-done.3), custom_call_target="tpu_custom_call" | custom-call | tf_op jit(solution)/shard_map/statistics/pallas_call | solution.py:61
  13.1 10.6 %all-to-all-start = ((f32[256,1,64]{2,1,0:T(1,128)}), f32[256,1,64]{2,1,0:T(1,128)S(1)}, u32[]{:S(2)}, u32[]{:S(2)}) async-start(f32[256,1,64]{2,1,0:T(1,128)} %bitcast.1), calls=%async_computation | async-start | bytes 262144 | tf_op jit(solution)/shard_map/statistics/all_to_all | solution.py:286
  23.8 1.7 %pad_maximum_fusion.refs_0_ = bf16[4,2,32,640]{3,2,1,0:T(8,128)(2,1)} fusion(bf16[1,2,32,640]{3,2,1,0:T(8,128)(2,1)} %bitcast.8, bf16[1,2,32,640]{3,2,1,0:T(8,128)(2,1)} %bitcast.7, bf16[1,2,32,640]{3,2,1,0:T(8,128)(2,1)S(1)} %bitcast.15, bf16[1,2,32,640]{3,2,1,0:T(8,128)(2,1)} %bitcast.14), kind=kLoop, calls=%fused_computation.4 | loop fusion | flops 491520 | bytes 655360 | tf_op jit(solution)/shard_map/keys_x/stack | solution.py:288
  25.5 2.1 %collective-permute-start.5 = (bf16[4,2,32,640]{3,2,1,0:T(8,128)(2,1)}, bf16[4,2,32,640]{3,2,1,0:T(8,128)(2,1)}, u32[]{:S(2)}, u32[]{:S(2)}) collective-permute-start(bf16[4,2,32,640]{3,2,1,0:T(8,128)(2,1)} %pad_maximum_fusion.refs_0_), channel_id=1, source_target_pairs={{0,128},{1,129},{2,130},{3,131},{4,132},{5,133},{6,134},{7,135},{8... | collective-permute-start | bytes 983048 | tf_op jit(solution)/shard_map/keys_x/ppermute | solution.py:289
  27.6 1.5 %collective-permute-start.4 = (bf16[4,2,32,640]{3,2,1,0:T(8,128)(2,1)}, bf16[4,2,32,640]{3,2,1,0:T(8,128)(2,1)}, u32[]{:S(2)}, u32[]{:S(2)}) collective-permute-start(bf16[4,2,32,640]{3,2,1,0:T(8,128)(2,1)} %pad_maximum_fusion.refs_0_), channel_id=1, source_target_pairs={{0,192},{1,193},{2,194},{3,195},{4,196},{5,197},{6,198},{7,199},{8... | collective-permute-start | bytes 983048 | tf_op jit(solution)/shard_map/keys_x/ppermute | solution.py:289
  29.0 0.6 collective-permute-start.3
  29.6 6.3 %all-to-all-done = f32[256,1,64]{2,1,0:T(1,128)S(1)} async-done(((f32[256,1,64]{2,1,0:T(1,128)}), f32[256,1,64]{2,1,0:T(1,128)S(1)}, u32[]{:S(2)}, u32[]{:S(2)}) %all-to-all-start) | async-done | bytes 65568 | tf_op jit(solution)/shard_map/statistics/all_to_all | solution.py:286
  35.9 0.4 shard_map.130
  36.4 0.0 copy-start.6
  36.4 1.8 %convert_reduce_fusion = (f32[32]{0:T(128)S(1)}, bf16[32,1280]{1,0:T(8,128)(2,1)S(1)}) fusion(f32[1280]{0:T(1024)} %param.15, bf16[1280,1280]{1,0:T(8,128)(2,1)S(1)} %copy-done, bf16[32,1280]{1,0:T(8,128)(2,1)} %x_ref.1, f32[1280]{0:T(1024)} %param.13, f32[1280]{0:T(1024)} %param.12, f32[1280]{0:T(1024)S(1)} %get-tuple-element.8, f32[1280]{0:T(1024)S(1)} %get-tuple-element.7), kind=kOutput, calls=%fused_computation.6 | convolution fusion | flops 105267168 | bytes 3466368 | tf_op jit(solution)/shard_map/dot_general | solution.py:294
  38.2 0.0 copy-start.5
  38.2 0.2 fusion.4
  38.5 0.1 fusion.7.x_ref
  38.6 0.4 fusion.1
  39.0 0.8 %broadcast_in_dim.5 = bf16[8,32,640]{2,1,0:T(8,128)(2,1)} broadcast(bf16[32,640]{1,0:T(8,128)(2,1)S(1)} %fusion.1), dimensions={1,2} | broadcast | bytes 368640 | tf_op jit(solution)/shard_map/broadcast_in_dim | solution.py:302
  39.7 4.1 %all-to-all-start.1 = ((bf16[8,32,640]{2,1,0:T(8,128)(2,1)}), bf16[8,32,640]{2,1,0:T(8,128)(2,1)}, u32[]{:S(2)}, u32[]{:S(2)}) async-start(bf16[8,32,640]{2,1,0:T(8,128)(2,1)} %broadcast_in_dim.5), calls=%async_computation.1 | async-start | bytes 655360 | tf_op jit(solution)/shard_map/queries/all_to_all | solution.py:275
  43.8 0.1 collective-permute-start.6
  43.9 0.5 collective-permute-start.9
  44.4 0.3 collective-permute-done.4.refs_2_
  44.7 0.0 collective-permute-start.8
  44.7 0.5 collective-permute-start.7
  45.2 0.7 collective-permute-done.6.refs_4_
  45.9 6.7 %all-to-all-done.1 = bf16[8,32,640]{2,1,0:T(8,128)(2,1)} async-done(((bf16[8,32,640]{2,1,0:T(8,128)(2,1)}), bf16[8,32,640]{2,1,0:T(8,128)(2,1)}, u32[]{:S(2)}, u32[]{:S(2)}) %all-to-all-start.1) | async-done | bytes 327712 | tf_op jit(solution)/shard_map/queries/all_to_all | solution.py:275
  52.6 1.4 %copy-done.1 = bf16[1280,640]{1,0:T(8,128)(2,1)S(1)} copy-done((bf16[1280,640]{1,0:T(8,128)(2,1)S(1)}, bf16[1280,640]{1,0:T(8,128)(2,1)}, u32[]{:S(2)}) %copy-start.1) | copy-done | bytes 1638424
  54.0 1.4 %copy-done.2 = bf16[1280,640]{1,0:T(8,128)(2,1)S(1)} copy-done((bf16[1280,640]{1,0:T(8,128)(2,1)S(1)}, bf16[1280,640]{1,0:T(8,128)(2,1)}, u32[]{:S(2)}) %copy-start.2) | copy-done | bytes 1638424
  55.4 6.1 %shard_map.131 = (bf16[8,32,768]{2,1,0:T(8,128)(2,1)S(1)}, bf16[2,32,640]{2,1,0:T(8,128)(2,1)}) custom-call(s32[1]{0:T(128)} %bitcast.3.place_ref, bf16[256,640]{1,0:T(8,128)(2,1)} %bitcast.4.q_ref, bf16[32,1280]{1,0:T(8,128)(2,1)S(1)} %fusion.7.x_ref, bf16[1280,640]{1,0:T(8,128)(2,1)S(1)} %copy-done.1, bf16[1280,640]{1,0:T(8,128)(2,1)S(1)} %copy-done.2, ...), custom_call_target="tpu_custom_call" | custom-call | flops 671088640 | bytes 8388608 | tf_op jit(solution)/shard_map/pallas_call | solution.py:197
  61.6 10.7 %all_to_all.15.parts_ref = bf16[8,32,768]{2,1,0:T(8,128)(2,1)S(1)} all-to-all(bf16[8,32,768]{2,1,0:T(8,128)(2,1)S(1)} %get-tuple-element.6), channel_id=1, replica_groups={{0,2,4,6,32,34,36,38},{1,3,5,7,33,35,37,39},{8,10,12,14,40,42,44,46},{9..., dimensions={0} | all-to-all | bytes 786432 | tf_op jit(solution)/shard_map/partials/all_to_all | solution.py:275
  72.3 0.8 %partials.1 = bf16[32,640]{1,0:T(8,128)(2,1)} custom-call(bf16[8,32,768]{2,1,0:T(8,128)(2,1)S(1)} %all_to_all.15.parts_ref), custom_call_target="tpu_custom_call" | custom-call | tf_op jit(solution)/shard_map/partials/pallas_call | solution.py:236
  (22 shorter events, 0.1 us)
Async XLA Ops:
  0.6 35.7 %copy-start = (bf16[1280,1280]{1,0:T(8,128)(2,1)S(1)}, bf16[1280,1280]{1,0:T(8,128)(2,1)}, u32[]{:S(2)}) copy-start(bf16[1280,1280]{1,0:T(8,128)(2,1)} %param.14) | copy-start | bytes 9830404
  0.6 23.1 %collective-permute-start = (bf16[2,32,640]{2,1,0:T(8,128)(2,1)}, bf16[2,32,640]{2,1,0:T(8,128)(2,1)S(1)}, u32[]{:S(2)}, u32[]{:S(2)}) collective-permute-start(bf16[2,32,640]{2,1,0:T(8,128)(2,1)} %param.21), channel_id=1, source_target_pairs={{0,16},{1,17},{2,18},{3,19},{4,20},{5,21},{6,22},{7,23},{8,24},{9,... | collective-permute-start | bytes 245768 | tf_op jit(solution)/shard_map/keys_z/ppermute | solution.py:283
  7.9 15.8 %collective-permute-start.2 = (bf16[2,32,640]{2,1,0:T(8,128)(2,1)}, bf16[2,32,640]{2,1,0:T(8,128)(2,1)}, u32[]{:S(2)}, u32[]{:S(2)}) collective-permute-start(bf16[2,32,640]{2,1,0:T(8,128)(2,1)} %param.21), channel_id=1, source_target_pairs={{0,24},{1,25},{2,26},{3,27},{4,28},{5,29},{6,30},{7,31},{8,0},{9,1... | collective-permute-start | bytes 245768 | tf_op jit(solution)/shard_map/keys_z/ppermute | solution.py:283
  7.9 15.8 %collective-permute-start.1 = (bf16[2,32,640]{2,1,0:T(8,128)(2,1)}, bf16[2,32,640]{2,1,0:T(8,128)(2,1)}, u32[]{:S(2)}, u32[]{:S(2)}) collective-permute-start(bf16[2,32,640]{2,1,0:T(8,128)(2,1)} %param.21), channel_id=1, source_target_pairs={{0,8},{1,9},{2,10},{3,11},{4,12},{5,13},{6,14},{7,15},{8,16},{9,17... | collective-permute-start | bytes 245768 | tf_op jit(solution)/shard_map/keys_z/ppermute | solution.py:283
  10.8 0.9 %copy-start.3 = (bf16[32,1280]{1,0:T(8,128)(2,1)S(1)}, bf16[32,1280]{1,0:T(8,128)(2,1)}, u32[]{:S(2)}) copy-start(bf16[32,1280]{1,0:T(8,128)(2,1)} %x_ref.1) | copy-start | bytes 245764
  13.1 22.8 %all-to-all-start = ((f32[256,1,64]{2,1,0:T(1,128)}), f32[256,1,64]{2,1,0:T(1,128)S(1)}, u32[]{:S(2)}, u32[]{:S(2)}) async-start(f32[256,1,64]{2,1,0:T(1,128)} %bitcast.1), calls=%async_computation | async-start | bytes 262144 | tf_op jit(solution)/shard_map/statistics/all_to_all | solution.py:286
  25.5 18.4 %collective-permute-start.5 = (bf16[4,2,32,640]{3,2,1,0:T(8,128)(2,1)}, bf16[4,2,32,640]{3,2,1,0:T(8,128)(2,1)}, u32[]{:S(2)}, u32[]{:S(2)}) collective-permute-start(bf16[4,2,32,640]{3,2,1,0:T(8,128)(2,1)} %pad_maximum_fusion.refs_0_), channel_id=1, source_target_pairs={{0,128},{1,129},{2,130},{3,131},{4,132},{5,133},{6,134},{7,135},{8... | collective-permute-start | bytes 983048 | tf_op jit(solution)/shard_map/keys_x/ppermute | solution.py:289
  27.6 17.1 %collective-permute-start.4 = (bf16[4,2,32,640]{3,2,1,0:T(8,128)(2,1)}, bf16[4,2,32,640]{3,2,1,0:T(8,128)(2,1)}, u32[]{:S(2)}, u32[]{:S(2)}) collective-permute-start(bf16[4,2,32,640]{3,2,1,0:T(8,128)(2,1)} %pad_maximum_fusion.refs_0_), channel_id=1, source_target_pairs={{0,192},{1,193},{2,194},{3,195},{4,196},{5,197},{6,198},{7,199},{8... | collective-permute-start | bytes 983048 | tf_op jit(solution)/shard_map/keys_x/ppermute | solution.py:289
  29.0 15.7 %collective-permute-start.3 = (bf16[4,2,32,640]{3,2,1,0:T(8,128)(2,1)}, bf16[4,2,32,640]{3,2,1,0:T(8,128)(2,1)}, u32[]{:S(2)}, u32[]{:S(2)}) collective-permute-start(bf16[4,2,32,640]{3,2,1,0:T(8,128)(2,1)} %pad_maximum_fusion.refs_0_), channel_id=1, source_target_pairs={{0,64},{1,65},{2,66},{3,67},{4,68},{5,69},{6,70},{7,71},{8,72},{9,... | collective-permute-start | bytes 983048 | tf_op jit(solution)/shard_map/keys_x/ppermute | solution.py:289
  36.4 2.1 %copy-start.6 = (f32[1280]{0:T(1024)S(1)}, f32[1280]{0:T(1024)}, u32[]{:S(2)}) copy-start(f32[1280]{0:T(1024)} %param.17) | copy-start | bytes 15364
  36.4 2.1 %copy-start.7 = (f32[1280]{0:T(1024)S(1)}, f32[1280]{0:T(1024)}, u32[]{:S(2)}) copy-start(f32[1280]{0:T(1024)} %param.16) | copy-start | bytes 15364
  36.4 2.2 %copy-start.4 = (bf16[1280,640]{1,0:T(8,128)(2,1)S(1)}, bf16[1280,640]{1,0:T(8,128)(2,1)}, u32[]{:S(2)}) copy-start(bf16[1280,640]{1,0:T(8,128)(2,1)} %param.18) | copy-start | bytes 4915204
  38.2 23.4 %copy-start.5 = (bf16[32,1280]{1,0:T(8,128)(2,1)}, bf16[32,1280]{1,0:T(8,128)(2,1)S(1)}, u32[]{:S(2)}) copy-start(bf16[32,1280]{1,0:T(8,128)(2,1)S(1)} %get-tuple-element.10) | copy-start | bytes 245764
  39.7 12.8 %all-to-all-start.1 = ((bf16[8,32,640]{2,1,0:T(8,128)(2,1)}), bf16[8,32,640]{2,1,0:T(8,128)(2,1)}, u32[]{:S(2)}, u32[]{:S(2)}) async-start(bf16[8,32,640]{2,1,0:T(8,128)(2,1)} %broadcast_in_dim.5), calls=%async_computation.1 | async-start | bytes 655360 | tf_op jit(solution)/shard_map/queries/all_to_all | solution.py:275
  43.8 2.1 %collective-permute-start.6 = (bf16[4,2,32,640]{3,2,1,0:T(8,128)(2,1)}, bf16[4,2,32,640]{3,2,1,0:T(8,128)(2,1)}, u32[]{:S(2)}, u32[]{:S(2)}) collective-permute-start(bf16[4,2,32,640]{3,2,1,0:T(8,128)(2,1)} %pad_maximum_fusion.refs_0_), channel_id=1, source_target_pairs={{0,1},{1,0},{2,3},{3,2},{4,5},{5,4},{6,7},{7,6},{8,9},{9,8},{10,11... | collective-permute-start | bytes 983048 | tf_op jit(solution)/shard_map/keys_core/ppermute | solution.py:306
  43.9 8.6 %collective-permute-start.9 = (bf16[4,2,32,640]{3,2,1,0:T(8,128)(2,1)}, bf16[4,2,32,640]{3,2,1,0:T(8,128)(2,1)}, u32[]{:S(2)}, u32[]{:S(2)}) collective-permute-start(bf16[4,2,32,640]{3,2,1,0:T(8,128)(2,1)} %collective-permute-done.5.refs_3_), channel_id=1, source_target_pairs={{0,1},{1,0},{2,3},{3,2},{4,5},{5,4},{6,7},{7,6},{8,9},{9,8},{10,11... | collective-permute-start | bytes 983048 | tf_op jit(solution)/shard_map/keys_core/ppermute | solution.py:306
  44.7 7.9 %collective-permute-start.8 = (bf16[4,2,32,640]{3,2,1,0:T(8,128)(2,1)}, bf16[4,2,32,640]{3,2,1,0:T(8,128)(2,1)}, u32[]{:S(2)}, u32[]{:S(2)}) collective-permute-start(bf16[4,2,32,640]{3,2,1,0:T(8,128)(2,1)} %collective-permute-done.4.refs_2_), channel_id=1, source_target_pairs={{0,1},{1,0},{2,3},{3,2},{4,5},{5,4},{6,7},{7,6},{8,9},{9,8},{10,11... | collective-permute-start | bytes 983048 | tf_op jit(solution)/shard_map/keys_core/ppermute | solution.py:306
  44.7 7.8 %collective-permute-start.7 = (bf16[4,2,32,640]{3,2,1,0:T(8,128)(2,1)}, bf16[4,2,32,640]{3,2,1,0:T(8,128)(2,1)}, u32[]{:S(2)}, u32[]{:S(2)}) collective-permute-start(bf16[4,2,32,640]{3,2,1,0:T(8,128)(2,1)} %collective-permute-done.3.refs_1_), channel_id=1, source_target_pairs={{0,1},{1,0},{2,3},{3,2},{4,5},{5,4},{6,7},{7,6},{8,9},{9,8},{10,11... | collective-permute-start | bytes 983048 | tf_op jit(solution)/shard_map/keys_core/ppermute | solution.py:306
  52.6 1.4 %copy-start.1 = (bf16[1280,640]{1,0:T(8,128)(2,1)S(1)}, bf16[1280,640]{1,0:T(8,128)(2,1)}, u32[]{:S(2)}) copy-start(bf16[1280,640]{1,0:T(8,128)(2,1)} %w_k_hbm.1) | copy-start | bytes 4915204
  54.0 1.4 %copy-start.2 = (bf16[1280,640]{1,0:T(8,128)(2,1)S(1)}, bf16[1280,640]{1,0:T(8,128)(2,1)}, u32[]{:S(2)}) copy-start(bf16[1280,640]{1,0:T(8,128)(2,1)} %w_v_hbm.1) | copy-start | bytes 4915204

commit v5 on v4

--- a/solution.py
+++ b/solution.py
@@ -98,19 +98,16 @@
     )(stats)
 
 
-def attend_kernel(place_ref, q_ref, x_ref, w_k_hbm, w_v_hbm, *refs):
-    sources, refs = refs[:-9], refs[-9:]
-    out_ref, fresh_ref, w_ref, kv_ref, p_ref, more_ref, numer_ref, total_ref, sems = refs
+def attend_kernel(place_ref, q_ref, fresh_ref, *refs):
+    sources, refs = refs[:-7], refs[-7:]
+    out_ref, kv_ref, p_ref, more_ref, numer_ref, total_ref, sems = refs
     copies = [
-        pltpu.make_async_copy(source, target, sems.at[i])
-        for i, (source, target) in enumerate(
-            [(w_k_hbm, w_ref.at[0]), (w_v_hbm, w_ref.at[1])]
-            + [(source, kv_ref.at[i]) for i, source in enumerate(sources)]
-        )
+        pltpu.make_async_copy(source, kv_ref.at[i], sems.at[i])
+        for i, source in enumerate(sources)
     ]
     for copy in copies:
         copy.start()
-    patch = x_ref.shape[0]
+    patch = fresh_ref.shape[1]
     rows = q_ref.shape[0]
     count = rows // patch
     place = place_ref[0]
@@ -126,11 +123,6 @@
     def with_ones(value):
         return jnp.concatenate([value, jnp.ones((value.shape[0], 128), jnp.bfloat16)], axis=1)
 
-    for i in range(2):
-        copies[i].wait()
-        fresh_ref[i] = jnp.dot(x_ref[...], w_ref[i], preferred_element_type=jnp.float32).astype(
-            jnp.bfloat16
-        )
     for pair, lanes in enumerate(pairs):
         score = lax.dot_general(
             two_heads(q_ref[pl.ds(own, patch), lanes]),
@@ -143,7 +135,7 @@
             with_ones(fresh_ref[1, :, lanes]),
             preferred_element_type=jnp.float32,
         )
-    for copy in copies[2:]:
+    for copy in copies:
         copy.wait()
 
     keys = p_ref.shape[1]
@@ -191,33 +183,29 @@
     out_ref[place, :, INNER:] = coded(total_ref[pl.ds(own, patch), :] + own_totals)
 
 
-def attend(place, query, x, w_key, w_value, key_parts):
-    rows, patch = query.shape[0], x.shape[0]
+def attend(place, query, fresh, key_parts):
+    rows, patch = query.shape[0], fresh.shape[1]
     keys = sum(p.shape[0] for p in key_parts) * patch
     return pl.pallas_call(
         attend_kernel,
-        out_shape=(
-            jax.ShapeDtypeStruct((rows // patch, patch, INNER + 128), jnp.bfloat16),
-            jax.ShapeDtypeStruct((2, patch, INNER), jnp.bfloat16),
-        ),
-        in_specs=[SMEM, VMEM, VMEM] + [HBM] * (2 + len(key_parts)),
-        out_specs=(VMEM, VMEM),
+        out_shape=jax.ShapeDtypeStruct((rows // patch, patch, INNER + 128), jnp.bfloat16),
+        in_specs=[SMEM, VMEM, VMEM] + [HBM] * len(key_parts),
+        out_specs=VMEM,
         scratch_shapes=[
-            pltpu.VMEM((2,) + w_key.shape, jnp.bfloat16),
             pltpu.VMEM((len(key_parts),) + key_parts[0].shape, jnp.bfloat16),
             pltpu.VMEM((2 * rows, keys), jnp.bfloat16),
             pltpu.VMEM((HEADS // 2, 2 * patch, 256), jnp.float32),
             pltpu.VMEM((rows, 128), jnp.float32),
             pltpu.VMEM((rows, 128), jnp.float32),
-            pltpu.SemaphoreType.DMA((2 + len(key_parts),)),
+            pltpu.SemaphoreType.DMA((len(key_parts),)),
         ],
         compiler_params=pltpu.CompilerParams(vmem_limit_bytes=ATT_LIMIT),
         cost_estimate=pl.CostEstimate(
             flops=rows * 4 * keys * INNER,
-            bytes_accessed=8 * 1024 * 1024,
+            bytes_accessed=4 * 1024 * 1024,
             transcendentals=rows * keys * HEADS,
         ),
-    )(place, query, x, w_key, w_value, *key_parts)
+    )(place, query, fresh, *key_parts)
 
 
 def combine_kernel(parts_ref, out_ref):
@@ -307,7 +295,13 @@
     row, col = lax.axis_index("row"), lax.axis_index("col")
     place = ((row & 1) << 2) | (((col >> 2) & 1) << 1) | ((col >> 1) & 1)
     place = place.reshape(1).astype(jnp.int32)
-    partial, fresh_kv = attend(place, query, lnorm, w_key, w_value, parts)
+    fresh_kv = jnp.stack(
+        [
+            jnp.dot(lnorm, w, preferred_element_type=jnp.float32).astype(jnp.bfloat16)
+            for w in (w_key, w_value)
+        ]
+    )
+    partial = attend(place, query, fresh_kv, parts)
     with jax.named_scope("partials"):
         attended = combine(exchange(partial, SHARE))
     return (stream, fresh_kv, attended)

time: 73.6 us -> 71.2 us (0.967)
  waiting for transfers between devices: 14 us -> 10.8 us
  matrix products: 2.18 us -> 4.52 us
  local copies, waits for them, and re-layouts: 4.59 us -> 3.43 us
    all_to_all x1, waiting for transfers between devices: 6.68 us -> 4.16 us  [exchange(): return lax.all_to_all(value, AXES, 0, 0, axis_index_groups=groups_of(mask))]
    dot_general x0 -> x2, matrix products: none -> 2.3 us  [local(): jnp.dot(lnorm, w, preferred_element_type=jnp.float32).astype(jnp.bfloat16)]
    unnamed x16 -> x20, local copies, waits for them, and re-layouts: 3.78 us -> 2.62 us
  transfers between devices with their start and end apart: 12 -> 12, of which waited for: 4 -> 3; matrix products, arithmetic and copies ran while one was open for 7% -> 10% of each run, Pallas kernels for 2% -> 3%
where the time goes in v5:
time: 71.2 us; the launch traced here: 70.7 us
  starting transfers between devices  30.1 us (42%)
  waiting for transfers between devices  10.8 us (15%)
  blocking collectives  10.7 us (15%)
  Pallas kernels  8.31 us (12%)
  matrix products  4.52 us (6%)
  local copies, waits for them, and re-layouts  3.43 us (5%)
  other arithmetic  1.96 us (3%)
  between operations  0.9 us (1%)
    all_to_all x1, blocking collectives, exchange(): return lax.all_to_all(value, AXES, 0, 0, axis_index_groups=groups_of(mask))  10.7 us
    all_to_all x1, starting transfers between devices, local(): stats = lax.all_to_all(here, AXES, 0, 0).reshape(DEVICES, 2 * GROUPS)  10.6 us
    ppermute x3, starting transfers between devices, local(): along_z = [lax.ppermute(stale_kv, AXES, moved(dz=d)) for d in (4, 2, 6)]  10.2 us
    all_to_all x1, waiting for transfers between devices, local(): stats = lax.all_to_all(here, AXES, 0, 0).reshape(DEVICES, 2 * GROUPS)  6.33 us
    pallas_call x1, Pallas kernels, attend(): pl.pallas_call(attend_kernel, out_shape=jax.ShapeDtypeStruct((rows // pat...  5.7 us
    all_to_all x1, waiting for transfers between devices, exchange(): return lax.all_to_all(value, AXES, 0, 0, axis_index_groups=groups_of(mask))  4.16 us
    ppermute x3, starting transfers between devices, local(): parts = [line] + [lax.ppermute(line, AXES, moved(dx=d)) for d in (1, 3, 2)]  4.1 us
    all_to_all x1, starting transfers between devices, exchange(): return lax.all_to_all(value, AXES, 0, 0, axis_index_groups=groups_of(mask))  4.07 us
  transfers between devices with their start and end apart: 12, of which 3 were waited for; matrix products, arithmetic and copies ran while one was open for 10% of the time, Pallas kernels for 3%

profile of v5, /device:TPU:2, one launch (start us, length us, event | category | flops | bytes accessed | tf_op | source)
XLA Modules:
  0.0 70.7 jit_solution(7709210212682442463)
XLA Ops:
  0.6 0.0 copy-start
  0.6 7.3 %collective-permute-start = (bf16[2,32,640]{2,1,0:T(8,128)(2,1)}, bf16[2,32,640]{2,1,0:T(8,128)(2,1)S(1)}, u32[]{:S(2)}, u32[]{:S(2)}) collective-permute-start(bf16[2,32,640]{2,1,0:T(8,128)(2,1)} %param.21), channel_id=1, source_target_pairs={{0,16},{1,17},{2,18},{3,19},{4,20},{5,21},{6,22},{7,23},{8,24},{9,... | collective-permute-start | bytes 245768 | tf_op jit(solution)/shard_map/keys_z/ppermute | solution.py:271
  7.9 2.9 %collective-permute-start.1 = (bf16[2,32,640]{2,1,0:T(8,128)(2,1)}, bf16[2,32,640]{2,1,0:T(8,128)(2,1)}, u32[]{:S(2)}, u32[]{:S(2)}) collective-permute-start(bf16[2,32,640]{2,1,0:T(8,128)(2,1)} %param.21), channel_id=1, source_target_pairs={{0,8},{1,9},{2,10},{3,11},{4,12},{5,13},{6,14},{7,15},{8,16},{9,17... | collective-permute-start | bytes 245768 | tf_op jit(solution)/shard_map/keys_z/ppermute | solution.py:271
  10.8 0.9 %copy-done.1 = bf16[32,1280]{1,0:T(8,128)(2,1)S(1)} copy-done((bf16[32,1280]{1,0:T(8,128)(2,1)S(1)}, bf16[32,1280]{1,0:T(8,128)(2,1)}, u32[]{:S(2)}) %copy-start.1) | copy-done | bytes 81944
  11.7 1.4 %statistics.1 = f32[256,64]{1,0:T(8,128)} custom-call(bf16[32,1280]{1,0:T(8,128)(2,1)S(1)} %copy-done.1), custom_call_target="tpu_custom_call" | custom-call | tf_op jit(solution)/shard_map/statistics/pallas_call | solution.py:61
  13.1 10.6 %all-to-all-start = ((f32[256,1,64]{2,1,0:T(1,128)}), f32[256,1,64]{2,1,0:T(1,128)S(1)}, u32[]{:S(2)}, u32[]{:S(2)}) async-start(f32[256,1,64]{2,1,0:T(1,128)} %bitcast.1), calls=%async_computation | async-start | bytes 262144 | tf_op jit(solution)/shard_map/statistics/all_to_all | solution.py:274
  23.8 1.7 %pad_maximum_fusion.refs_0_ = bf16[4,2,32,640]{3,2,1,0:T(8,128)(2,1)} fusion(bf16[1,2,32,640]{3,2,1,0:T(8,128)(2,1)} %bitcast.10, bf16[1,2,32,640]{3,2,1,0:T(8,128)(2,1)} %bitcast.9, bf16[1,2,32,640]{3,2,1,0:T(8,128)(2,1)S(1)} %bitcast.20, bf16[1,2,32,640]{3,2,1,0:T(8,128)(2,1)} %bitcast.19), kind=kLoop, calls=%fused_computation.8 | loop fusion | flops 491520 | bytes 655360 | tf_op jit(solution)/shard_map/keys_x/stack | solution.py:276
  25.5 2.1 %collective-permute-start.5 = (bf16[4,2,32,640]{3,2,1,0:T(8,128)(2,1)}, bf16[4,2,32,640]{3,2,1,0:T(8,128)(2,1)}, u32[]{:S(2)}, u32[]{:S(2)}) collective-permute-start(bf16[4,2,32,640]{3,2,1,0:T(8,128)(2,1)} %pad_maximum_fusion.refs_0_), channel_id=1, source_target_pairs={{0,128},{1,129},{2,130},{3,131},{4,132},{5,133},{6,134},{7,135},{8... | collective-permute-start | bytes 983048 | tf_op jit(solution)/shard_map/keys_x/ppermute | solution.py:277
  27.6 1.5 %collective-permute-start.4 = (bf16[4,2,32,640]{3,2,1,0:T(8,128)(2,1)}, bf16[4,2,32,640]{3,2,1,0:T(8,128)(2,1)}, u32[]{:S(2)}, u32[]{:S(2)}) collective-permute-start(bf16[4,2,32,640]{3,2,1,0:T(8,128)(2,1)} %pad_maximum_fusion.refs_0_), channel_id=1, source_target_pairs={{0,192},{1,193},{2,194},{3,195},{4,196},{5,197},{6,198},{7,199},{8... | collective-permute-start | bytes 983048 | tf_op jit(solution)/shard_map/keys_x/ppermute | solution.py:277
  29.0 0.6 collective-permute-start.3
  29.6 6.3 %all-to-all-done = f32[256,1,64]{2,1,0:T(1,128)S(1)} async-done(((f32[256,1,64]{2,1,0:T(1,128)}), f32[256,1,64]{2,1,0:T(1,128)S(1)}, u32[]{:S(2)}, u32[]{:S(2)}) %all-to-all-start) | async-done | bytes 65568 | tf_op jit(solution)/shard_map/statistics/all_to_all | solution.py:274
  35.9 0.4 shard_map.130
  36.5 1.8 %convert_reduce_fusion = (f32[32]{0:T(128)S(1)}, bf16[32,1280]{1,0:T(8,128)(2,1)S(1)}) fusion(f32[1280]{0:T(1024)} %param.15, bf16[1280,1280]{1,0:T(8,128)(2,1)S(1)} %copy-done, bf16[32,1280]{1,0:T(8,128)(2,1)} %x_ref.1, f32[1280]{0:T(1024)} %param.13, f32[1280]{0:T(1024)} %param.12, f32[1280]{0:T(1024)S(1)} %get-tuple-element.4, f32[1280]{0:T(1024)S(1)} %get-tuple-element.3), kind=kOutput, calls=%fused_computation.10 | convolution fusion | flops 105267168 | bytes 3466368 | tf_op jit(solution)/shard_map/dot_general | solution.py:282
  38.2 0.0 copy-start.5
  38.3 0.2 fusion.6
  38.5 0.4 fusion.3
  38.9 0.8 %broadcast_in_dim.5 = bf16[8,32,640]{2,1,0:T(8,128)(2,1)} broadcast(bf16[32,640]{1,0:T(8,128)(2,1)S(1)} %fusion.3), dimensions={1,2} | broadcast | bytes 368640 | tf_op jit(solution)/shard_map/broadcast_in_dim | solution.py:290
  39.7 4.1 %all-to-all-start.1 = ((bf16[8,32,640]{2,1,0:T(8,128)(2,1)}), bf16[8,32,640]{2,1,0:T(8,128)(2,1)}, u32[]{:S(2)}, u32[]{:S(2)}) async-start(bf16[8,32,640]{2,1,0:T(8,128)(2,1)} %broadcast_in_dim.5), calls=%async_computation.1 | async-start | bytes 655360 | tf_op jit(solution)/shard_map/queries/all_to_all | solution.py:263
  43.8 0.1 collective-permute-start.6
  43.9 0.5 collective-permute-start.9
  44.4 0.3 collective-permute-done.4.refs_2_
  44.7 0.0 collective-permute-start.8
  44.7 0.5 collective-permute-start.7
  45.2 1.9 %fusion.2 = bf16[1,32,640]{2,1,0:T(8,128)(2,1)S(1)} fusion(bf16[1280,640]{1,0:T(8,128)(2,1)} %param.20, bf16[32,1280]{1,0:T(8,128)(2,1)S(1)} %get-tuple-element.6, f32[1280]{0:T(1024)S(1)} %copy-done.8, f32[1280]{0:T(1024)S(1)} %copy-done.9, f32[32]{0:T(128)S(1)} %add_rsqrt_fusion, f32[32]{0:T(128)S(1)} %broadcast_multiply_fusion), kind=kOutput, calls=%fused_computation.6 | convolution fusion | flops 52695040 | bytes 1771776 | tf_op jit(solution)/shard_map/dot_general | solution.py:300
  47.1 0.4 fusion.1
  47.6 0.0 copy-start.2
  47.6 0.7 %copy-done.3 = bf16[4,2,32,640]{3,2,1,0:T(8,128)(2,1)} copy-done((bf16[4,2,32,640]{3,2,1,0:T(8,128)(2,1)}, bf16[4,2,32,640]{3,2,1,0:T(8,128)(2,1)S(1)}, u32[]{:S(2)}) %copy-start.3) | copy-done | bytes 327704
  48.3 4.2 %all-to-all-done.1 = bf16[8,32,640]{2,1,0:T(8,128)(2,1)} async-done(((bf16[8,32,640]{2,1,0:T(8,128)(2,1)}), bf16[8,32,640]{2,1,0:T(8,128)(2,1)}, u32[]{:S(2)}, u32[]{:S(2)}) %all-to-all-start.1) | async-done | bytes 327712 | tf_op jit(solution)/shard_map/queries/all_to_all | solution.py:263
  52.5 1.0 %copy-done.4 = bf16[4,2,32,640]{3,2,1,0:T(8,128)(2,1)S(1)} copy-done((bf16[4,2,32,640]{3,2,1,0:T(8,128)(2,1)S(1)}, bf16[4,2,32,640]{3,2,1,0:T(8,128)(2,1)}, u32[]{:S(2)}) %copy-start.4) | copy-done | bytes 327704
  53.5 5.7 %shard_map.131 = bf16[8,32,768]{2,1,0:T(8,128)(2,1)S(1)} custom-call(s32[1]{0:T(128)} %bitcast.5.place_ref, bf16[256,640]{1,0:T(8,128)(2,1)} %bitcast.6.q_ref, bf16[2,32,640]{2,1,0:T(8,128)(2,1)S(1)} %pad_maximum_fusion.1.fresh_ref, bf16[4,2,32,640]{3,2,1,0:T(8,128)(2,1)} %pad_maximum_fusion.refs_0_, bf16[4,2,32,640]{3,2,1,0:T(8,128)(2,1)} %collective-permute-done.3.refs_1_, ...), custom_call_target="tpu_custom_call" | custom-call | flops 671088640 | bytes 4194304 | tf_op jit(solution)/shard_map/pallas_call | solution.py:189
  59.2 10.7 %all_to_all.15.parts_ref = bf16[8,32,768]{2,1,0:T(8,128)(2,1)S(1)} all-to-all(bf16[8,32,768]{2,1,0:T(8,128)(2,1)S(1)} %shard_map.131), channel_id=1, replica_groups={{0,2,4,6,32,34,36,38},{1,3,5,7,33,35,37,39},{8,10,12,14,40,42,44,46},{9..., dimensions={0} | all-to-all | bytes 786432 | tf_op jit(solution)/shard_map/partials/all_to_all | solution.py:263
  69.9 0.8 %partials.1 = bf16[32,640]{1,0:T(8,128)(2,1)} custom-call(bf16[8,32,768]{2,1,0:T(8,128)(2,1)S(1)} %all_to_all.15.parts_ref), custom_call_target="tpu_custom_call" | custom-call | tf_op jit(solution)/shard_map/partials/pallas_call | solution.py:224
  (28 shorter events, 0.1 us)
Async XLA Ops:
  0.6 35.8 %copy-start = (bf16[1280,1280]{1,0:T(8,128)(2,1)S(1)}, bf16[1280,1280]{1,0:T(8,128)(2,1)}, u32[]{:S(2)}) copy-start(bf16[1280,1280]{1,0:T(8,128)(2,1)} %param.14) | copy-start | bytes 9830404
  0.6 23.1 %collective-permute-start = (bf16[2,32,640]{2,1,0:T(8,128)(2,1)}, bf16[2,32,640]{2,1,0:T(8,128)(2,1)S(1)}, u32[]{:S(2)}, u32[]{:S(2)}) collective-permute-start(bf16[2,32,640]{2,1,0:T(8,128)(2,1)} %param.21), channel_id=1, source_target_pairs={{0,16},{1,17},{2,18},{3,19},{4,20},{5,21},{6,22},{7,23},{8,24},{9,... | collective-permute-start | bytes 245768 | tf_op jit(solution)/shard_map/keys_z/ppermute | solution.py:271
  7.9 15.8 %collective-permute-start.2 = (bf16[2,32,640]{2,1,0:T(8,128)(2,1)}, bf16[2,32,640]{2,1,0:T(8,128)(2,1)}, u32[]{:S(2)}, u32[]{:S(2)}) collective-permute-start(bf16[2,32,640]{2,1,0:T(8,128)(2,1)} %param.21), channel_id=1, source_target_pairs={{0,24},{1,25},{2,26},{3,27},{4,28},{5,29},{6,30},{7,31},{8,0},{9,1... | collective-permute-start | bytes 245768 | tf_op jit(solution)/shard_map/keys_z/ppermute | solution.py:271
  7.9 15.8 %collective-permute-start.1 = (bf16[2,32,640]{2,1,0:T(8,128)(2,1)}, bf16[2,32,640]{2,1,0:T(8,128)(2,1)}, u32[]{:S(2)}, u32[]{:S(2)}) collective-permute-start(bf16[2,32,640]{2,1,0:T(8,128)(2,1)} %param.21), channel_id=1, source_target_pairs={{0,8},{1,9},{2,10},{3,11},{4,12},{5,13},{6,14},{7,15},{8,16},{9,17... | collective-permute-start | bytes 245768 | tf_op jit(solution)/shard_map/keys_z/ppermute | solution.py:271
  10.8 0.9 %copy-start.1 = (bf16[32,1280]{1,0:T(8,128)(2,1)S(1)}, bf16[32,1280]{1,0:T(8,128)(2,1)}, u32[]{:S(2)}) copy-start(bf16[32,1280]{1,0:T(8,128)(2,1)} %x_ref.1) | copy-start | bytes 245764
  13.1 22.8 %all-to-all-start = ((f32[256,1,64]{2,1,0:T(1,128)}), f32[256,1,64]{2,1,0:T(1,128)S(1)}, u32[]{:S(2)}, u32[]{:S(2)}) async-start(f32[256,1,64]{2,1,0:T(1,128)} %bitcast.1), calls=%async_computation | async-start | bytes 262144 | tf_op jit(solution)/shard_map/statistics/all_to_all | solution.py:274
  25.5 18.4 %collective-permute-start.5 = (bf16[4,2,32,640]{3,2,1,0:T(8,128)(2,1)}, bf16[4,2,32,640]{3,2,1,0:T(8,128)(2,1)}, u32[]{:S(2)}, u32[]{:S(2)}) collective-permute-start(bf16[4,2,32,640]{3,2,1,0:T(8,128)(2,1)} %pad_maximum_fusion.refs_0_), channel_id=1, source_target_pairs={{0,128},{1,129},{2,130},{3,131},{4,132},{5,133},{6,134},{7,135},{8... | collective-permute-start | bytes 983048 | tf_op jit(solution)/shard_map/keys_x/ppermute | solution.py:277
  27.6 17.1 %collective-permute-start.4 = (bf16[4,2,32,640]{3,2,1,0:T(8,128)(2,1)}, bf16[4,2,32,640]{3,2,1,0:T(8,128)(2,1)}, u32[]{:S(2)}, u32[]{:S(2)}) collective-permute-start(bf16[4,2,32,640]{3,2,1,0:T(8,128)(2,1)} %pad_maximum_fusion.refs_0_), channel_id=1, source_target_pairs={{0,192},{1,193},{2,194},{3,195},{4,196},{5,197},{6,198},{7,199},{8... | collective-permute-start | bytes 983048 | tf_op jit(solution)/shard_map/keys_x/ppermute | solution.py:277
  29.0 15.7 %collective-permute-start.3 = (bf16[4,2,32,640]{3,2,1,0:T(8,128)(2,1)}, bf16[4,2,32,640]{3,2,1,0:T(8,128)(2,1)}, u32[]{:S(2)}, u32[]{:S(2)}) collective-permute-start(bf16[4,2,32,640]{3,2,1,0:T(8,128)(2,1)} %pad_maximum_fusion.refs_0_), channel_id=1, source_target_pairs={{0,64},{1,65},{2,66},{3,67},{4,68},{5,69},{6,70},{7,71},{8,72},{9,... | collective-permute-start | bytes 983048 | tf_op jit(solution)/shard_map/keys_x/ppermute | solution.py:277
  36.4 2.1 %copy-start.6 = (bf16[1280,640]{1,0:T(8,128)(2,1)S(1)}, bf16[1280,640]{1,0:T(8,128)(2,1)}, u32[]{:S(2)}) copy-start(bf16[1280,640]{1,0:T(8,128)(2,1)} %param.18) | copy-start | bytes 4915204
  36.4 2.0 %copy-start.8 = (f32[1280]{0:T(1024)S(1)}, f32[1280]{0:T(1024)}, u32[]{:S(2)}) copy-start(f32[1280]{0:T(1024)} %param.17) | copy-start | bytes 15364
  36.4 2.0 %copy-start.9 = (f32[1280]{0:T(1024)S(1)}, f32[1280]{0:T(1024)}, u32[]{:S(2)}) copy-start(f32[1280]{0:T(1024)} %param.16) | copy-start | bytes 15364
  38.2 8.9 %copy-start.5 = (bf16[32,1280]{1,0:T(8,128)(2,1)}, bf16[32,1280]{1,0:T(8,128)(2,1)S(1)}, u32[]{:S(2)}) copy-start(bf16[32,1280]{1,0:T(8,128)(2,1)S(1)} %get-tuple-element.6) | copy-start | bytes 245764
  39.7 12.8 %all-to-all-start.1 = ((bf16[8,32,640]{2,1,0:T(8,128)(2,1)}), bf16[8,32,640]{2,1,0:T(8,128)(2,1)}, u32[]{:S(2)}, u32[]{:S(2)}) async-start(bf16[8,32,640]{2,1,0:T(8,128)(2,1)} %broadcast_in_dim.5), calls=%async_computation.1 | async-start | bytes 655360 | tf_op jit(solution)/shard_map/queries/all_to_all | solution.py:263
  43.8 3.3 %copy-start.7 = (bf16[1280,640]{1,0:T(8,128)(2,1)S(1)}, bf16[1280,640]{1,0:T(8,128)(2,1)}, u32[]{:S(2)}) copy-start(bf16[1280,640]{1,0:T(8,128)(2,1)} %param.19) | copy-start | bytes 4915204
  43.8 3.8 %collective-permute-start.6 = (bf16[4,2,32,640]{3,2,1,0:T(8,128)(2,1)}, bf16[4,2,32,640]{3,2,1,0:T(8,128)(2,1)S(1)}, u32[]{:S(2)}, u32[]{:S(2)}) collective-permute-start(bf16[4,2,32,640]{3,2,1,0:T(8,128)(2,1)} %pad_maximum_fusion.refs_0_), channel_id=1, source_target_pairs={{0,1},{1,0},{2,3},{3,2},{4,5},{5,4},{6,7},{7,6},{8,9},{9,8},{10,11... | collective-permute-start | bytes 983048 | tf_op jit(solution)/shard_map/keys_core/ppermute | solution.py:294
  43.9 8.6 %collective-permute-start.9 = (bf16[4,2,32,640]{3,2,1,0:T(8,128)(2,1)}, bf16[4,2,32,640]{3,2,1,0:T(8,128)(2,1)}, u32[]{:S(2)}, u32[]{:S(2)}) collective-permute-start(bf16[4,2,32,640]{3,2,1,0:T(8,128)(2,1)} %collective-permute-done.5.refs_3_), channel_id=1, source_target_pairs={{0,1},{1,0},{2,3},{3,2},{4,5},{5,4},{6,7},{7,6},{8,9},{9,8},{10,11... | collective-permute-start | bytes 983048 | tf_op jit(solution)/shard_map/keys_core/ppermute | solution.py:294
  44.7 7.8 %collective-permute-start.8 = (bf16[4,2,32,640]{3,2,1,0:T(8,128)(2,1)}, bf16[4,2,32,640]{3,2,1,0:T(8,128)(2,1)}, u32[]{:S(2)}, u32[]{:S(2)}) collective-permute-start(bf16[4,2,32,640]{3,2,1,0:T(8,128)(2,1)} %collective-permute-done.4.refs_2_), channel_id=1, source_target_pairs={{0,1},{1,0},{2,3},{3,2},{4,5},{5,4},{6,7},{7,6},{8,9},{9,8},{10,11... | collective-permute-start | bytes 983048 | tf_op jit(solution)/shard_map/keys_core/ppermute | solution.py:294
  44.7 7.8 %collective-permute-start.7 = (bf16[4,2,32,640]{3,2,1,0:T(8,128)(2,1)}, bf16[4,2,32,640]{3,2,1,0:T(8,128)(2,1)}, u32[]{:S(2)}, u32[]{:S(2)}) collective-permute-start(bf16[4,2,32,640]{3,2,1,0:T(8,128)(2,1)} %collective-permute-done.3.refs_1_), channel_id=1, source_target_pairs={{0,1},{1,0},{2,3},{3,2},{4,5},{5,4},{6,7},{7,6},{8,9},{9,8},{10,11... | collective-permute-start | bytes 983048 | tf_op jit(solution)/shard_map/keys_core/ppermute | solution.py:294
  47.6 11.6 %copy-start.2 = (bf16[2,32,640]{2,1,0:T(8,128)(2,1)}, bf16[2,32,640]{2,1,0:T(8,128)(2,1)S(1)}, u32[]{:S(2)}) copy-start(bf16[2,32,640]{2,1,0:T(8,128)(2,1)S(1)} %pad_maximum_fusion.1.fresh_ref) | copy-start | bytes 245764
  47.6 0.7 %copy-start.3 = (bf16[4,2,32,640]{3,2,1,0:T(8,128)(2,1)}, bf16[4,2,32,640]{3,2,1,0:T(8,128)(2,1)S(1)}, u32[]{:S(2)}) copy-start(bf16[4,2,32,640]{3,2,1,0:T(8,128)(2,1)S(1)} %collective-permute-done.6.refs_4_) | copy-start | bytes 983044
  52.5 1.0 %copy-start.4 = (bf16[4,2,32,640]{3,2,1,0:T(8,128)(2,1)S(1)}, bf16[4,2,32,640]{3,2,1,0:T(8,128)(2,1)}, u32[]{:S(2)}) copy-start(bf16[4,2,32,640]{3,2,1,0:T(8,128)(2,1)} %copy-done.3) | copy-start | bytes 983044

commit v6 on v5

--- a/solution.py
+++ b/solution.py
@@ -291,6 +291,7 @@
     with jax.named_scope("queries"):
         query = exchange(query, SHARE).reshape(shared * latent.shape[0], INNER)
     with jax.named_scope("keys_core"):
+        parts[:2] = lax.optimization_barrier(parts[:2])
         parts = parts + [lax.ppermute(part, AXES, moved(dcore=1)) for part in parts]
     row, col = lax.axis_index("row"), lax.axis_index("col")
     place = ((row & 1) << 2) | (((col >> 2) & 1) << 1) | ((col >> 1) & 1)

time: 71.2 us -> 70.3 us (0.987)
  local copies, waits for them, and re-layouts: 3.43 us -> 1.73 us
  waiting for transfers between devices: 10.8 us -> 11.6 us
    unnamed x20 -> x16, local copies, waits for them, and re-layouts: 2.62 us -> 0.93 us
where the time goes in v6:
time: 70.3 us; the launch traced here: 69.9 us
  starting transfers between devices  30 us (43%)
  waiting for transfers between devices  11.6 us (17%)
  blocking collectives  10.7 us (15%)
  Pallas kernels  8.49 us (12%)
  matrix products  4.52 us (6%)
  other arithmetic  1.96 us (3%)
  local copies, waits for them, and re-layouts  1.73 us (2%)
  between operations  0.87 us (1%)
    all_to_all x1, blocking collectives, exchange(): return lax.all_to_all(value, AXES, 0, 0, axis_index_groups=groups_of(mask))  10.7 us
    all_to_all x1, starting transfers between devices, local(): stats = lax.all_to_all(here, AXES, 0, 0).reshape(DEVICES, 2 * GROUPS)  10.6 us
    ppermute x3, starting transfers between devices, local(): along_z = [lax.ppermute(stale_kv, AXES, moved(dz=d)) for d in (4, 2, 6)]  10.2 us
    all_to_all x1, waiting for transfers between devices, local(): stats = lax.all_to_all(here, AXES, 0, 0).reshape(DEVICES, 2 * GROUPS)  6.31 us
    pallas_call x1, Pallas kernels, attend(): pl.pallas_call(attend_kernel, out_shape=jax.ShapeDtypeStruct((rows // pat...  5.89 us
    all_to_all x1, waiting for transfers between devices, exchange(): return lax.all_to_all(value, AXES, 0, 0, axis_index_groups=groups_of(mask))  4.62 us
    ppermute x3, starting transfers between devices, local(): parts = [line] + [lax.ppermute(line, AXES, moved(dx=d)) for d in (1, 3, 2)]  4.1 us
    all_to_all x1, starting transfers between devices, exchange(): return lax.all_to_all(value, AXES, 0, 0, axis_index_groups=groups_of(mask))  4.07 us
  transfers between devices with their start and end apart: 12, of which 3 were waited for; matrix products, arithmetic and copies ran while one was open for 10% of the time, Pallas kernels for 3%

profile of v6, /device:TPU:2, one launch (start us, length us, event | category | flops | bytes accessed | tf_op | source)
XLA Modules:
  0.0 69.9 jit_solution(14515701768052387191)
XLA Ops:
  0.6 0.0 copy-start
  0.6 7.3 %collective-permute-start = (bf16[2,32,640]{2,1,0:T(8,128)(2,1)}, bf16[2,32,640]{2,1,0:T(8,128)(2,1)S(1)}, u32[]{:S(2)}, u32[]{:S(2)}) collective-permute-start(bf16[2,32,640]{2,1,0:T(8,128)(2,1)} %param.21), channel_id=1, source_target_pairs={{0,16},{1,17},{2,18},{3,19},{4,20},{5,21},{6,22},{7,23},{8,24},{9,... | collective-permute-start | bytes 245768 | tf_op jit(solution)/shard_map/keys_z/ppermute | solution.py:271
  7.9 2.9 %collective-permute-start.1 = (bf16[2,32,640]{2,1,0:T(8,128)(2,1)}, bf16[2,32,640]{2,1,0:T(8,128)(2,1)}, u32[]{:S(2)}, u32[]{:S(2)}) collective-permute-start(bf16[2,32,640]{2,1,0:T(8,128)(2,1)} %param.21), channel_id=1, source_target_pairs={{0,8},{1,9},{2,10},{3,11},{4,12},{5,13},{6,14},{7,15},{8,16},{9,17... | collective-permute-start | bytes 245768 | tf_op jit(solution)/shard_map/keys_z/ppermute | solution.py:271
  10.8 0.9 %copy-done.1 = bf16[32,1280]{1,0:T(8,128)(2,1)S(1)} copy-done((bf16[32,1280]{1,0:T(8,128)(2,1)S(1)}, bf16[32,1280]{1,0:T(8,128)(2,1)}, u32[]{:S(2)}) %copy-start.1) | copy-done | bytes 81944
  11.7 1.4 %statistics.1 = f32[256,64]{1,0:T(8,128)} custom-call(bf16[32,1280]{1,0:T(8,128)(2,1)S(1)} %copy-done.1), custom_call_target="tpu_custom_call" | custom-call | tf_op jit(solution)/shard_map/statistics/pallas_call | solution.py:61
  13.1 10.6 %all-to-all-start = ((f32[256,1,64]{2,1,0:T(1,128)}), f32[256,1,64]{2,1,0:T(1,128)S(1)}, u32[]{:S(2)}, u32[]{:S(2)}) async-start(f32[256,1,64]{2,1,0:T(1,128)} %bitcast.1), calls=%async_computation | async-start | bytes 262144 | tf_op jit(solution)/shard_map/statistics/all_to_all | solution.py:274
  23.8 1.7 %pad_maximum_fusion.refs_0_ = bf16[4,2,32,640]{3,2,1,0:T(8,128)(2,1)} fusion(bf16[1,2,32,640]{3,2,1,0:T(8,128)(2,1)} %bitcast.10, bf16[1,2,32,640]{3,2,1,0:T(8,128)(2,1)} %bitcast.9, bf16[1,2,32,640]{3,2,1,0:T(8,128)(2,1)S(1)} %bitcast.20, bf16[1,2,32,640]{3,2,1,0:T(8,128)(2,1)} %bitcast.19), kind=kLoop, calls=%fused_computation.8 | loop fusion | flops 491520 | bytes 655360 | tf_op jit(solution)/shard_map/keys_x/stack | solution.py:276
  25.5 2.1 %collective-permute-start.5 = (bf16[4,2,32,640]{3,2,1,0:T(8,128)(2,1)}, bf16[4,2,32,640]{3,2,1,0:T(8,128)(2,1)}, u32[]{:S(2)}, u32[]{:S(2)}) collective-permute-start(bf16[4,2,32,640]{3,2,1,0:T(8,128)(2,1)} %pad_maximum_fusion.refs_0_), channel_id=1, source_target_pairs={{0,128},{1,129},{2,130},{3,131},{4,132},{5,133},{6,134},{7,135},{8... | collective-permute-start | bytes 983048 | tf_op jit(solution)/shard_map/keys_x/ppermute | solution.py:277
  27.6 1.5 %collective-permute-start.4 = (bf16[4,2,32,640]{3,2,1,0:T(8,128)(2,1)}, bf16[4,2,32,640]{3,2,1,0:T(8,128)(2,1)}, u32[]{:S(2)}, u32[]{:S(2)}) collective-permute-start(bf16[4,2,32,640]{3,2,1,0:T(8,128)(2,1)} %pad_maximum_fusion.refs_0_), channel_id=1, source_target_pairs={{0,192},{1,193},{2,194},{3,195},{4,196},{5,197},{6,198},{7,199},{8... | collective-permute-start | bytes 983048 | tf_op jit(solution)/shard_map/keys_x/ppermute | solution.py:277
  29.0 0.6 collective-permute-start.3
  29.6 6.3 %all-to-all-done = f32[256,1,64]{2,1,0:T(1,128)S(1)} async-done(((f32[256,1,64]{2,1,0:T(1,128)}), f32[256,1,64]{2,1,0:T(1,128)S(1)}, u32[]{:S(2)}, u32[]{:S(2)}) %all-to-all-start) | async-done | bytes 65568 | tf_op jit(solution)/shard_map/statistics/all_to_all | solution.py:274
  35.9 0.4 shard_map.130
  36.4 0.0 copy-start.6
  36.4 0.0 copy-start.7
  36.4 1.8 %convert_reduce_fusion = (f32[32]{0:T(128)S(1)}, bf16[32,1280]{1,0:T(8,128)(2,1)S(1)}) fusion(f32[1280]{0:T(1024)} %param.15, bf16[1280,1280]{1,0:T(8,128)(2,1)S(1)} %copy-done, bf16[32,1280]{1,0:T(8,128)(2,1)} %x_ref.1, f32[1280]{0:T(1024)} %param.13, f32[1280]{0:T(1024)} %param.12, f32[1280]{0:T(1024)S(1)} %get-tuple-element.8, f32[1280]{0:T(1024)S(1)} %get-tuple-element.7), kind=kOutput, calls=%fused_computation.10 | convolution fusion | flops 105267168 | bytes 3466368 | tf_op jit(solution)/shard_map/dot_general | solution.py:282
  38.2 0.0 copy-start.3
  38.2 0.2 fusion.6
  38.5 0.4 fusion.3
  38.9 0.8 %broadcast_in_dim.5 = bf16[8,32,640]{2,1,0:T(8,128)(2,1)} broadcast(bf16[32,640]{1,0:T(8,128)(2,1)S(1)} %fusion.3), dimensions={1,2} | broadcast | bytes 368640 | tf_op jit(solution)/shard_map/broadcast_in_dim | solution.py:290
  39.7 4.1 %all-to-all-start.1 = ((bf16[8,32,640]{2,1,0:T(8,128)(2,1)}), bf16[8,32,640]{2,1,0:T(8,128)(2,1)}, u32[]{:S(2)}, u32[]{:S(2)}) async-start(bf16[8,32,640]{2,1,0:T(8,128)(2,1)} %broadcast_in_dim.5), calls=%async_computation.1 | async-start | bytes 655360 | tf_op jit(solution)/shard_map/queries/all_to_all | solution.py:263
  43.8 0.0 copy-start.5
  43.8 0.7 collective-permute-done.3.refs_1_
  44.4 0.5 collective-permute-start.7
  45.0 0.0 collective-permute-start.9
  45.0 0.5 collective-permute-start.8
  45.5 1.9 %fusion.2 = bf16[1,32,640]{2,1,0:T(8,128)(2,1)S(1)} fusion(bf16[1280,640]{1,0:T(8,128)(2,1)} %param.20, bf16[32,1280]{1,0:T(8,128)(2,1)S(1)} %get-tuple-element.10, f32[1280]{0:T(1024)S(1)} %copy-done.6, f32[1280]{0:T(1024)S(1)} %copy-done.7, f32[32]{0:T(128)S(1)} %add_rsqrt_fusion, f32[32]{0:T(128)S(1)} %broadcast_multiply_fusion), kind=kOutput, calls=%fused_computation.6 | convolution fusion | flops 52695040 | bytes 1771776 | tf_op jit(solution)/shard_map/dot_general | solution.py:301
  47.4 0.4 fusion.1
  47.8 0.0 copy-start.2
  47.8 4.6 %all-to-all-done.1 = bf16[8,32,640]{2,1,0:T(8,128)(2,1)} async-done(((bf16[8,32,640]{2,1,0:T(8,128)(2,1)}), bf16[8,32,640]{2,1,0:T(8,128)(2,1)}, u32[]{:S(2)}, u32[]{:S(2)}) %all-to-all-start.1) | async-done | bytes 327712 | tf_op jit(solution)/shard_map/queries/all_to_all | solution.py:263
  52.5 5.9 %shard_map.131 = bf16[8,32,768]{2,1,0:T(8,128)(2,1)S(1)} custom-call(s32[1]{0:T(128)} %bitcast.5.place_ref, bf16[256,640]{1,0:T(8,128)(2,1)} %bitcast.6.q_ref, bf16[2,32,640]{2,1,0:T(8,128)(2,1)S(1)} %pad_maximum_fusion.1.fresh_ref, bf16[4,2,32,640]{3,2,1,0:T(8,128)(2,1)} %pad_maximum_fusion.refs_0_, bf16[4,2,32,640]{3,2,1,0:T(8,128)(2,1)} %collective-permute-done.3.refs_1_, ...), custom_call_target="tpu_custom_call" | custom-call | flops 671088640 | bytes 4194304 | tf_op jit(solution)/shard_map/pallas_call | solution.py:189
  58.4 10.7 %all_to_all.15.parts_ref = bf16[8,32,768]{2,1,0:T(8,128)(2,1)S(1)} all-to-all(bf16[8,32,768]{2,1,0:T(8,128)(2,1)S(1)} %shard_map.131), channel_id=1, replica_groups={{0,2,4,6,32,34,36,38},{1,3,5,7,33,35,37,39},{8,10,12,14,40,42,44,46},{9..., dimensions={0} | all-to-all | bytes 786432 | tf_op jit(solution)/shard_map/partials/all_to_all | solution.py:263
  69.1 0.8 %partials.1 = bf16[32,640]{1,0:T(8,128)(2,1)} custom-call(bf16[8,32,768]{2,1,0:T(8,128)(2,1)S(1)} %all_to_all.15.parts_ref), custom_call_target="tpu_custom_call" | custom-call | tf_op jit(solution)/shard_map/partials/pallas_call | solution.py:224
  (24 shorter events, 0.1 us)
Async XLA Ops:
  0.6 35.8 %copy-start = (bf16[1280,1280]{1,0:T(8,128)(2,1)S(1)}, bf16[1280,1280]{1,0:T(8,128)(2,1)}, u32[]{:S(2)}) copy-start(bf16[1280,1280]{1,0:T(8,128)(2,1)} %param.14) | copy-start | bytes 9830404
  0.6 23.1 %collective-permute-start = (bf16[2,32,640]{2,1,0:T(8,128)(2,1)}, bf16[2,32,640]{2,1,0:T(8,128)(2,1)S(1)}, u32[]{:S(2)}, u32[]{:S(2)}) collective-permute-start(bf16[2,32,640]{2,1,0:T(8,128)(2,1)} %param.21), channel_id=1, source_target_pairs={{0,16},{1,17},{2,18},{3,19},{4,20},{5,21},{6,22},{7,23},{8,24},{9,... | collective-permute-start | bytes 245768 | tf_op jit(solution)/shard_map/keys_z/ppermute | solution.py:271
  7.9 15.8 %collective-permute-start.2 = (bf16[2,32,640]{2,1,0:T(8,128)(2,1)}, bf16[2,32,640]{2,1,0:T(8,128)(2,1)}, u32[]{:S(2)}, u32[]{:S(2)}) collective-permute-start(bf16[2,32,640]{2,1,0:T(8,128)(2,1)} %param.21), channel_id=1, source_target_pairs={{0,24},{1,25},{2,26},{3,27},{4,28},{5,29},{6,30},{7,31},{8,0},{9,1... | collective-permute-start | bytes 245768 | tf_op jit(solution)/shard_map/keys_z/ppermute | solution.py:271
  7.9 15.8 %collective-permute-start.1 = (bf16[2,32,640]{2,1,0:T(8,128)(2,1)}, bf16[2,32,640]{2,1,0:T(8,128)(2,1)}, u32[]{:S(2)}, u32[]{:S(2)}) collective-permute-start(bf16[2,32,640]{2,1,0:T(8,128)(2,1)} %param.21), channel_id=1, source_target_pairs={{0,8},{1,9},{2,10},{3,11},{4,12},{5,13},{6,14},{7,15},{8,16},{9,17... | collective-permute-start | bytes 245768 | tf_op jit(solution)/shard_map/keys_z/ppermute | solution.py:271
  10.8 0.9 %copy-start.1 = (bf16[32,1280]{1,0:T(8,128)(2,1)S(1)}, bf16[32,1280]{1,0:T(8,128)(2,1)}, u32[]{:S(2)}) copy-start(bf16[32,1280]{1,0:T(8,128)(2,1)} %x_ref.1) | copy-start | bytes 245764
  13.1 22.8 %all-to-all-start = ((f32[256,1,64]{2,1,0:T(1,128)}), f32[256,1,64]{2,1,0:T(1,128)S(1)}, u32[]{:S(2)}, u32[]{:S(2)}) async-start(f32[256,1,64]{2,1,0:T(1,128)} %bitcast.1), calls=%async_computation | async-start | bytes 262144 | tf_op jit(solution)/shard_map/statistics/all_to_all | solution.py:274
  25.5 19.4 %collective-permute-start.5 = (bf16[4,2,32,640]{3,2,1,0:T(8,128)(2,1)}, bf16[4,2,32,640]{3,2,1,0:T(8,128)(2,1)}, u32[]{:S(2)}, u32[]{:S(2)}) collective-permute-start(bf16[4,2,32,640]{3,2,1,0:T(8,128)(2,1)} %pad_maximum_fusion.refs_0_), channel_id=1, source_target_pairs={{0,128},{1,129},{2,130},{3,131},{4,132},{5,133},{6,134},{7,135},{8... | collective-permute-start | bytes 983048 | tf_op jit(solution)/shard_map/keys_x/ppermute | solution.py:277
  27.6 17.4 %collective-permute-start.4 = (bf16[4,2,32,640]{3,2,1,0:T(8,128)(2,1)}, bf16[4,2,32,640]{3,2,1,0:T(8,128)(2,1)}, u32[]{:S(2)}, u32[]{:S(2)}) collective-permute-start(bf16[4,2,32,640]{3,2,1,0:T(8,128)(2,1)} %pad_maximum_fusion.refs_0_), channel_id=1, source_target_pairs={{0,192},{1,193},{2,194},{3,195},{4,196},{5,197},{6,198},{7,199},{8... | collective-permute-start | bytes 983048 | tf_op jit(solution)/shard_map/keys_x/ppermute | solution.py:277
  29.0 15.4 %collective-permute-start.3 = (bf16[4,2,32,640]{3,2,1,0:T(8,128)(2,1)}, bf16[4,2,32,640]{3,2,1,0:T(8,128)(2,1)}, u32[]{:S(2)}, u32[]{:S(2)}) collective-permute-start(bf16[4,2,32,640]{3,2,1,0:T(8,128)(2,1)} %pad_maximum_fusion.refs_0_), channel_id=1, source_target_pairs={{0,64},{1,65},{2,66},{3,67},{4,68},{5,69},{6,70},{7,71},{8,72},{9,... | collective-permute-start | bytes 983048 | tf_op jit(solution)/shard_map/keys_x/ppermute | solution.py:277
  36.4 2.1 %copy-start.4 = (bf16[1280,640]{1,0:T(8,128)(2,1)S(1)}, bf16[1280,640]{1,0:T(8,128)(2,1)}, u32[]{:S(2)}) copy-start(bf16[1280,640]{1,0:T(8,128)(2,1)} %param.18) | copy-start | bytes 4915204
  36.4 2.0 %copy-start.6 = (f32[1280]{0:T(1024)S(1)}, f32[1280]{0:T(1024)}, u32[]{:S(2)}) copy-start(f32[1280]{0:T(1024)} %param.17) | copy-start | bytes 15364
  36.4 2.0 %copy-start.7 = (f32[1280]{0:T(1024)S(1)}, f32[1280]{0:T(1024)}, u32[]{:S(2)}) copy-start(f32[1280]{0:T(1024)} %param.16) | copy-start | bytes 15364
  38.2 9.1 %copy-start.3 = (bf16[32,1280]{1,0:T(8,128)(2,1)}, bf16[32,1280]{1,0:T(8,128)(2,1)S(1)}, u32[]{:S(2)}) copy-start(bf16[32,1280]{1,0:T(8,128)(2,1)S(1)} %get-tuple-element.10) | copy-start | bytes 245764
  39.7 12.8 %all-to-all-start.1 = ((bf16[8,32,640]{2,1,0:T(8,128)(2,1)}), bf16[8,32,640]{2,1,0:T(8,128)(2,1)}, u32[]{:S(2)}, u32[]{:S(2)}) async-start(bf16[8,32,640]{2,1,0:T(8,128)(2,1)} %broadcast_in_dim.5), calls=%async_computation.1 | async-start | bytes 655360 | tf_op jit(solution)/shard_map/queries/all_to_all | solution.py:263
  43.8 3.6 %copy-start.5 = (bf16[1280,640]{1,0:T(8,128)(2,1)S(1)}, bf16[1280,640]{1,0:T(8,128)(2,1)}, u32[]{:S(2)}) copy-start(bf16[1280,640]{1,0:T(8,128)(2,1)} %param.19) | copy-start | bytes 4915204
  44.4 8.0 %collective-permute-start.6 = (bf16[4,2,32,640]{3,2,1,0:T(8,128)(2,1)}, bf16[4,2,32,640]{3,2,1,0:T(8,128)(2,1)}, u32[]{:S(2)}, u32[]{:S(2)}) collective-permute-start(bf16[4,2,32,640]{3,2,1,0:T(8,128)(2,1)} %pad_maximum_fusion.refs_0_), channel_id=1, source_target_pairs={{0,1},{1,0},{2,3},{3,2},{4,5},{5,4},{6,7},{7,6},{8,9},{9,8},{10,11... | collective-permute-start | bytes 983048 | tf_op jit(solution)/shard_map/keys_core/ppermute | solution.py:295
  44.4 8.0 %collective-permute-start.7 = (bf16[4,2,32,640]{3,2,1,0:T(8,128)(2,1)}, bf16[4,2,32,640]{3,2,1,0:T(8,128)(2,1)}, u32[]{:S(2)}, u32[]{:S(2)}) collective-permute-start(bf16[4,2,32,640]{3,2,1,0:T(8,128)(2,1)} %collective-permute-done.3.refs_1_), channel_id=1, source_target_pairs={{0,1},{1,0},{2,3},{3,2},{4,5},{5,4},{6,7},{7,6},{8,9},{9,8},{10,11... | collective-permute-start | bytes 983048 | tf_op jit(solution)/shard_map/keys_core/ppermute | solution.py:295
  45.0 7.5 %collective-permute-start.9 = (bf16[4,2,32,640]{3,2,1,0:T(8,128)(2,1)}, bf16[4,2,32,640]{3,2,1,0:T(8,128)(2,1)}, u32[]{:S(2)}, u32[]{:S(2)}) collective-permute-start(bf16[4,2,32,640]{3,2,1,0:T(8,128)(2,1)} %collective-permute-done.5.refs_3_), channel_id=1, source_target_pairs={{0,1},{1,0},{2,3},{3,2},{4,5},{5,4},{6,7},{7,6},{8,9},{9,8},{10,11... | collective-permute-start | bytes 983048 | tf_op jit(solution)/shard_map/keys_core/ppermute | solution.py:295
  45.0 7.5 %collective-permute-start.8 = (bf16[4,2,32,640]{3,2,1,0:T(8,128)(2,1)}, bf16[4,2,32,640]{3,2,1,0:T(8,128)(2,1)}, u32[]{:S(2)}, u32[]{:S(2)}) collective-permute-start(bf16[4,2,32,640]{3,2,1,0:T(8,128)(2,1)} %collective-permute-done.4.refs_2_), channel_id=1, source_target_pairs={{0,1},{1,0},{2,3},{3,2},{4,5},{5,4},{6,7},{7,6},{8,9},{9,8},{10,11... | collective-permute-start | bytes 983048 | tf_op jit(solution)/shard_map/keys_core/ppermute | solution.py:295
  47.8 10.6 %copy-start.2 = (bf16[2,32,640]{2,1,0:T(8,128)(2,1)}, bf16[2,32,640]{2,1,0:T(8,128)(2,1)S(1)}, u32[]{:S(2)}) copy-start(bf16[2,32,640]{2,1,0:T(8,128)(2,1)S(1)} %pad_maximum_fusion.1.fresh_ref) | copy-start | bytes 245764

commit v7 on v6

--- a/solution.py
+++ b/solution.py
@@ -67,7 +67,7 @@
     )(x)
 
 
-def coefficients_kernel(entries, stats_ref, out_ref):
+def coefficients_kernel(entries, stats_ref, mean_ref, scale_ref):
     peers = stats_ref.shape[0]
     means = stats_ref[:, :GROUPS]
     mean = jnp.sum(means, axis=0, keepdims=True) * (1.0 / peers)
@@ -79,21 +79,21 @@
     scale = jnp.concatenate([scale, rest], axis=1)
     both = lax.dot_general(
         jnp.concatenate([pieces(mean), pieces(scale)], axis=0),
-        member_of(out_ref.shape[1]),
+        member_of(mean_ref.shape[0]),
         NT,
         preferred_element_type=jnp.float32,
     )
-    out_ref[...] = jnp.concatenate(
-        [both[at : at + 1] + both[at + 1 : at + 2] + both[at + 2 : at + 3] for at in (0, 3)], axis=0
-    )
+    for at, ref in ((0, mean_ref), (3, scale_ref)):
+        row = both[at : at + 1] + both[at + 1 : at + 2] + both[at + 2 : at + 3]
+        ref[...] = row.reshape(ref.shape)
 
 
 def coefficients(stats, entries, chans):
     return pl.pallas_call(
         functools.partial(coefficients_kernel, entries),
-        out_shape=jax.ShapeDtypeStruct((2, chans), jnp.float32),
+        out_shape=(jax.ShapeDtypeStruct((chans,), jnp.float32),) * 2,
         in_specs=[VMEM],
-        out_specs=VMEM,
+        out_specs=(VMEM, VMEM),
         compiler_params=pltpu.CompilerParams(vmem_limit_bytes=8 * 1024 * 1024),
     )(stats)
 
@@ -276,8 +276,8 @@
         line = jnp.stack([stale_kv] + along_z)
         parts = [line] + [lax.ppermute(line, AXES, moved(dx=d)) for d in (1, 3, 2)]
     rows, chans = latent.shape
-    group = coefficients(stats, rows * (chans // GROUPS), chans)
-    scaled = (latent.astype(jnp.float32) - group[0:1]) * group[1:2]
+    mean, scale = coefficients(stats, rows * (chans // GROUPS), chans)
+    scaled = (latent.astype(jnp.float32) - mean) * scale
     normed = (scaled * gn_gain + gn_bias).astype(jnp.bfloat16)
     stream = (jnp.dot(normed, w_in, preferred_element_type=jnp.float32) + b_in).astype(jnp.bfloat16)
     wide = stream.astype(jnp.float32)

time: 70.3 us -> 70.3 us (level)
  no operation moved by 1% of the time
where the time goes in v7:
time: 70.3 us; the launch traced here: 69.9 us
  starting transfers between devices  30 us (43%)
  waiting for transfers between devices  11.6 us (17%)
  blocking collectives  10.7 us (15%)
  Pallas kernels  8.5 us (12%)
  matrix products  4.52 us (6%)
  other arithmetic  1.97 us (3%)
  local copies, waits for them, and re-layouts  1.69 us (2%)
  between operations  0.87 us (1%)
    all_to_all x1, blocking collectives, exchange(): return lax.all_to_all(value, AXES, 0, 0, axis_index_groups=groups_of(mask))  10.7 us
    all_to_all x1, starting transfers between devices, local(): stats = lax.all_to_all(here, AXES, 0, 0).reshape(DEVICES, 2 * GROUPS)  10.6 us
    ppermute x3, starting transfers between devices, local(): along_z = [lax.ppermute(stale_kv, AXES, moved(dz=d)) for d in (4, 2, 6)]  10.2 us
    all_to_all x1, waiting for transfers between devices, local(): stats = lax.all_to_all(here, AXES, 0, 0).reshape(DEVICES, 2 * GROUPS)  6.32 us
    pallas_call x1, Pallas kernels, attend(): pl.pallas_call(attend_kernel, out_shape=jax.ShapeDtypeStruct((rows // pat...  5.89 us
    all_to_all x1, waiting for transfers between devices, exchange(): return lax.all_to_all(value, AXES, 0, 0, axis_index_groups=groups_of(mask))  4.58 us
    ppermute x3, starting transfers between devices, local(): parts = [line] + [lax.ppermute(line, AXES, moved(dx=d)) for d in (1, 3, 2)]  4.1 us
    all_to_all x1, starting transfers between devices, exchange(): return lax.all_to_all(value, AXES, 0, 0, axis_index_groups=groups_of(mask))  4.06 us
  transfers between devices with their start and end apart: 12, of which 3 were waited for; matrix products, arithmetic and copies ran while one was open for 10% of the time, Pallas kernels for 3%

profile of v7, /device:TPU:2, one launch (start us, length us, event | category | flops | bytes accessed | tf_op | source)
XLA Modules:
  0.0 69.9 jit_solution(3939428875397529833)
XLA Ops:
  0.6 0.0 copy-start
  0.6 7.3 %collective-permute-start = (bf16[2,32,640]{2,1,0:T(8,128)(2,1)}, bf16[2,32,640]{2,1,0:T(8,128)(2,1)S(1)}, u32[]{:S(2)}, u32[]{:S(2)}) collective-permute-start(bf16[2,32,640]{2,1,0:T(8,128)(2,1)} %param.21), channel_id=1, source_target_pairs={{0,16},{1,17},{2,18},{3,19},{4,20},{5,21},{6,22},{7,23},{8,24},{9,... | collective-permute-start | bytes 245768 | tf_op jit(solution)/shard_map/keys_z/ppermute | solution.py:271
  7.9 2.9 %collective-permute-start.1 = (bf16[2,32,640]{2,1,0:T(8,128)(2,1)}, bf16[2,32,640]{2,1,0:T(8,128)(2,1)}, u32[]{:S(2)}, u32[]{:S(2)}) collective-permute-start(bf16[2,32,640]{2,1,0:T(8,128)(2,1)} %param.21), channel_id=1, source_target_pairs={{0,8},{1,9},{2,10},{3,11},{4,12},{5,13},{6,14},{7,15},{8,16},{9,17... | collective-permute-start | bytes 245768 | tf_op jit(solution)/shard_map/keys_z/ppermute | solution.py:271
  10.8 0.9 %copy-done.1 = bf16[32,1280]{1,0:T(8,128)(2,1)S(1)} copy-done((bf16[32,1280]{1,0:T(8,128)(2,1)S(1)}, bf16[32,1280]{1,0:T(8,128)(2,1)}, u32[]{:S(2)}) %copy-start.1) | copy-done | bytes 81944
  11.7 1.4 %statistics.1 = f32[256,64]{1,0:T(8,128)} custom-call(bf16[32,1280]{1,0:T(8,128)(2,1)S(1)} %copy-done.1), custom_call_target="tpu_custom_call" | custom-call | tf_op jit(solution)/shard_map/statistics/pallas_call | solution.py:61
  13.1 10.6 %all-to-all-start = ((f32[256,1,64]{2,1,0:T(1,128)}), f32[256,1,64]{2,1,0:T(1,128)S(1)}, u32[]{:S(2)}, u32[]{:S(2)}) async-start(f32[256,1,64]{2,1,0:T(1,128)} %bitcast.1), calls=%async_computation | async-start | bytes 262144 | tf_op jit(solution)/shard_map/statistics/all_to_all | solution.py:274
  23.8 1.7 %pad_maximum_fusion.refs_0_ = bf16[4,2,32,640]{3,2,1,0:T(8,128)(2,1)} fusion(bf16[1,2,32,640]{3,2,1,0:T(8,128)(2,1)} %bitcast.10, bf16[1,2,32,640]{3,2,1,0:T(8,128)(2,1)} %bitcast.9, bf16[1,2,32,640]{3,2,1,0:T(8,128)(2,1)S(1)} %bitcast.20, bf16[1,2,32,640]{3,2,1,0:T(8,128)(2,1)} %bitcast.19), kind=kLoop, calls=%fused_computation.8 | loop fusion | flops 491520 | bytes 655360 | tf_op jit(solution)/shard_map/keys_x/stack | solution.py:276
  25.5 2.1 %collective-permute-start.5 = (bf16[4,2,32,640]{3,2,1,0:T(8,128)(2,1)}, bf16[4,2,32,640]{3,2,1,0:T(8,128)(2,1)}, u32[]{:S(2)}, u32[]{:S(2)}) collective-permute-start(bf16[4,2,32,640]{3,2,1,0:T(8,128)(2,1)} %pad_maximum_fusion.refs_0_), channel_id=1, source_target_pairs={{0,128},{1,129},{2,130},{3,131},{4,132},{5,133},{6,134},{7,135},{8... | collective-permute-start | bytes 983048 | tf_op jit(solution)/shard_map/keys_x/ppermute | solution.py:277
  27.6 1.5 %collective-permute-start.4 = (bf16[4,2,32,640]{3,2,1,0:T(8,128)(2,1)}, bf16[4,2,32,640]{3,2,1,0:T(8,128)(2,1)}, u32[]{:S(2)}, u32[]{:S(2)}) collective-permute-start(bf16[4,2,32,640]{3,2,1,0:T(8,128)(2,1)} %pad_maximum_fusion.refs_0_), channel_id=1, source_target_pairs={{0,192},{1,193},{2,194},{3,195},{4,196},{5,197},{6,198},{7,199},{8... | collective-permute-start | bytes 983048 | tf_op jit(solution)/shard_map/keys_x/ppermute | solution.py:277
  29.1 0.6 collective-permute-start.3
  29.6 6.3 %all-to-all-done = f32[256,1,64]{2,1,0:T(1,128)S(1)} async-done(((f32[256,1,64]{2,1,0:T(1,128)}), f32[256,1,64]{2,1,0:T(1,128)S(1)}, u32[]{:S(2)}, u32[]{:S(2)}) %all-to-all-start) | async-done | bytes 65568 | tf_op jit(solution)/shard_map/statistics/all_to_all | solution.py:274
  35.9 0.4 shard_map.130
  36.4 0.0 copy-start.4
  36.4 0.0 copy-start.6
  36.4 0.0 copy-start.7
  36.4 1.8 %convert_reduce_fusion = (f32[32]{0:T(128)S(1)}, bf16[32,1280]{1,0:T(8,128)(2,1)S(1)}) fusion(f32[1280]{0:T(1024)} %param.15, bf16[1280,1280]{1,0:T(8,128)(2,1)S(1)} %copy-done, bf16[32,1280]{1,0:T(8,128)(2,1)} %x_ref.1, f32[1280]{0:T(1024)} %param.13, f32[1280]{0:T(1024)} %param.12, f32[1280]{0:T(1024)S(1)} %get-tuple-element.8, f32[1280]{0:T(1024)S(1)} %get-tuple-element.7), kind=kOutput, calls=%fused_computation.10 | convolution fusion | flops 105267168 | bytes 3466368 | tf_op jit(solution)/shard_map/dot_general | solution.py:282
  38.2 0.0 copy-start.3
  38.2 0.2 fusion.6
  38.4 0.4 fusion.3
  38.9 0.8 %broadcast_in_dim.5 = bf16[8,32,640]{2,1,0:T(8,128)(2,1)} broadcast(bf16[32,640]{1,0:T(8,128)(2,1)S(1)} %fusion.3), dimensions={1,2} | broadcast | bytes 368640 | tf_op jit(solution)/shard_map/broadcast_in_dim | solution.py:290
  39.6 4.1 %all-to-all-start.1 = ((bf16[8,32,640]{2,1,0:T(8,128)(2,1)}), bf16[8,32,640]{2,1,0:T(8,128)(2,1)}, u32[]{:S(2)}, u32[]{:S(2)}) async-start(bf16[8,32,640]{2,1,0:T(8,128)(2,1)} %broadcast_in_dim.5), calls=%async_computation.1 | async-start | bytes 655360 | tf_op jit(solution)/shard_map/queries/all_to_all | solution.py:263
  43.7 0.7 %collective-permute-done.3.refs_1_ = bf16[4,2,32,640]{3,2,1,0:T(8,128)(2,1)} collective-permute-done((bf16[4,2,32,640]{3,2,1,0:T(8,128)(2,1)}, bf16[4,2,32,640]{3,2,1,0:T(8,128)(2,1)}, u32[]{:S(2)}, u32[]{:S(2)}) %collective-permute-start.3) | collective-permute-done | bytes 327712 | tf_op jit(solution)/shard_map/keys_x/ppermute | solution.py:277
  44.5 0.5 collective-permute-start.7
  45.0 0.0 collective-permute-start.9
  45.0 0.5 collective-permute-start.8
  45.5 1.9 %fusion.2 = bf16[1,32,640]{2,1,0:T(8,128)(2,1)S(1)} fusion(bf16[1280,640]{1,0:T(8,128)(2,1)} %param.20, bf16[32,1280]{1,0:T(8,128)(2,1)S(1)} %get-tuple-element.12, f32[1280]{0:T(1024)S(1)} %copy-done.6, f32[1280]{0:T(1024)S(1)} %copy-done.7, f32[32]{0:T(128)S(1)} %add_rsqrt_fusion, f32[32]{0:T(128)S(1)} %broadcast_multiply_fusion), kind=kOutput, calls=%fused_computation.6 | convolution fusion | flops 52695040 | bytes 1771776 | tf_op jit(solution)/shard_map/dot_general | solution.py:301
  47.4 0.4 fusion.1
  47.8 0.0 copy-start.2
  47.9 4.6 %all-to-all-done.1 = bf16[8,32,640]{2,1,0:T(8,128)(2,1)} async-done(((bf16[8,32,640]{2,1,0:T(8,128)(2,1)}), bf16[8,32,640]{2,1,0:T(8,128)(2,1)}, u32[]{:S(2)}, u32[]{:S(2)}) %all-to-all-start.1) | async-done | bytes 327712 | tf_op jit(solution)/shard_map/queries/all_to_all | solution.py:263
  52.5 5.9 %shard_map.131 = bf16[8,32,768]{2,1,0:T(8,128)(2,1)S(1)} custom-call(s32[1]{0:T(128)} %bitcast.5.place_ref, bf16[256,640]{1,0:T(8,128)(2,1)} %bitcast.6.q_ref, bf16[2,32,640]{2,1,0:T(8,128)(2,1)S(1)} %pad_maximum_fusion.1.fresh_ref, bf16[4,2,32,640]{3,2,1,0:T(8,128)(2,1)} %pad_maximum_fusion.refs_0_, bf16[4,2,32,640]{3,2,1,0:T(8,128)(2,1)} %collective-permute-done.3.refs_1_, ...), custom_call_target="tpu_custom_call" | custom-call | flops 671088640 | bytes 4194304 | tf_op jit(solution)/shard_map/pallas_call | solution.py:189
  58.4 10.7 %all_to_all.15.parts_ref = bf16[8,32,768]{2,1,0:T(8,128)(2,1)S(1)} all-to-all(bf16[8,32,768]{2,1,0:T(8,128)(2,1)S(1)} %shard_map.131), channel_id=1, replica_groups={{0,2,4,6,32,34,36,38},{1,3,5,7,33,35,37,39},{8,10,12,14,40,42,44,46},{9..., dimensions={0} | all-to-all | bytes 786432 | tf_op jit(solution)/shard_map/partials/all_to_all | solution.py:263
  69.0 0.8 %partials.1 = bf16[32,640]{1,0:T(8,128)(2,1)} custom-call(bf16[8,32,768]{2,1,0:T(8,128)(2,1)S(1)} %all_to_all.15.parts_ref), custom_call_target="tpu_custom_call" | custom-call | tf_op jit(solution)/shard_map/partials/pallas_call | solution.py:224
  (23 shorter events, 0.1 us)
Async XLA Ops:
  0.6 35.7 %copy-start = (bf16[1280,1280]{1,0:T(8,128)(2,1)S(1)}, bf16[1280,1280]{1,0:T(8,128)(2,1)}, u32[]{:S(2)}) copy-start(bf16[1280,1280]{1,0:T(8,128)(2,1)} %param.14) | copy-start | bytes 9830404
  0.6 23.1 %collective-permute-start = (bf16[2,32,640]{2,1,0:T(8,128)(2,1)}, bf16[2,32,640]{2,1,0:T(8,128)(2,1)S(1)}, u32[]{:S(2)}, u32[]{:S(2)}) collective-permute-start(bf16[2,32,640]{2,1,0:T(8,128)(2,1)} %param.21), channel_id=1, source_target_pairs={{0,16},{1,17},{2,18},{3,19},{4,20},{5,21},{6,22},{7,23},{8,24},{9,... | collective-permute-start | bytes 245768 | tf_op jit(solution)/shard_map/keys_z/ppermute | solution.py:271
  7.9 15.8 %collective-permute-start.2 = (bf16[2,32,640]{2,1,0:T(8,128)(2,1)}, bf16[2,32,640]{2,1,0:T(8,128)(2,1)}, u32[]{:S(2)}, u32[]{:S(2)}) collective-permute-start(bf16[2,32,640]{2,1,0:T(8,128)(2,1)} %param.21), channel_id=1, source_target_pairs={{0,24},{1,25},{2,26},{3,27},{4,28},{5,29},{6,30},{7,31},{8,0},{9,1... | collective-permute-start | bytes 245768 | tf_op jit(solution)/shard_map/keys_z/ppermute | solution.py:271
  7.9 15.8 %collective-permute-start.1 = (bf16[2,32,640]{2,1,0:T(8,128)(2,1)}, bf16[2,32,640]{2,1,0:T(8,128)(2,1)}, u32[]{:S(2)}, u32[]{:S(2)}) collective-permute-start(bf16[2,32,640]{2,1,0:T(8,128)(2,1)} %param.21), channel_id=1, source_target_pairs={{0,8},{1,9},{2,10},{3,11},{4,12},{5,13},{6,14},{7,15},{8,16},{9,17... | collective-permute-start | bytes 245768 | tf_op jit(solution)/shard_map/keys_z/ppermute | solution.py:271
  10.8 0.9 %copy-start.1 = (bf16[32,1280]{1,0:T(8,128)(2,1)S(1)}, bf16[32,1280]{1,0:T(8,128)(2,1)}, u32[]{:S(2)}) copy-start(bf16[32,1280]{1,0:T(8,128)(2,1)} %x_ref.1) | copy-start | bytes 245764
  13.1 22.8 %all-to-all-start = ((f32[256,1,64]{2,1,0:T(1,128)}), f32[256,1,64]{2,1,0:T(1,128)S(1)}, u32[]{:S(2)}, u32[]{:S(2)}) async-start(f32[256,1,64]{2,1,0:T(1,128)} %bitcast.1), calls=%async_computation | async-start | bytes 262144 | tf_op jit(solution)/shard_map/statistics/all_to_all | solution.py:274
  25.5 19.4 %collective-permute-start.5 = (bf16[4,2,32,640]{3,2,1,0:T(8,128)(2,1)}, bf16[4,2,32,640]{3,2,1,0:T(8,128)(2,1)}, u32[]{:S(2)}, u32[]{:S(2)}) collective-permute-start(bf16[4,2,32,640]{3,2,1,0:T(8,128)(2,1)} %pad_maximum_fusion.refs_0_), channel_id=1, source_target_pairs={{0,128},{1,129},{2,130},{3,131},{4,132},{5,133},{6,134},{7,135},{8... | collective-permute-start | bytes 983048 | tf_op jit(solution)/shard_map/keys_x/ppermute | solution.py:277
  27.6 17.4 %collective-permute-start.4 = (bf16[4,2,32,640]{3,2,1,0:T(8,128)(2,1)}, bf16[4,2,32,640]{3,2,1,0:T(8,128)(2,1)}, u32[]{:S(2)}, u32[]{:S(2)}) collective-permute-start(bf16[4,2,32,640]{3,2,1,0:T(8,128)(2,1)} %pad_maximum_fusion.refs_0_), channel_id=1, source_target_pairs={{0,192},{1,193},{2,194},{3,195},{4,196},{5,197},{6,198},{7,199},{8... | collective-permute-start | bytes 983048 | tf_op jit(solution)/shard_map/keys_x/ppermute | solution.py:277
  29.1 15.4 %collective-permute-start.3 = (bf16[4,2,32,640]{3,2,1,0:T(8,128)(2,1)}, bf16[4,2,32,640]{3,2,1,0:T(8,128)(2,1)}, u32[]{:S(2)}, u32[]{:S(2)}) collective-permute-start(bf16[4,2,32,640]{3,2,1,0:T(8,128)(2,1)} %pad_maximum_fusion.refs_0_), channel_id=1, source_target_pairs={{0,64},{1,65},{2,66},{3,67},{4,68},{5,69},{6,70},{7,71},{8,72},{9,... | collective-permute-start | bytes 983048 | tf_op jit(solution)/shard_map/keys_x/ppermute | solution.py:277
  36.4 2.1 %copy-start.4 = (bf16[1280,640]{1,0:T(8,128)(2,1)S(1)}, bf16[1280,640]{1,0:T(8,128)(2,1)}, u32[]{:S(2)}) copy-start(bf16[1280,640]{1,0:T(8,128)(2,1)} %param.18) | copy-start | bytes 4915204
  36.4 2.0 %copy-start.6 = (f32[1280]{0:T(1024)S(1)}, f32[1280]{0:T(1024)}, u32[]{:S(2)}) copy-start(f32[1280]{0:T(1024)} %param.17) | copy-start | bytes 15364
  36.4 2.0 %copy-start.7 = (f32[1280]{0:T(1024)S(1)}, f32[1280]{0:T(1024)}, u32[]{:S(2)}) copy-start(f32[1280]{0:T(1024)} %param.16) | copy-start | bytes 15364
  38.2 9.2 %copy-start.3 = (bf16[32,1280]{1,0:T(8,128)(2,1)}, bf16[32,1280]{1,0:T(8,128)(2,1)S(1)}, u32[]{:S(2)}) copy-start(bf16[32,1280]{1,0:T(8,128)(2,1)S(1)} %get-tuple-element.12) | copy-start | bytes 245764
  39.6 12.8 %all-to-all-start.1 = ((bf16[8,32,640]{2,1,0:T(8,128)(2,1)}), bf16[8,32,640]{2,1,0:T(8,128)(2,1)}, u32[]{:S(2)}, u32[]{:S(2)}) async-start(bf16[8,32,640]{2,1,0:T(8,128)(2,1)} %broadcast_in_dim.5), calls=%async_computation.1 | async-start | bytes 655360 | tf_op jit(solution)/shard_map/queries/all_to_all | solution.py:263
  43.7 3.6 %copy-start.5 = (bf16[1280,640]{1,0:T(8,128)(2,1)S(1)}, bf16[1280,640]{1,0:T(8,128)(2,1)}, u32[]{:S(2)}) copy-start(bf16[1280,640]{1,0:T(8,128)(2,1)} %param.19) | copy-start | bytes 4915204
  44.4 8.0 %collective-permute-start.6 = (bf16[4,2,32,640]{3,2,1,0:T(8,128)(2,1)}, bf16[4,2,32,640]{3,2,1,0:T(8,128)(2,1)}, u32[]{:S(2)}, u32[]{:S(2)}) collective-permute-start(bf16[4,2,32,640]{3,2,1,0:T(8,128)(2,1)} %pad_maximum_fusion.refs_0_), channel_id=1, source_target_pairs={{0,1},{1,0},{2,3},{3,2},{4,5},{5,4},{6,7},{7,6},{8,9},{9,8},{10,11... | collective-permute-start | bytes 983048 | tf_op jit(solution)/shard_map/keys_core/ppermute | solution.py:295
  44.5 8.0 %collective-permute-start.7 = (bf16[4,2,32,640]{3,2,1,0:T(8,128)(2,1)}, bf16[4,2,32,640]{3,2,1,0:T(8,128)(2,1)}, u32[]{:S(2)}, u32[]{:S(2)}) collective-permute-start(bf16[4,2,32,640]{3,2,1,0:T(8,128)(2,1)} %collective-permute-done.3.refs_1_), channel_id=1, source_target_pairs={{0,1},{1,0},{2,3},{3,2},{4,5},{5,4},{6,7},{7,6},{8,9},{9,8},{10,11... | collective-permute-start | bytes 983048 | tf_op jit(solution)/shard_map/keys_core/ppermute | solution.py:295
  45.0 7.5 %collective-permute-start.9 = (bf16[4,2,32,640]{3,2,1,0:T(8,128)(2,1)}, bf16[4,2,32,640]{3,2,1,0:T(8,128)(2,1)}, u32[]{:S(2)}, u32[]{:S(2)}) collective-permute-start(bf16[4,2,32,640]{3,2,1,0:T(8,128)(2,1)} %collective-permute-done.5.refs_3_), channel_id=1, source_target_pairs={{0,1},{1,0},{2,3},{3,2},{4,5},{5,4},{6,7},{7,6},{8,9},{9,8},{10,11... | collective-permute-start | bytes 983048 | tf_op jit(solution)/shard_map/keys_core/ppermute | solution.py:295
  45.0 7.5 %collective-permute-start.8 = (bf16[4,2,32,640]{3,2,1,0:T(8,128)(2,1)}, bf16[4,2,32,640]{3,2,1,0:T(8,128)(2,1)}, u32[]{:S(2)}, u32[]{:S(2)}) collective-permute-start(bf16[4,2,32,640]{3,2,1,0:T(8,128)(2,1)} %collective-permute-done.4.refs_2_), channel_id=1, source_target_pairs={{0,1},{1,0},{2,3},{3,2},{4,5},{5,4},{6,7},{7,6},{8,9},{9,8},{10,11... | collective-permute-start | bytes 983048 | tf_op jit(solution)/shard_map/keys_core/ppermute | solution.py:295
  47.8 10.5 %copy-start.2 = (bf16[2,32,640]{2,1,0:T(8,128)(2,1)}, bf16[2,32,640]{2,1,0:T(8,128)(2,1)S(1)}, u32[]{:S(2)}) copy-start(bf16[2,32,640]{2,1,0:T(8,128)(2,1)S(1)} %pad_maximum_fusion.1.fresh_ref) | copy-start | bytes 245764

commit v8 on v7

--- a/solution.py
+++ b/solution.py
@@ -138,13 +138,13 @@
     for copy in copies:
         copy.wait()
 
-    keys = p_ref.shape[1]
+    keys = p_ref.shape[2]
     row = lax.broadcasted_iota(jnp.int32, (2 * rows, 1), 0)
     row = jnp.where(row >= rows, row - rows, row)
     is_own = (row >= own) & (row < own + patch)
     totals = jnp.zeros((rows, 128), jnp.float32)
     own_totals = jnp.zeros((patch, 128), jnp.float32)
-    step = 128
+    step = 256
     for pair, lanes in enumerate(pairs):
         query = two_heads(q_ref[:, lanes])
         key = kv_ref[:, :, 0, :, lanes].reshape(keys, 128)
@@ -157,8 +157,8 @@
             if at == 0:
                 column = lax.broadcasted_iota(jnp.int32, (1, step), 1)
                 weight = jnp.where(is_own & (column < patch), 0.0, weight)
-            p_ref[:, at : at + step] = weight.astype(jnp.bfloat16)
-        acc = jnp.dot(p_ref[...], with_ones(value), preferred_element_type=jnp.float32)
+            p_ref[pair % 2, :, at : at + step] = weight.astype(jnp.bfloat16)
+        acc = jnp.dot(p_ref[pair % 2], with_ones(value), preferred_element_type=jnp.float32)
         numer = jnp.where(low, acc[:rows, :128], acc[rows:, :128])
         out_ref[:, :, lanes] = numer.astype(jnp.bfloat16).reshape(count, patch, 128)
         numer_ref[...] = numer
@@ -193,7 +193,7 @@
         out_specs=VMEM,
         scratch_shapes=[
             pltpu.VMEM((len(key_parts),) + key_parts[0].shape, jnp.bfloat16),
-            pltpu.VMEM((2 * rows, keys), jnp.bfloat16),
+            pltpu.VMEM((2, 2 * rows, keys), jnp.bfloat16),
             pltpu.VMEM((HEADS // 2, 2 * patch, 256), jnp.float32),
             pltpu.VMEM((rows, 128), jnp.float32),
             pltpu.VMEM((rows, 128), jnp.float32),

time: 70.3 us -> 70.2 us (level)
  no operation moved by 1% of the time
where the time goes in v8:
time: 70.2 us; the launch traced here: 69.8 us
  starting transfers between devices  30 us (43%)
  waiting for transfers between devices  11.6 us (17%)
  blocking collectives  10.7 us (15%)
  Pallas kernels  8.41 us (12%)
  matrix products  4.52 us (6%)
  other arithmetic  1.97 us (3%)
  local copies, waits for them, and re-layouts  1.69 us (2%)
  between operations  0.87 us (1%)
    all_to_all x1, blocking collectives, exchange(): return lax.all_to_all(value, AXES, 0, 0, axis_index_groups=groups_of(mask))  10.7 us
    all_to_all x1, starting transfers between devices, local(): stats = lax.all_to_all(here, AXES, 0, 0).reshape(DEVICES, 2 * GROUPS)  10.6 us
    ppermute x3, starting transfers between devices, local(): along_z = [lax.ppermute(stale_kv, AXES, moved(dz=d)) for d in (4, 2, 6)]  10.2 us
    all_to_all x1, waiting for transfers between devices, local(): stats = lax.all_to_all(here, AXES, 0, 0).reshape(DEVICES, 2 * GROUPS)  6.32 us
    pallas_call x1, Pallas kernels, attend(): pl.pallas_call(attend_kernel, out_shape=jax.ShapeDtypeStruct((rows // pat...  5.8 us
    all_to_all x1, waiting for transfers between devices, exchange(): return lax.all_to_all(value, AXES, 0, 0, axis_index_groups=groups_of(mask))  4.58 us
    ppermute x3, starting transfers between devices, local(): parts = [line] + [lax.ppermute(line, AXES, moved(dx=d)) for d in (1, 3, 2)]  4.1 us
    all_to_all x1, starting transfers between devices, exchange(): return lax.all_to_all(value, AXES, 0, 0, axis_index_groups=groups_of(mask))  4.06 us
  transfers between devices with their start and end apart: 12, of which 3 were waited for; matrix products, arithmetic and copies ran while one was open for 10% of the time, Pallas kernels for 3%

profile of v8, /device:TPU:2, one launch (start us, length us, event | category | flops | bytes accessed | tf_op | source)
XLA Modules:
  0.0 69.8 jit_solution(7742311792594913689)
XLA Ops:
  0.6 0.0 copy-start
  0.6 7.3 %collective-permute-start = (bf16[2,32,640]{2,1,0:T(8,128)(2,1)}, bf16[2,32,640]{2,1,0:T(8,128)(2,1)S(1)}, u32[]{:S(2)}, u32[]{:S(2)}) collective-permute-start(bf16[2,32,640]{2,1,0:T(8,128)(2,1)} %param.21), channel_id=1, source_target_pairs={{0,16},{1,17},{2,18},{3,19},{4,20},{5,21},{6,22},{7,23},{8,24},{9,... | collective-permute-start | bytes 245768 | tf_op jit(solution)/shard_map/keys_z/ppermute | solution.py:271
  7.9 2.9 %collective-permute-start.1 = (bf16[2,32,640]{2,1,0:T(8,128)(2,1)}, bf16[2,32,640]{2,1,0:T(8,128)(2,1)}, u32[]{:S(2)}, u32[]{:S(2)}) collective-permute-start(bf16[2,32,640]{2,1,0:T(8,128)(2,1)} %param.21), channel_id=1, source_target_pairs={{0,8},{1,9},{2,10},{3,11},{4,12},{5,13},{6,14},{7,15},{8,16},{9,17... | collective-permute-start | bytes 245768 | tf_op jit(solution)/shard_map/keys_z/ppermute | solution.py:271
  10.8 0.9 %copy-done.1 = bf16[32,1280]{1,0:T(8,128)(2,1)S(1)} copy-done((bf16[32,1280]{1,0:T(8,128)(2,1)S(1)}, bf16[32,1280]{1,0:T(8,128)(2,1)}, u32[]{:S(2)}) %copy-start.1) | copy-done | bytes 81944
  11.7 1.4 %statistics.1 = f32[256,64]{1,0:T(8,128)} custom-call(bf16[32,1280]{1,0:T(8,128)(2,1)S(1)} %copy-done.1), custom_call_target="tpu_custom_call" | custom-call | tf_op jit(solution)/shard_map/statistics/pallas_call | solution.py:61
  13.1 10.6 %all-to-all-start = ((f32[256,1,64]{2,1,0:T(1,128)}), f32[256,1,64]{2,1,0:T(1,128)S(1)}, u32[]{:S(2)}, u32[]{:S(2)}) async-start(f32[256,1,64]{2,1,0:T(1,128)} %bitcast.1), calls=%async_computation | async-start | bytes 262144 | tf_op jit(solution)/shard_map/statistics/all_to_all | solution.py:274
  23.8 1.7 %pad_maximum_fusion.refs_0_ = bf16[4,2,32,640]{3,2,1,0:T(8,128)(2,1)} fusion(bf16[1,2,32,640]{3,2,1,0:T(8,128)(2,1)} %bitcast.10, bf16[1,2,32,640]{3,2,1,0:T(8,128)(2,1)} %bitcast.9, bf16[1,2,32,640]{3,2,1,0:T(8,128)(2,1)S(1)} %bitcast.20, bf16[1,2,32,640]{3,2,1,0:T(8,128)(2,1)} %bitcast.19), kind=kLoop, calls=%fused_computation.8 | loop fusion | flops 491520 | bytes 655360 | tf_op jit(solution)/shard_map/keys_x/stack | solution.py:276
  25.5 2.1 %collective-permute-start.5 = (bf16[4,2,32,640]{3,2,1,0:T(8,128)(2,1)}, bf16[4,2,32,640]{3,2,1,0:T(8,128)(2,1)}, u32[]{:S(2)}, u32[]{:S(2)}) collective-permute-start(bf16[4,2,32,640]{3,2,1,0:T(8,128)(2,1)} %pad_maximum_fusion.refs_0_), channel_id=1, source_target_pairs={{0,128},{1,129},{2,130},{3,131},{4,132},{5,133},{6,134},{7,135},{8... | collective-permute-start | bytes 983048 | tf_op jit(solution)/shard_map/keys_x/ppermute | solution.py:277
  27.6 1.5 %collective-permute-start.4 = (bf16[4,2,32,640]{3,2,1,0:T(8,128)(2,1)}, bf16[4,2,32,640]{3,2,1,0:T(8,128)(2,1)}, u32[]{:S(2)}, u32[]{:S(2)}) collective-permute-start(bf16[4,2,32,640]{3,2,1,0:T(8,128)(2,1)} %pad_maximum_fusion.refs_0_), channel_id=1, source_target_pairs={{0,192},{1,193},{2,194},{3,195},{4,196},{5,197},{6,198},{7,199},{8... | collective-permute-start | bytes 983048 | tf_op jit(solution)/shard_map/keys_x/ppermute | solution.py:277
  29.1 0.6 collective-permute-start.3
  29.6 6.3 %all-to-all-done = f32[256,1,64]{2,1,0:T(1,128)S(1)} async-done(((f32[256,1,64]{2,1,0:T(1,128)}), f32[256,1,64]{2,1,0:T(1,128)S(1)}, u32[]{:S(2)}, u32[]{:S(2)}) %all-to-all-start) | async-done | bytes 65568 | tf_op jit(solution)/shard_map/statistics/all_to_all | solution.py:274
  35.9 0.4 shard_map.130
  36.4 0.0 copy-start.4
  36.4 0.0 copy-start.6
  36.4 0.0 copy-start.7
  36.4 1.8 %convert_reduce_fusion = (f32[32]{0:T(128)S(1)}, bf16[32,1280]{1,0:T(8,128)(2,1)S(1)}) fusion(f32[1280]{0:T(1024)} %param.15, bf16[1280,1280]{1,0:T(8,128)(2,1)S(1)} %copy-done, bf16[32,1280]{1,0:T(8,128)(2,1)} %x_ref.1, f32[1280]{0:T(1024)} %param.13, f32[1280]{0:T(1024)} %param.12, f32[1280]{0:T(1024)S(1)} %get-tuple-element.8, f32[1280]{0:T(1024)S(1)} %get-tuple-element.7), kind=kOutput, calls=%fused_computation.10 | convolution fusion | flops 105267168 | bytes 3466368 | tf_op jit(solution)/shard_map/dot_general | solution.py:282
  38.2 0.0 copy-start.3
  38.2 0.2 fusion.6
  38.4 0.4 fusion.3
  38.9 0.8 %broadcast_in_dim.5 = bf16[8,32,640]{2,1,0:T(8,128)(2,1)} broadcast(bf16[32,640]{1,0:T(8,128)(2,1)S(1)} %fusion.3), dimensions={1,2} | broadcast | bytes 368640 | tf_op jit(solution)/shard_map/broadcast_in_dim | solution.py:290
  39.6 4.1 %all-to-all-start.1 = ((bf16[8,32,640]{2,1,0:T(8,128)(2,1)}), bf16[8,32,640]{2,1,0:T(8,128)(2,1)}, u32[]{:S(2)}, u32[]{:S(2)}) async-start(bf16[8,32,640]{2,1,0:T(8,128)(2,1)} %broadcast_in_dim.5), calls=%async_computation.1 | async-start | bytes 655360 | tf_op jit(solution)/shard_map/queries/all_to_all | solution.py:263
  43.7 0.7 %collective-permute-done.3.refs_1_ = bf16[4,2,32,640]{3,2,1,0:T(8,128)(2,1)} collective-permute-done((bf16[4,2,32,640]{3,2,1,0:T(8,128)(2,1)}, bf16[4,2,32,640]{3,2,1,0:T(8,128)(2,1)}, u32[]{:S(2)}, u32[]{:S(2)}) %collective-permute-start.3) | collective-permute-done | bytes 327712 | tf_op jit(solution)/shard_map/keys_x/ppermute | solution.py:277
  44.5 0.5 collective-permute-start.7
  45.0 0.0 collective-permute-start.9
  45.0 0.5 collective-permute-start.8
  45.5 1.9 %fusion.2 = bf16[1,32,640]{2,1,0:T(8,128)(2,1)S(1)} fusion(bf16[1280,640]{1,0:T(8,128)(2,1)} %param.20, bf16[32,1280]{1,0:T(8,128)(2,1)S(1)} %get-tuple-element.12, f32[1280]{0:T(1024)S(1)} %copy-done.6, f32[1280]{0:T(1024)S(1)} %copy-done.7, f32[32]{0:T(128)S(1)} %add_rsqrt_fusion, f32[32]{0:T(128)S(1)} %broadcast_multiply_fusion), kind=kOutput, calls=%fused_computation.6 | convolution fusion | flops 52695040 | bytes 1771776 | tf_op jit(solution)/shard_map/dot_general | solution.py:301
  47.4 0.4 fusion.1
  47.8 0.0 copy-start.2
  47.9 4.6 %all-to-all-done.1 = bf16[8,32,640]{2,1,0:T(8,128)(2,1)} async-done(((bf16[8,32,640]{2,1,0:T(8,128)(2,1)}), bf16[8,32,640]{2,1,0:T(8,128)(2,1)}, u32[]{:S(2)}, u32[]{:S(2)}) %all-to-all-start.1) | async-done | bytes 327712 | tf_op jit(solution)/shard_map/queries/all_to_all | solution.py:263
  52.5 5.8 %shard_map.131 = bf16[8,32,768]{2,1,0:T(8,128)(2,1)S(1)} custom-call(s32[1]{0:T(128)} %bitcast.5.place_ref, bf16[256,640]{1,0:T(8,128)(2,1)} %bitcast.6.q_ref, bf16[2,32,640]{2,1,0:T(8,128)(2,1)S(1)} %pad_maximum_fusion.1.fresh_ref, bf16[4,2,32,640]{3,2,1,0:T(8,128)(2,1)} %pad_maximum_fusion.refs_0_, bf16[4,2,32,640]{3,2,1,0:T(8,128)(2,1)} %collective-permute-done.3.refs_1_, ...), custom_call_target="tpu_custom_call" | custom-call | flops 671088640 | bytes 4194304 | tf_op jit(solution)/shard_map/pallas_call | solution.py:189
  58.3 10.7 %all_to_all.15.parts_ref = bf16[8,32,768]{2,1,0:T(8,128)(2,1)S(1)} all-to-all(bf16[8,32,768]{2,1,0:T(8,128)(2,1)S(1)} %shard_map.131), channel_id=1, replica_groups={{0,2,4,6,32,34,36,38},{1,3,5,7,33,35,37,39},{8,10,12,14,40,42,44,46},{9..., dimensions={0} | all-to-all | bytes 786432 | tf_op jit(solution)/shard_map/partials/all_to_all | solution.py:263
  68.9 0.8 %partials.1 = bf16[32,640]{1,0:T(8,128)(2,1)} custom-call(bf16[8,32,768]{2,1,0:T(8,128)(2,1)S(1)} %all_to_all.15.parts_ref), custom_call_target="tpu_custom_call" | custom-call | tf_op jit(solution)/shard_map/partials/pallas_call | solution.py:224
  (23 shorter events, 0.1 us)
Async XLA Ops:
  0.6 35.7 %copy-start = (bf16[1280,1280]{1,0:T(8,128)(2,1)S(1)}, bf16[1280,1280]{1,0:T(8,128)(2,1)}, u32[]{:S(2)}) copy-start(bf16[1280,1280]{1,0:T(8,128)(2,1)} %param.14) | copy-start | bytes 9830404
  0.6 23.1 %collective-permute-start = (bf16[2,32,640]{2,1,0:T(8,128)(2,1)}, bf16[2,32,640]{2,1,0:T(8,128)(2,1)S(1)}, u32[]{:S(2)}, u32[]{:S(2)}) collective-permute-start(bf16[2,32,640]{2,1,0:T(8,128)(2,1)} %param.21), channel_id=1, source_target_pairs={{0,16},{1,17},{2,18},{3,19},{4,20},{5,21},{6,22},{7,23},{8,24},{9,... | collective-permute-start | bytes 245768 | tf_op jit(solution)/shard_map/keys_z/ppermute | solution.py:271
  7.9 15.8 %collective-permute-start.2 = (bf16[2,32,640]{2,1,0:T(8,128)(2,1)}, bf16[2,32,640]{2,1,0:T(8,128)(2,1)}, u32[]{:S(2)}, u32[]{:S(2)}) collective-permute-start(bf16[2,32,640]{2,1,0:T(8,128)(2,1)} %param.21), channel_id=1, source_target_pairs={{0,24},{1,25},{2,26},{3,27},{4,28},{5,29},{6,30},{7,31},{8,0},{9,1... | collective-permute-start | bytes 245768 | tf_op jit(solution)/shard_map/keys_z/ppermute | solution.py:271
  7.9 15.8 %collective-permute-start.1 = (bf16[2,32,640]{2,1,0:T(8,128)(2,1)}, bf16[2,32,640]{2,1,0:T(8,128)(2,1)}, u32[]{:S(2)}, u32[]{:S(2)}) collective-permute-start(bf16[2,32,640]{2,1,0:T(8,128)(2,1)} %param.21), channel_id=1, source_target_pairs={{0,8},{1,9},{2,10},{3,11},{4,12},{5,13},{6,14},{7,15},{8,16},{9,17... | collective-permute-start | bytes 245768 | tf_op jit(solution)/shard_map/keys_z/ppermute | solution.py:271
  10.8 0.9 %copy-start.1 = (bf16[32,1280]{1,0:T(8,128)(2,1)S(1)}, bf16[32,1280]{1,0:T(8,128)(2,1)}, u32[]{:S(2)}) copy-start(bf16[32,1280]{1,0:T(8,128)(2,1)} %x_ref.1) | copy-start | bytes 245764
  13.1 22.8 %all-to-all-start = ((f32[256,1,64]{2,1,0:T(1,128)}), f32[256,1,64]{2,1,0:T(1,128)S(1)}, u32[]{:S(2)}, u32[]{:S(2)}) async-start(f32[256,1,64]{2,1,0:T(1,128)} %bitcast.1), calls=%async_computation | async-start | bytes 262144 | tf_op jit(solution)/shard_map/statistics/all_to_all | solution.py:274
  25.5 19.4 %collective-permute-start.5 = (bf16[4,2,32,640]{3,2,1,0:T(8,128)(2,1)}, bf16[4,2,32,640]{3,2,1,0:T(8,128)(2,1)}, u32[]{:S(2)}, u32[]{:S(2)}) collective-permute-start(bf16[4,2,32,640]{3,2,1,0:T(8,128)(2,1)} %pad_maximum_fusion.refs_0_), channel_id=1, source_target_pairs={{0,128},{1,129},{2,130},{3,131},{4,132},{5,133},{6,134},{7,135},{8... | collective-permute-start | bytes 983048 | tf_op jit(solution)/shard_map/keys_x/ppermute | solution.py:277
  27.6 17.4 %collective-permute-start.4 = (bf16[4,2,32,640]{3,2,1,0:T(8,128)(2,1)}, bf16[4,2,32,640]{3,2,1,0:T(8,128)(2,1)}, u32[]{:S(2)}, u32[]{:S(2)}) collective-permute-start(bf16[4,2,32,640]{3,2,1,0:T(8,128)(2,1)} %pad_maximum_fusion.refs_0_), channel_id=1, source_target_pairs={{0,192},{1,193},{2,194},{3,195},{4,196},{5,197},{6,198},{7,199},{8... | collective-permute-start | bytes 983048 | tf_op jit(solution)/shard_map/keys_x/ppermute | solution.py:277
  29.1 15.4 %collective-permute-start.3 = (bf16[4,2,32,640]{3,2,1,0:T(8,128)(2,1)}, bf16[4,2,32,640]{3,2,1,0:T(8,128)(2,1)}, u32[]{:S(2)}, u32[]{:S(2)}) collective-permute-start(bf16[4,2,32,640]{3,2,1,0:T(8,128)(2,1)} %pad_maximum_fusion.refs_0_), channel_id=1, source_target_pairs={{0,64},{1,65},{2,66},{3,67},{4,68},{5,69},{6,70},{7,71},{8,72},{9,... | collective-permute-start | bytes 983048 | tf_op jit(solution)/shard_map/keys_x/ppermute | solution.py:277
  36.4 2.1 %copy-start.4 = (bf16[1280,640]{1,0:T(8,128)(2,1)S(1)}, bf16[1280,640]{1,0:T(8,128)(2,1)}, u32[]{:S(2)}) copy-start(bf16[1280,640]{1,0:T(8,128)(2,1)} %param.18) | copy-start | bytes 4915204
  36.4 2.0 %copy-start.6 = (f32[1280]{0:T(1024)S(1)}, f32[1280]{0:T(1024)}, u32[]{:S(2)}) copy-start(f32[1280]{0:T(1024)} %param.17) | copy-start | bytes 15364
  36.4 2.0 %copy-start.7 = (f32[1280]{0:T(1024)S(1)}, f32[1280]{0:T(1024)}, u32[]{:S(2)}) copy-start(f32[1280]{0:T(1024)} %param.16) | copy-start | bytes 15364
  38.2 9.2 %copy-start.3 = (bf16[32,1280]{1,0:T(8,128)(2,1)}, bf16[32,1280]{1,0:T(8,128)(2,1)S(1)}, u32[]{:S(2)}) copy-start(bf16[32,1280]{1,0:T(8,128)(2,1)S(1)} %get-tuple-element.12) | copy-start | bytes 245764
  39.6 12.8 %all-to-all-start.1 = ((bf16[8,32,640]{2,1,0:T(8,128)(2,1)}), bf16[8,32,640]{2,1,0:T(8,128)(2,1)}, u32[]{:S(2)}, u32[]{:S(2)}) async-start(bf16[8,32,640]{2,1,0:T(8,128)(2,1)} %broadcast_in_dim.5), calls=%async_computation.1 | async-start | bytes 655360 | tf_op jit(solution)/shard_map/queries/all_to_all | solution.py:263
  43.7 3.6 %copy-start.5 = (bf16[1280,640]{1,0:T(8,128)(2,1)S(1)}, bf16[1280,640]{1,0:T(8,128)(2,1)}, u32[]{:S(2)}) copy-start(bf16[1280,640]{1,0:T(8,128)(2,1)} %param.19) | copy-start | bytes 4915204
  44.4 8.0 %collective-permute-start.6 = (bf16[4,2,32,640]{3,2,1,0:T(8,128)(2,1)}, bf16[4,2,32,640]{3,2,1,0:T(8,128)(2,1)}, u32[]{:S(2)}, u32[]{:S(2)}) collective-permute-start(bf16[4,2,32,640]{3,2,1,0:T(8,128)(2,1)} %pad_maximum_fusion.refs_0_), channel_id=1, source_target_pairs={{0,1},{1,0},{2,3},{3,2},{4,5},{5,4},{6,7},{7,6},{8,9},{9,8},{10,11... | collective-permute-start | bytes 983048 | tf_op jit(solution)/shard_map/keys_core/ppermute | solution.py:295
  44.5 8.0 %collective-permute-start.7 = (bf16[4,2,32,640]{3,2,1,0:T(8,128)(2,1)}, bf16[4,2,32,640]{3,2,1,0:T(8,128)(2,1)}, u32[]{:S(2)}, u32[]{:S(2)}) collective-permute-start(bf16[4,2,32,640]{3,2,1,0:T(8,128)(2,1)} %collective-permute-done.3.refs_1_), channel_id=1, source_target_pairs={{0,1},{1,0},{2,3},{3,2},{4,5},{5,4},{6,7},{7,6},{8,9},{9,8},{10,11... | collective-permute-start | bytes 983048 | tf_op jit(solution)/shard_map/keys_core/ppermute | solution.py:295
  45.0 7.5 %collective-permute-start.9 = (bf16[4,2,32,640]{3,2,1,0:T(8,128)(2,1)}, bf16[4,2,32,640]{3,2,1,0:T(8,128)(2,1)}, u32[]{:S(2)}, u32[]{:S(2)}) collective-permute-start(bf16[4,2,32,640]{3,2,1,0:T(8,128)(2,1)} %collective-permute-done.5.refs_3_), channel_id=1, source_target_pairs={{0,1},{1,0},{2,3},{3,2},{4,5},{5,4},{6,7},{7,6},{8,9},{9,8},{10,11... | collective-permute-start | bytes 983048 | tf_op jit(solution)/shard_map/keys_core/ppermute | solution.py:295
  45.0 7.5 %collective-permute-start.8 = (bf16[4,2,32,640]{3,2,1,0:T(8,128)(2,1)}, bf16[4,2,32,640]{3,2,1,0:T(8,128)(2,1)}, u32[]{:S(2)}, u32[]{:S(2)}) collective-permute-start(bf16[4,2,32,640]{3,2,1,0:T(8,128)(2,1)} %collective-permute-done.4.refs_2_), channel_id=1, source_target_pairs={{0,1},{1,0},{2,3},{3,2},{4,5},{5,4},{6,7},{7,6},{8,9},{9,8},{10,11... | collective-permute-start | bytes 983048 | tf_op jit(solution)/shard_map/keys_core/ppermute | solution.py:295
  47.8 10.4 %copy-start.2 = (bf16[2,32,640]{2,1,0:T(8,128)(2,1)}, bf16[2,32,640]{2,1,0:T(8,128)(2,1)S(1)}, u32[]{:S(2)}) copy-start(bf16[2,32,640]{2,1,0:T(8,128)(2,1)S(1)} %pad_maximum_fusion.1.fresh_ref) | copy-start | bytes 245764
